TPU v7x, 32 devices: a whole 2x2x4 slice. The times are simulated.
32 devices in a mesh: seq: 8 (over z, x), tp: 4 (over y, core).
Axes of the slice: x: 2, y: 2, z: 4, core: 2. Of those that a mesh axis runs over, the one named last changes fastest.
Arguments:
- latents_in: bfloat16 [16384, 1024], P(('seq', 'tp')), may hold values from -6 to 6
- gain_one: float32 [1024], replicated, may hold values from 0.5 to 1.5
- w_qkv: bfloat16 [1024, 3, 1024], P(None, None, 'tp'), may hold values from -0.1875 to 0.1875
- w_out: bfloat16 [1024, 1024], P(None, 'tp'), may hold values from -0.75 to 0.75
- gain_two: float32 [1024], replicated, may hold values from 0.5 to 1.5
- w_gate: bfloat16 [1024, 2816], P(None, 'tp'), may hold values from -0.1875 to 0.1875
- w_up: bfloat16 [1024, 2816], P(None, 'tp'), may hold values from -0.1875 to 0.1875
- w_down: bfloat16 [1024, 2816], P(None, 'tp'), may hold values from -0.109375 to 0.109375
- cotangent: bfloat16 [16384, 1024], P(('seq', 'tp')), may hold values from -6 to 6
- doc_lengths: int32 [8, 3], P('seq'), may hold values from 256 to 1024, as said below
- valid_lengths: int32 [8, 3], P('seq'), may hold values from 192 to 1024, as said below
- hash_ids: int32 [6, 16384], P(None, ('seq', 'tp')), may hold values from 0 to 500001
- hash_weights: float32 [6, 16384], P(None, ('seq', 'tp')), may hold values from -6 to 6
Outputs:
- latents_out: bfloat16 [16384, 1024], P(('seq', 'tp'))
- grad_latents: float32 [16384, 1024], P(('seq', 'tp'))
- grad_gain_one: float32 [1024], replicated
- grad_w_qkv: float32 [1024, 3, 1024], P('seq', None, 'tp')
- grad_w_out: float32 [1024, 1024], P('seq', 'tp')
- grad_gain_two: float32 [1024], replicated
- grad_w_gate: float32 [1024, 2816], P('seq', 'tp')
- grad_w_up: float32 [1024, 2816], P('seq', 'tp')
- grad_w_down: float32 [1024, 2816], P('seq', 'tp')
- hash_counts: float32 [6, 500002], replicated
Inputs may be any that keep to these rules, and one draw needn't show every extreme that they name: `doc_lengths`: in each group the 3 lengths sum to 2048; one of them is 1024, the others at least one eighth of 2048. `valid_lengths`: each sequence's valid patches are at least three quarters of its length and come first in it.
All inputs are finite; a program needn't handle non-finite values.
Results may differ from a plain program's by a relative error of at most 0.018.
Values may be sent and summed in bfloat16 or wider, within the bound.
A program may use at most 256 MiB of HBM per device.

v0:
```python
import jax
import jax.numpy as jnp
from jax import lax
from jax.sharding import PartitionSpec as P

HEAD_DIM = 64
HASH_ROWS = 500002


EPSILON = 1e-05
MASKED = -1e30


def norm_rows(row_data, gain):
    scaling = lax.rsqrt(jnp.mean(row_data * row_data, axis=-1, keepdims=True) + EPSILON)
    return (row_data * scaling * gain, scaling)


def norm_back(row_data, scaling, gain, grad_norm):
    weighted = grad_norm * gain
    inner_mean = jnp.mean(weighted * row_data, axis=-1, keepdims=True)
    grad_rows = scaling * weighted - row_data * scaling * scaling * scaling * inner_mean
    grad_gain = jnp.sum(grad_norm * row_data * scaling, axis=0)
    return (grad_rows, grad_gain)


def doc_layout(doc_lengths, valid_lengths, group_rows):
    lengths = doc_lengths[0]
    valid_count = valid_lengths[0]
    doc_ends = jnp.cumsum(lengths)
    doc_starts = doc_ends - lengths
    positions = jnp.arange(group_rows, dtype=jnp.int32)
    doc_ids = jnp.sum((positions[:, None] >= doc_ends[None, :]).astype(jnp.int32), axis=1)
    usable = jnp.any(
        (positions[:, None] >= doc_starts[None, :])
        & (positions[:, None] < (doc_starts + valid_count)[None, :]),
        axis=1,
    )
    return (doc_ids, usable)


def block_mask(doc_ids, usable, start_row, block_rows):
    key_reach = start_row + block_rows
    query_places = start_row + jnp.arange(block_rows, dtype=jnp.int32)
    key_places = jnp.arange(key_reach, dtype=jnp.int32)
    causal = key_places[None, :] <= query_places[:, None]
    same_doc = doc_ids[start_row:key_reach][:, None] == doc_ids[None, :key_reach]
    return causal & same_doc & usable[None, :key_reach]


def score_block(query_part, key_part, allowed, scaling):
    scores = (
        jnp.einsum("qhd,khd->hqk", query_part, key_part, preferred_element_type=jnp.float32)
        * scaling
    )
    return jnp.where(allowed[None], scores, MASKED)


def contract_rows(left, right):
    return lax.dot_general(
        left, right, (((0,), (0,)), ((), ())), preferred_element_type=jnp.float32
    )


def count_rows(id_table, weight_table):
    ngram_count = id_table.shape[0]
    offsets = jnp.arange(ngram_count, dtype=jnp.int32)[:, None] * HASH_ROWS
    flat_ids = (id_table + offsets).reshape(-1)
    counted = jax.ops.segment_sum(
        weight_table.reshape(-1), flat_ids, num_segments=ngram_count * HASH_ROWS
    )
    return counted.reshape(ngram_count, HASH_ROWS)


def shards(
    latents_in,
    gain_one,
    w_qkv,
    w_out,
    gain_two,
    w_gate,
    w_up,
    w_down,
    cotangent,
    doc_lengths,
    valid_lengths,
    hash_ids,
    hash_weights,
):
    local_rows, model_width = latents_in.shape
    tp_count = lax.axis_size("tp")
    group_rows = local_rows * tp_count
    local_width = w_qkv.shape[2]
    heads_local = local_width // HEAD_DIM
    block_rows = min(512, group_rows)
    scaling = HEAD_DIM ** (-0.5)
    doc_ids, usable = doc_layout(doc_lengths, valid_lengths, group_rows)
    row_data = latents_in.astype(jnp.float32)
    normed, scale_one = norm_rows(row_data, gain_one)
    normed_low = normed.astype(jnp.bfloat16)
    normed_all = lax.all_gather(normed_low, "tp", axis=0, tiled=True)
    qkv_weight = w_qkv.reshape(model_width, 3 * local_width)
    mixed_qkv = jnp.dot(normed_all, qkv_weight, preferred_element_type=jnp.float32).astype(
        jnp.bfloat16
    )
    mixed_qkv = mixed_qkv.reshape(group_rows, 3, heads_local, HEAD_DIM)
    queries = mixed_qkv[:, 0]
    key_rows = mixed_qkv[:, 1]
    value_rows = mixed_qkv[:, 2]
    head_blocks = []
    log_blocks = []
    for start_row in range(0, group_rows, block_rows):
        key_reach = start_row + block_rows
        allowed = block_mask(doc_ids, usable, start_row, block_rows)
        scores = score_block(queries[start_row:key_reach], key_rows[:key_reach], allowed, scaling)
        row_max = jnp.max(scores, axis=-1, keepdims=True)
        log_total = row_max + jnp.log(jnp.sum(jnp.exp(scores - row_max), axis=-1, keepdims=True))
        attn_probs = jnp.exp(scores - log_total).astype(jnp.bfloat16)
        head_blocks.append(
            jnp.einsum(
                "hqk,khd->qhd",
                attn_probs,
                value_rows[:key_reach],
                preferred_element_type=jnp.float32,
            ).astype(jnp.bfloat16)
        )
        log_blocks.append(log_total)
    heads_out = jnp.concatenate(head_blocks, axis=0).reshape(group_rows, local_width)
    branch = lax.psum_scatter(
        jnp.dot(heads_out, w_out.T, preferred_element_type=jnp.float32),
        "tp",
        scatter_dimension=0,
        tiled=True,
    )
    hidden = row_data + branch
    normed_two, scale_two = norm_rows(hidden, gain_two)
    normed_two_low = normed_two.astype(jnp.bfloat16)
    normed_two_all = lax.all_gather(normed_two_low, "tp", axis=0, tiled=True)
    gate_val = jnp.dot(normed_two_all, w_gate, preferred_element_type=jnp.float32)
    up_val = jnp.dot(normed_two_all, w_up, preferred_element_type=jnp.float32)
    sigmoid_val = jax.nn.sigmoid(gate_val)
    silu_val = gate_val * sigmoid_val
    activation = (silu_val * up_val).astype(jnp.bfloat16)
    result = hidden + lax.psum_scatter(
        jnp.dot(activation, w_down.T, preferred_element_type=jnp.float32).astype(jnp.bfloat16),
        "tp",
        scatter_dimension=0,
        tiled=True,
    ).astype(jnp.float32)
    latents_out = result.astype(jnp.bfloat16)
    grad_result = cotangent.astype(jnp.float32)
    cot_all = lax.all_gather(cotangent, "tp", axis=0, tiled=True)
    grad_act = jnp.dot(cot_all, w_down, preferred_element_type=jnp.float32)
    grad_down = contract_rows(cot_all, activation)
    grad_gate = (grad_act * up_val * sigmoid_val * (1.0 + gate_val * (1.0 - sigmoid_val))).astype(
        jnp.bfloat16
    )
    grad_up = (grad_act * silu_val).astype(jnp.bfloat16)
    grad_normed_two = lax.psum_scatter(
        jnp.dot(grad_gate, w_gate.T, preferred_element_type=jnp.float32)
        + jnp.dot(grad_up, w_up.T, preferred_element_type=jnp.float32),
        "tp",
        scatter_dimension=0,
        tiled=True,
    )
    grad_w_gate = contract_rows(normed_two_all, grad_gate)
    grad_w_up = contract_rows(normed_two_all, grad_up)
    grad_hidden_norm, grad_gain_two = norm_back(hidden, scale_two, gain_two, grad_normed_two)
    grad_hidden = grad_result + grad_hidden_norm
    grad_branch = grad_hidden.astype(jnp.bfloat16)
    branch_all = lax.all_gather(grad_branch, "tp", axis=0, tiled=True)
    grad_heads = jnp.dot(branch_all, w_out, preferred_element_type=jnp.float32).astype(jnp.bfloat16)
    grad_w_out = contract_rows(branch_all, heads_out)
    grad_heads = grad_heads.reshape(group_rows, heads_local, HEAD_DIM)
    grad_keys = jnp.zeros((group_rows, heads_local, HEAD_DIM), jnp.float32)
    grad_values = jnp.zeros((group_rows, heads_local, HEAD_DIM), jnp.float32)
    query_grads = []
    for number, start_row in enumerate(range(0, group_rows, block_rows)):
        key_reach = start_row + block_rows
        allowed = block_mask(doc_ids, usable, start_row, block_rows)
        query_part = queries[start_row:key_reach]
        key_part = key_rows[:key_reach]
        grad_part = grad_heads[start_row:key_reach]
        scores = score_block(query_part, key_part, allowed, scaling)
        attn_probs = jnp.exp(scores - log_blocks[number])
        probs_low = attn_probs.astype(jnp.bfloat16)
        grad_probs = jnp.einsum(
            "qhd,khd->hqk", grad_part, value_rows[:key_reach], preferred_element_type=jnp.float32
        )
        row_inner = jnp.sum(attn_probs * grad_probs, axis=-1, keepdims=True)
        grad_scores = (attn_probs * (grad_probs - row_inner)).astype(jnp.bfloat16)
        query_grads.append(
            jnp.einsum("hqk,khd->qhd", grad_scores, key_part, preferred_element_type=jnp.float32)
            * scaling
        )
        grad_keys = grad_keys.at[:key_reach].add(
            jnp.einsum("hqk,qhd->khd", grad_scores, query_part, preferred_element_type=jnp.float32)
            * scaling
        )
        grad_values = grad_values.at[:key_reach].add(
            jnp.einsum("hqk,qhd->khd", probs_low, grad_part, preferred_element_type=jnp.float32)
        )
    grad_mixed = jnp.stack([jnp.concatenate(query_grads, axis=0), grad_keys, grad_values], axis=1)
    grad_mixed = grad_mixed.astype(jnp.bfloat16).reshape(group_rows, 3 * local_width)
    grad_normed = lax.psum_scatter(
        jnp.dot(grad_mixed, qkv_weight.T, preferred_element_type=jnp.float32).astype(jnp.bfloat16),
        "tp",
        scatter_dimension=0,
        tiled=True,
    ).astype(jnp.float32)
    grad_w_qkv = contract_rows(normed_all, grad_mixed).reshape(model_width, 3, local_width)
    grad_rows_norm, grad_gain_one = norm_back(row_data, scale_one, gain_one, grad_normed)
    grad_latents = grad_hidden + grad_rows_norm
    hash_counts, gain_one_total, gain_two_total = lax.psum(
        (count_rows(hash_ids, hash_weights), grad_gain_one, grad_gain_two), ("seq", "tp")
    )
    qkv_total, out_total, gate_total, up_total, down_total = (
        lax.psum_scatter(
            grad_w_qkv.astype(jnp.bfloat16), "seq", scatter_dimension=0, tiled=True
        ).astype(jnp.float32),
        lax.psum_scatter(
            grad_w_out.astype(jnp.bfloat16), "seq", scatter_dimension=0, tiled=True
        ).astype(jnp.float32),
        lax.psum_scatter(
            grad_w_gate.astype(jnp.bfloat16), "seq", scatter_dimension=0, tiled=True
        ).astype(jnp.float32),
        lax.psum_scatter(
            grad_w_up.astype(jnp.bfloat16), "seq", scatter_dimension=0, tiled=True
        ).astype(jnp.float32),
        lax.psum_scatter(
            grad_down.astype(jnp.bfloat16), "seq", scatter_dimension=0, tiled=True
        ).astype(jnp.float32),
    )
    return (
        latents_out,
        grad_latents,
        gain_one_total,
        qkv_total,
        out_total,
        gain_two_total,
        gate_total,
        up_total,
        down_total,
        hash_counts,
    )


def solution(mesh):
    in_specs = (
        P(("seq", "tp"), None),
        P(),
        P(None, None, "tp"),
        P(None, "tp"),
        P(),
        P(None, "tp"),
        P(None, "tp"),
        P(None, "tp"),
        P(("seq", "tp"), None),
        P("seq", None),
        P("seq", None),
        P(None, ("seq", "tp")),
        P(None, ("seq", "tp")),
    )
    out_specs = (
        P(("seq", "tp"), None),
        P(("seq", "tp"), None),
        P(),
        P("seq", None, "tp"),
        P("seq", "tp"),
        P(),
        P("seq", "tp"),
        P("seq", "tp"),
        P("seq", "tp"),
        P(),
    )
    return jax.shard_map(shards, mesh=mesh, in_specs=in_specs, out_specs=out_specs, check_vma=False)
```

profile of v0, /device:TPU:0, one launch (start us, length us, event | category | flops | bytes accessed | tf_op | source)
XLA Modules:
  0.0 895.3 jit_solution(16045899847573076391)
XLA Ops:
  19.0 31.2 %all-gather.5.cloned.1.call-done = bf16[2048,1024]{1,0:T(8,128)(2,1)} async-done(((bf16[512,1024]{1,0:T(8,128)(2,1)}), bf16[2048,1024]{1,0:T(8,128)(2,1)}) %all-gather.5.cloned.1.call-update) | async-done | bytes 4194320 | tf_op jit(solution)/shard_map/all_gather | solution.py:101
  98.1 71.8 %reduce-scatter.16.cloned.1.call-done = f32[512,1024]{1,0:T(8,128)} async-done(((f32[2048,1024]{1,0:T(8,128)}), f32[512,1024]{1,0:T(8,128)}) %reduce-scatter.16.cloned.1.call-update) | async-done | bytes 2097168 | tf_op jit(solution)/shard_map/reduce_scatter | solution.py:129
  175.3 34.0 %all-gather.7.cloned.1.call-done = bf16[2048,1024]{1,0:T(8,128)(2,1)} async-done(((bf16[512,1024]{1,0:T(8,128)(2,1)}), bf16[2048,1024]{1,0:T(8,128)(2,1)}) %all-gather.7.cloned.1.call-update) | async-done | bytes 4194320 | tf_op jit(solution)/shard_map/all_gather | solution.py:138
  209.4 8.4 fusion.84
  223.0 22.3 %all-gather.9.cloned.1.call-done = bf16[2048,1024]{1,0:T(8,128)(2,1)} async-done(((bf16[512,1024]{1,0:T(8,128)(2,1)}), bf16[2048,1024]{1,0:T(8,128)(2,1)}) %all-gather.9.cloned.1.call-update) | async-done | bytes 4194320 | tf_op jit(solution)/shard_map/all_gather | solution.py:152
  245.4 10.5 %multiply_convert_fusion.3 = (bf16[2048,704]{0,1:T(8,128)(2,1)S(1)}, bf16[2048,704]{0,1:T(8,128)(2,1)S(1)}, bf16[2048,704]{0,1:T(8,128)(2,1)}) fusion(f32[2048,704]{0,1:T(8,128)} %fusion.84, f32[2048,704]{0,1:T(8,128)} %fusion.85, bf16[2048,1024]{1,0:T(8,128)(2,1)} %all-gather.9.cloned.1.call-done, bf16[1024,704]{0,1:T(8,128)(2,1)S(1)} %copy-done), kind=kOutput, calls=%fused_computation.24 | convolution fusion | flops 2974416896 | bytes 25821184 | tf_op jit(solution)/shard_map/dot_general | solution.py:153
  265.3 71.8 %reduce-scatter.20.cloned.1.call-done = f32[512,1024]{1,0:T(8,128)} async-done(((f32[2048,1024]{1,0:T(8,128)}), f32[512,1024]{1,0:T(8,128)}) %reduce-scatter.20.cloned.1.call-update) | async-done | bytes 2097168 | tf_op jit(solution)/shard_map/reduce_scatter | solution.py:159
  366.8 10.1 %all-gather.11.cloned.1.call-done = bf16[2048,1024]{1,0:T(8,128)(2,1)} async-done(((bf16[512,1024]{1,0:T(8,128)(2,1)}), bf16[2048,1024]{1,0:T(8,128)(2,1)}) %all-gather.11.cloned.1.call-update) | async-done | bytes 4194320 | tf_op jit(solution)/shard_map/all_gather | solution.py:171
  403.6 7.4 multiply_reduce_fusion.1
  411.1 6.9 multiply_convert_fusion.1
  421.9 12.8 %multiply_reduce_fusion = (f32[4,512]{1,0:T(4,128)S(1)}, f32[4,512,2048]{2,1,0:T(8,128)}) fusion(f32[4,512,2048]{2,1,0:T(8,128)} %copy-done.1, f32[4,512]{1,0:T(4,128)S(1)} %copy-done.38, pred[512,2048]{1,0:T(8,128)(4,1)S(1)} %copy-done.10, bf16[512,4,64]{0,2,1:T(8,128)(2,1)S(1)} %bitcast.248, bf16[2048,3,4,64]{0,3,2,1:T(8,128)(2,1)S(1)} %bitcast.238), kind=kOutput, calls=%fused_computation.2 | convolution fusion | flops 557840384 | bytes 35930112 | tf_op jit(solution)/shard_map/qhd,khd->hqk/dot_general | solution.py:187
  434.8 12.2 %multiply_convert_fusion = bf16[4,512,2048]{2,1,0:T(8,128)(2,1)S(1)} fusion(f32[4,512,2048]{2,1,0:T(8,128)} %get-tuple-element.160, f32[4,512,2048]{2,1,0:T(8,128)} %copy-done.1, f32[4,512]{1,0:T(4,128)S(1)} %get-tuple-element.159, f32[4,512]{1,0:T(4,128)S(1)} %copy-done.38, pred[512,2048]{1,0:T(8,128)(4,1)S(1)} %copy-done.10), kind=kLoop, calls=%fused_computation.1 | loop fusion | flops 25165824 | bytes 43008000 | tf_op jit(solution)/shard_map/convert_element_type | solution.py:191
  461.5 8.4 fusion.20
  469.9 7.6 fusion.22
  487.6 7.0 convolution_convert_fusion.1
  494.7 7.0 convolution_convert_fusion
  502.5 21.9 %scatter_custom_fusion = f32[3000012]{0:T(1024)} fusion(s32[3072]{0:T(1024)S(1)} %reshape.646, f32[3072]{0:T(1024)S(1)} %reshape.648, f32[]{:T(128)} %constant.225.clone.1), kind=kCustom, calls=%fused_computation.22 | custom fusion | flops 3072 | bytes 12000052 | tf_op jit(solution)/shard_map/scatter-add | solution.py:69
  524.4 16.5 %reshape.643 = f32[6,500002]{1,0:T(8,128)} reshape(f32[3000012]{0:T(1024)} %scatter_custom_fusion) | data formatting | bytes 24000096 | tf_op jit(solution)/shard_map/reshape | solution.py:72
  548.0 45.8 %reduce-scatter.32.cloned.1.call-done = bf16[128,704]{1,0:T(8,128)(2,1)} async-done(((bf16[1024,704]{1,0:T(8,128)(2,1)}), bf16[128,704]{1,0:T(8,128)(2,1)}) %reduce-scatter.32.cloned.1.call-update) | async-done | bytes 180240
  597.3 83.7 %reduce-scatter.26.cloned.1.call-done = bf16[128,256]{1,0:T(8,128)(2,1)} async-done(((bf16[1024,256]{1,0:T(8,128)(2,1)}), bf16[128,256]{1,0:T(8,128)(2,1)}) %reduce-scatter.26.cloned.1.call-update) | async-done | bytes 65552 | tf_op jit(solution)/shard_map/reduce_scatter | solution.py:221
  682.5 90.9 %reduce-scatter.24.cloned.1.call-done = bf16[128,3,256]{2,0,1:T(8,128)(2,1)} async-done(((bf16[1024,3,256]{2,0,1:T(8,128)(2,1)}), bf16[128,3,256]{2,0,1:T(8,128)(2,1)}) %reduce-scatter.24.cloned.1.call-update) | async-done | bytes 196624 | tf_op jit(solution)/shard_map/reduce_scatter | solution.py:218
  775.1 47.2 %reduce-scatter.22.cloned.1.call-done = bf16[512,1024]{1,0:T(8,128)(2,1)} async-done(((bf16[2048,1024]{1,0:T(8,128)(2,1)}), bf16[512,1024]{1,0:T(8,128)(2,1)}) %reduce-scatter.22.cloned.1.call-update) | async-done | bytes 1048592 | tf_op jit(solution)/shard_map/reduce_scatter | solution.py:205
  825.5 41.3 %all-reduce.2 = (f32[1024]{0:T(1024)}, f32[1024]{0:T(1024)}) all-reduce(f32[1024]{0:T(1024)} %get-tuple-element.124, f32[1024]{0:T(1024)} %get-tuple-element.122), channel_id=1, replica_groups=mesh['seq'=8,'tp'=4] {'seq','tp'}, use_global_device_ids=true, to_apply=%region_24.25 | all-reduce | flops 2048 | bytes 16384 | tf_op jit(solution)/shard_map/psum | solution.py:214
  876.6 11.1 %copy.63 = f32[6,500002]{1,0:T(8,128)} copy(f32[6,500002]{1,0:T(8,128)} %all-reduce.5.cloned.1.call-done) | data formatting | bytes 24000096
  (263 shorter events, 190.5 us)
Async XLA Ops:
  8.0 237.4 %copy-start = (bf16[1024,704]{0,1:T(8,128)(2,1)S(1)}, bf16[1024,704]{0,1:T(8,128)(2,1)}, u32[]{:S(2)}) copy-start(bf16[1024,704]{0,1:T(8,128)(2,1)} %param.40) | copy-start | bytes 4325380
  8.1 42.2 %all-gather.5.cloned.1.call-start = ((), (), s32[]{:S(2)}) async-start(), calls=%async_computation.9 | async-start | bytes 5242880 | tf_op jit(solution)/shard_map/all_gather | solution.py:101
  12.9 157.0 %reduce-scatter.16.cloned.1.call-start = ((), (), s32[]{:S(2)}) async-start(), calls=%async_computation.10 | async-start | bytes 10485760 | tf_op jit(solution)/shard_map/reduce_scatter | solution.py:129
  15.4 75.6 %copy-start.22 = (pred[512,512]{0,1:T(8,128)(4,1)}, pred[512,512]{0,1:T(8,128)(4,1)S(1)}, u32[]{:S(2)}) copy-start(pred[512,512]{0,1:T(8,128)(4,1)S(1)} %fusion.60) | copy-start | bytes 786436
  18.1 46.2 %copy-start.9 = (pred[512,2048]{1,0:T(8,128)(4,1)}, pred[512,2048]{1,0:T(8,128)(4,1)S(1)}, u32[]{:S(2)}) copy-start(pred[512,2048]{1,0:T(8,128)(4,1)S(1)} %fusion.12) | copy-start | bytes 3145732
  19.0 58.0 %copy-start.13 = (pred[512,1536]{1,0:T(8,128)(4,1)}, pred[512,1536]{1,0:T(8,128)(4,1)S(1)}, u32[]{:S(2)}) copy-start(pred[512,1536]{1,0:T(8,128)(4,1)S(1)} %fusion.15) | copy-start | bytes 2359300
  98.0 111.3 %all-gather.7.cloned.1.call-start = ((), (), s32[]{:S(2)}) async-start(), calls=%async_computation.11 | async-start | bytes 5242880 | tf_op jit(solution)/shard_map/all_gather | solution.py:138
  172.1 167.9 %copy-start.4 = (f32[512,1024]{1,0:T(8,128)}, f32[512,1024]{1,0:T(8,128)S(1)}, u32[]{:S(2)}) copy-start(f32[512,1024]{1,0:T(8,128)S(1)} %get-tuple-element.129) | copy-start | bytes 6291460
  174.7 70.6 %all-gather.9.cloned.1.call-start = ((), (), s32[]{:S(2)}) async-start(), calls=%async_computation.13 | async-start | bytes 5242880 | tf_op jit(solution)/shard_map/all_gather | solution.py:152
  175.3 161.8 %reduce-scatter.20.cloned.1.call-start = ((), (), s32[]{:S(2)}) async-start(), calls=%async_computation.14 | async-start | bytes 10485760 | tf_op jit(solution)/shard_map/reduce_scatter | solution.py:159
  265.2 111.7 %all-gather.11.cloned.1.call-start = ((), (), s32[]{:S(2)}) async-start(), calls=%async_computation.15 | async-start | bytes 5242880 | tf_op jit(solution)/shard_map/all_gather | solution.py:171
  342.3 198.7 %reduce-scatter.28.cloned.1.call-start = ((), (), s32[]{:S(2)}) async-start(), calls=%async_computation.20 | async-start | bytes 1769472
  350.4 194.1 %reduce-scatter.30.cloned.1.call-start = ((), (), s32[]{:S(2)}) async-start(), calls=%async_computation.21 | async-start | bytes 1769472
  358.9 235.0 %reduce-scatter.32.cloned.1.call-start = ((), (), s32[]{:S(2)}) async-start(), calls=%async_computation.22 | async-start | bytes 1769472
  366.8 314.2 %reduce-scatter.26.cloned.1.call-start = ((), (), s32[]{:S(2)}) async-start(), calls=%async_computation.18 | async-start | bytes 589824 | tf_op jit(solution)/shard_map/reduce_scatter | solution.py:221
  477.5 295.9 %reduce-scatter.24.cloned.1.call-start = ((), (), s32[]{:S(2)}) async-start(), calls=%async_computation.17 | async-start | bytes 1769472 | tf_op jit(solution)/shard_map/reduce_scatter | solution.py:218
  487.6 334.8 %reduce-scatter.22.cloned.1.call-start = ((), (), s32[]{:S(2)}) async-start(), calls=%async_computation.16 | async-start | bytes 5242880 | tf_op jit(solution)/shard_map/reduce_scatter | solution.py:205
  494.7 377.1 %reduce-scatter.18.cloned.1.call-start = ((), (), s32[]{:S(2)}) async-start(), calls=%async_computation.12 | async-start | bytes 5242880 | tf_op jit(solution)/shard_map/reduce_scatter | solution.py:144
  501.7 374.9 %all-reduce.5.cloned.1.call-start = ((), (), s32[]{:S(2)}) async-start(), calls=%async_computation.19 | async-start | bytes 32006144 | tf_op jit(solution)/shard_map/psum | solution.py:214
  540.9 281.5 %copy-start.44 = (f32[1024]{0:T(1024)S(1)}, f32[1024]{0:T(1024)}, u32[]{:S(2)}) copy-start(f32[1024]{0:T(1024)} %param.34) | copy-start | bytes 12292
  540.9 281.5 %copy-start.46 = (f32[512]{0:T(512)S(1)}, f32[512]{0:T(512)}, u32[]{:S(2)}) copy-start(f32[512]{0:T(512)} %copy-done.45) | copy-start | bytes 6148
  540.9 330.9 %copy-start.5 = (f32[512,1024]{1,0:T(8,128)S(1)}, f32[512,1024]{1,0:T(8,128)}, u32[]{:S(2)}) copy-start(f32[512,1024]{1,0:T(8,128)} %copy-done.4) | copy-start | bytes 6291460
  540.9 330.9 %copy-start.40 = (f32[1024]{0:T(1024)S(1)}, f32[1024]{0:T(1024)}, u32[]{:S(2)}) copy-start(f32[1024]{0:T(1024)} %param.37) | copy-start | bytes 12292
  540.9 330.9 %copy-start.43 = (f32[512]{0:T(512)S(1)}, f32[512]{0:T(512)}, u32[]{:S(2)}) copy-start(f32[512]{0:T(512)} %copy-done.41) | copy-start | bytes 6148
  (59 other events, 332.5 us)
Sparse Core Ops, SparseCore 0:
  13.0 37.1 all-gather.4
  98.1 71.7 reduce-scatter.15
  174.8 34.4 all-gather.6
  210.8 34.4 all-gather.8
  265.3 71.6 reduce-scatter.19
  342.4 34.4 all-gather.10
  380.4 64.9 reduce-scatter.27
  449.2 63.8 reduce-scatter.29
  516.5 77.3 reduce-scatter.31
  597.4 83.4 reduce-scatter.25
  685.0 88.3 reduce-scatter.23
  776.0 46.3 reduce-scatter.21
  824.9 46.9 reduce-scatter.17
Sparse Core Ops, SparseCore 1:
  541.0 305.6 all-reduce.4
where the time goes:
time: 904 us; the launch traced here: 895 us
  waiting for transfers between devices  514 us (57%)
  matrix products  175 us (19%)
  other arithmetic  97.4 us (11%)
  local copies, waits for them, and re-layouts  50.5 us (6%)
  blocking collectives  41.3 us (5%)
  between operations  16.7 us (2%)
    reduce_scatter x1, waiting for transfers between devices, shards(): lax.psum_scatter(grad_w_qkv.astype(jnp.bfloat16), 'seq', scatter_dimensio...  90.9 us
    reduce_scatter x1, waiting for transfers between devices, shards(): lax.psum_scatter(grad_w_out.astype(jnp.bfloat16), 'seq', scatter_dimensio...  83.7 us
    reduce_scatter x1, waiting for transfers between devices, shards(): lax.psum_scatter(jnp.dot(heads_out, w_out.T, preferred_element_type=jnp.f...  71.8 us
    reduce_scatter x1, waiting for transfers between devices, shards(): lax.psum_scatter(jnp.dot(grad_gate, w_gate.T, preferred_element_type=jnp....  71.8 us
    reduce_scatter x1, waiting for transfers between devices, shards(): lax.psum_scatter(jnp.dot(grad_mixed, qkv_weight.T, preferred_element_type...  47.2 us
    unnamed x17, waiting for transfers between devices  46.6 us
    psum x1, blocking collectives, shards(): lax.psum((count_rows(hash_ids, hash_weights), grad_gain_one, grad_gain_tw...  41.3 us
    all_gather x1, waiting for transfers between devices, shards(): normed_two_all = lax.all_gather(normed_two_low, 'tp', axis=0, tiled=True)  34 us
  transfers between devices with their start and end apart: 14, of which 11 were waited for; matrix products, arithmetic and copies ran while one was open for 25% of the time, Pallas kernels for 0%

commit v1 on v0

v1 whole, which is shorter than its diff:
```python
import functools

import jax
import jax.numpy as jnp
from jax import lax
from jax.experimental import pallas as pl
from jax.experimental.pallas import tpu as pltpu
from jax.sharding import PartitionSpec as P

HEAD_DIM = 64
EPSILON = 1e-05
MASKED = -1e30
BF = jnp.bfloat16
F32 = jnp.float32
QB = 256
VMEM_BYTES = 56 * 1024 * 1024


def flip(x, axis, bits):
    count = lax.axis_size(axis)
    return lax.ppermute(x, axis, [(i, i ^ bits) for i in range(count)])


def dot(a, b):
    return lax.dot_general(a, b, (((1,), (0,)), ((), ())), preferred_element_type=F32)


def cost(flops, moved):
    return pl.CostEstimate(flops=flops, bytes_accessed=moved, transcendentals=0)


def params():
    return pltpu.CompilerParams(vmem_limit_bytes=VMEM_BYTES)


def whole(shape):
    return pl.BlockSpec(shape, lambda i, sc: (0,) * len(shape))


def gather_rows(x):
    across = flip(x, "tp", 2)
    return [x, flip(x, "tp", 1), across, flip(across, "tp", 1)]


def scatter_far(part_two, part_three):
    both = (part_two.astype(F32) + flip(part_three, "tp", 1).astype(F32)).astype(BF)
    return flip(both, "tp", 2)


def scatter_sum(part_zero, part_one, far):
    return part_zero.astype(F32) + flip(part_one, "tp", 1).astype(F32) + far.astype(F32)


def norm_rows(row_data, gain):
    scaling = lax.rsqrt(jnp.mean(row_data * row_data, axis=-1, keepdims=True) + EPSILON)
    return (row_data * scaling * gain, scaling)


def norm_back(row_data, scaling, gain, grad_norm):
    weighted = grad_norm * gain
    inner_mean = jnp.mean(weighted * row_data, axis=-1, keepdims=True)
    grad_rows = scaling * weighted - row_data * scaling * scaling * scaling * inner_mean
    grad_gain = jnp.sum(grad_norm * row_data * scaling, axis=0)
    return (grad_rows, grad_gain)


def qkv_kernel(sc, a_ref, b_ref, w_ref, *rest):
    out_ref = rest[-1]
    step = pl.program_id(0)

    @pl.when(step < 2)
    def _():
        out_ref[...] = dot(a_ref[...], w_ref[...]).astype(BF)

    @pl.when(step >= 2)
    def _():
        out_ref[...] = dot(b_ref[...], w_ref[...]).astype(BF)


def qkv_call(sc, first, a, b, w, into):
    half, width = a.shape[0] // 2, w.shape[1]
    rows = 4 * a.shape[0]
    pair = lambda which: pl.BlockSpec(
        (half, a.shape[1]), lambda i, sc: (jnp.clip(i - 2 * which, 0, 1), 0)
    )
    extra = [] if into is None else [into]
    return pl.pallas_call(
        qkv_kernel,
        grid_spec=pltpu.PrefetchScalarGridSpec(
            num_scalar_prefetch=1,
            grid=(4,),
            in_specs=[pair(0), pair(1), whole(w.shape)] + [pl.BlockSpec(memory_space=pl.ANY)] * len(extra),
            out_specs=pl.BlockSpec(
                (half, width), lambda i, sc: ((sc[0] ^ (first + i // 2)) * 2 + i % 2, 0)
            ),
        ),
        out_shape=jax.ShapeDtypeStruct((rows, width), BF),
        input_output_aliases={4: 0} if extra else {},
        compiler_params=params(),
        cost_estimate=cost(2 * 2 * a.shape[0] * a.shape[1] * width, 4_000_000),
        name="qkv",
    )(sc, a, b, w, *extra)


def doc_bounds(sc, places):
    low = jnp.where(places >= sc[2], sc[2], jnp.where(places >= sc[1], sc[1], 0))
    end = jnp.where(places >= sc[2], sc[5], jnp.where(places >= sc[1], sc[4], sc[3]))
    return low, jnp.minimum(places, end - 1)


def head_rows(x, h):
    where = lax.broadcasted_iota(jnp.int32, x.shape, 0) // HEAD_DIM
    return jnp.where(where == h, x, jnp.zeros_like(x))


def head_lanes(x, h):
    where = lax.broadcasted_iota(jnp.int32, x.shape, 1) // HEAD_DIM
    return jnp.where(where == h, x, jnp.zeros_like(x))


def attend_kernel(first, heads, sc, qkv_ref, wo_ref, *rest):
    heads_ref, lse_ref, pa_ref, pb_ref, vt_ref, qt_ref, acc_ref = rest[-7:]
    width = heads * HEAD_DIM
    step = pl.program_id(0)

    @pl.when(step == 0)
    def _():
        for n in range(qkv_ref.shape[0] // QB):
            vt_ref[:, n * QB : (n + 1) * QB] = qkv_ref[n * QB : (n + 1) * QB, 2 * width :].T

    rank = first + 1 - step // 2
    start = (sc[0] ^ rank) * (2 * QB) + (step % 2) * QB
    start = pl.multiple_of(start, QB)
    q_t = qkv_ref[pl.ds(start, QB), :width].T * jnp.asarray(HEAD_DIM**-0.5, BF)
    for h in range(heads):
        qt_ref[h] = head_rows(q_t, h)
    acc_ref[...] = jnp.zeros_like(acc_ref)
    places = start + lax.broadcasted_iota(jnp.int32, (1, QB), 1)
    low, high = doc_bounds(sc, places)
    low_first, _ = doc_bounds(sc, start)

    def body(kb, state):
        at = pl.multiple_of(kb * QB, QB)
        keys = qkv_ref[pl.ds(at, QB), width : 2 * width]
        value_t = vt_ref[:, pl.ds(at, QB)]
        spot = at + lax.broadcasted_iota(jnp.int32, (QB, QB), 0)
        allowed = (spot >= low) & (spot <= high)
        fresh = []
        for h in range(heads):
            top, total = state[h]
            scores = jnp.where(allowed, dot(keys, qt_ref[h]), MASKED)
            new_top = jnp.maximum(top, jnp.max(scores, axis=0, keepdims=True))
            fade = jnp.exp(top - new_top)
            probs = jnp.exp(scores - new_top)
            total = total * fade + jnp.sum(probs, axis=0, keepdims=True)
            part = slice(h * HEAD_DIM, (h + 1) * HEAD_DIM)
            acc_ref[part] = acc_ref[part] * fade + dot(value_t[part], probs.astype(BF))
            fresh.append((new_top, total))
        return tuple(fresh)

    begin = tuple(
        (jnp.full((1, QB), MASKED, F32), jnp.zeros((1, QB), F32)) for _ in range(heads)
    )
    state = lax.fori_loop(low_first // QB, start // QB + 1, body, begin)
    lse_ref[...] = jnp.zeros_like(lse_ref)
    for h in range(heads):
        top, total = state[h]
        part = slice(h * HEAD_DIM, (h + 1) * HEAD_DIM)
        acc_ref[part] = acc_ref[part] * (1.0 / total)
        lse_ref[h : h + 1] = top + jnp.log(total)
    out = acc_ref[...].T.astype(BF)
    heads_ref[...] = out
    partial = dot(out, wo_ref[...]).astype(BF)

    @pl.when(step < 2)
    def _():
        pa_ref[...] = partial

    @pl.when(step >= 2)
    def _():
        pb_ref[...] = partial


def attend_call(sc, first, qkv, wo_t, heads_into, lse_into):
    rows, width = qkv.shape[0], qkv.shape[1] // 3
    heads = width // HEAD_DIM
    model = wo_t.shape[1]
    half = rows // 8
    assert half == QB
    extra = [] if heads_into is None else [heads_into, lse_into]
    spot = lambda i: 2 * (first + 1 - i // 2) + i % 2
    pair = lambda which: pl.BlockSpec(
        (half, model), lambda i, sc: (jnp.clip(i - 2 * which, 0, 1), 0)
    )
    return pl.pallas_call(
        functools.partial(attend_kernel, first, heads),
        grid_spec=pltpu.PrefetchScalarGridSpec(
            num_scalar_prefetch=1,
            grid=(4,),
            in_specs=[whole(qkv.shape), whole(wo_t.shape)]
            + [pl.BlockSpec(memory_space=pl.ANY)] * len(extra),
            out_specs=[
                pl.BlockSpec((half, width), lambda i, sc: (spot(i), 0)),
                pl.BlockSpec((8, half), lambda i, sc: (0, spot(i))),
                pair(0),
                pair(1),
            ],
            scratch_shapes=[
                pltpu.VMEM((width, rows), BF),
                pltpu.VMEM((heads, width, QB), BF),
                pltpu.VMEM((width, QB), F32),
            ],
        ),
        out_shape=[
            jax.ShapeDtypeStruct((rows, width), BF),
            jax.ShapeDtypeStruct((8, rows), F32),
            jax.ShapeDtypeStruct((rows // 4, model), BF),
            jax.ShapeDtypeStruct((rows // 4, model), BF),
        ],
        input_output_aliases={3: 0, 4: 1} if extra else {},
        compiler_params=params(),
        cost_estimate=cost(6_000_000_000, 8_000_000),
        name="attend",
    )(sc, qkv, wo_t, *extra)


def attend_back_kernel(first, last, heads, sc, ga_ref, gb_ref, wo_ref, qkv_ref, heads_ref, lse_ref, *rest):
    width = heads * HEAD_DIM
    kt_ref, qt_ref, gt_ref, qs_ref, gs_ref, dqt_ref = rest[-6:]
    if last:
        dq_in, dk_in, dv_in, mixed_ref, dk_ref, dv_ref = rest[:-6]
    else:
        dq_ref, dk_ref, dv_ref = rest[:-6]
    step = pl.program_id(0)
    rows = qkv_ref.shape[0]

    @pl.when(step == 0)
    def _():
        for n in range(rows // QB):
            kt_ref[:, n * QB : (n + 1) * QB] = qkv_ref[n * QB : (n + 1) * QB, width : 2 * width].T
        if last:
            dk_ref[...] = dk_in[...]
            dv_ref[...] = dv_in[...]
            mixed_ref[: rows // 2, :width] = dq_in[...]
        else:
            dk_ref[...] = jnp.zeros_like(dk_ref)
            dv_ref[...] = jnp.zeros_like(dv_ref)

    rank = first + step // 2
    start = (sc[0] ^ rank) * (2 * QB) + (step % 2) * QB
    start = pl.multiple_of(start, QB)

    @pl.when(step < 2)
    def _():
        gs_ref[:QB] = dot(ga_ref[...], wo_ref[...]).astype(BF)

    @pl.when(step >= 2)
    def _():
        gs_ref[:QB] = dot(gb_ref[...], wo_ref[...]).astype(BF)

    grad = gs_ref[:QB]
    grad_t = grad.T
    out_t = heads_ref[...].T
    product = grad_t.astype(F32) * out_t.astype(F32)
    query = qkv_ref[pl.ds(start, QB), :width] * jnp.asarray(HEAD_DIM**-0.5, BF)
    q_t = query.T
    inner = []
    for h in range(heads):
        part = slice(h * HEAD_DIM, (h + 1) * HEAD_DIM)
        inner.append(jnp.sum(product[part], axis=0, keepdims=True))
        qt_ref[h] = head_rows(q_t, h)
        gt_ref[h] = head_rows(grad_t, h)
        qs_ref[h * QB : (h + 1) * QB] = head_lanes(query, h)
        gs_ref[h * QB : (h + 1) * QB] = head_lanes(grad, h)
    dqt_ref[...] = jnp.zeros_like(dqt_ref)
    places = start + lax.broadcasted_iota(jnp.int32, (1, QB), 1)
    low, high = doc_bounds(sc, places)
    low_first, _ = doc_bounds(sc, start)

    def body(kb, carry):
        at = pl.multiple_of(kb * QB, QB)
        keys = qkv_ref[pl.ds(at, QB), width : 2 * width]
        values = qkv_ref[pl.ds(at, QB), 2 * width :]
        spot = at + lax.broadcasted_iota(jnp.int32, (QB, QB), 0)
        allowed = (spot >= low) & (spot <= high)
        all_probs, all_grads = [], []
        for h in range(heads):
            part = slice(h * HEAD_DIM, (h + 1) * HEAD_DIM)
            scores = jnp.where(allowed, dot(keys, qt_ref[h]), MASKED)
            probs = jnp.exp(scores - lse_ref[h : h + 1])
            grad_probs = dot(values, gt_ref[h])
            grad_scores = (probs * (grad_probs - inner[h])).astype(BF)
            all_probs.append(probs.astype(BF))
            all_grads.append(grad_scores)
            dqt_ref[part] += dot(kt_ref[part, pl.ds(at, QB)], grad_scores)
        dv_ref[pl.ds(at, QB)] += dot(jnp.concatenate(all_probs, axis=1), gs_ref[...])
        dk_ref[pl.ds(at, QB)] += dot(jnp.concatenate(all_grads, axis=1), qs_ref[...])
        return carry

    lax.fori_loop(low_first // QB, start // QB + 1, body, 0)
    dq = (dqt_ref[...] * HEAD_DIM**-0.5).T.astype(BF)
    if not last:
        dq_ref[...] = dq
    else:
        to = rows // 2 + step * QB
        mixed_ref[pl.ds(pl.multiple_of(to, QB), QB), :width] = dq

        @pl.when(step == 3)
        def _():
            for r in range(4):
                take = pl.ds(pl.multiple_of((sc[0] ^ r) * 2 * QB, QB), 2 * QB)
                put = slice(r * 2 * QB, (r + 1) * 2 * QB)
                mixed_ref[put, width : 2 * width] = dk_ref[take].astype(BF)
                mixed_ref[put, 2 * width :] = dv_ref[take].astype(BF)


def attend_back_call(sc, first, ga, gb, wo, qkv, heads_out, lse, earlier):
    rows, width = qkv.shape[0], qkv.shape[1] // 3
    heads = width // HEAD_DIM
    model = wo.shape[0]
    half = rows // 8
    last = earlier is not None
    pair = lambda which: pl.BlockSpec(
        (half, model), lambda i, sc: (jnp.clip(i - 2 * which, 0, 1), 0)
    )
    in_specs = [
        pair(0),
        pair(1),
        whole(wo.shape),
        whole(qkv.shape),
        pl.BlockSpec((half, width), lambda i, sc: (2 * first + i, 0)),
        pl.BlockSpec((8, half), lambda i, sc: (0, 2 * first + i)),
    ]
    sums = jax.ShapeDtypeStruct((rows, width), F32)
    scratch = [
        pltpu.VMEM((width, rows), BF),
        pltpu.VMEM((heads, width, QB), BF),
        pltpu.VMEM((heads, width, QB), BF),
        pltpu.VMEM((heads * QB, width), BF),
        pltpu.VMEM((heads * QB, width), BF),
        pltpu.VMEM((width, QB), F32),
    ]
    if last:
        in_specs += [whole((rows // 2, width)), whole((rows, width)), whole((rows, width))]
        out_shape = jax.ShapeDtypeStruct((rows, 3 * width), BF)
        out_specs = whole((rows, 3 * width))
        scratch = [pltpu.VMEM((rows, width), F32), pltpu.VMEM((rows, width), F32)] + scratch
    else:
        out_shape = [jax.ShapeDtypeStruct((rows // 2, width), BF), sums, sums]
        out_specs = [
            pl.BlockSpec((half, width), lambda i, sc: (i, 0)),
            whole((rows, width)),
            whole((rows, width)),
        ]
    return pl.pallas_call(
        functools.partial(attend_back_kernel, first, last, heads),
        grid_spec=pltpu.PrefetchScalarGridSpec(
            num_scalar_prefetch=1,
            grid=(4,),
            in_specs=in_specs,
            out_specs=out_specs,
            scratch_shapes=scratch,
        ),
        out_shape=out_shape,
        compiler_params=params(),
        cost_estimate=cost(12_000_000_000, 12_000_000),
        name="attend_back",
    )(sc, ga, gb, wo, qkv, heads_out, lse, *(earlier or ()))


def feed_kernel(na_ref, nb_ref, ca_ref, cb_ref, wg_ref, wu_ref, wd_ref, wgt_ref, wut_ref, wdt_ref, *rest):
    act_ref, gg_ref, gu_ref, nall_ref, call_ref, da_ref, db_ref, xa_ref, xb_ref = rest[-9:]
    step = pl.program_id(0)

    @pl.when(step < 2)
    def _():
        nall_ref[...] = na_ref[...]
        call_ref[...] = ca_ref[...]

    @pl.when(step >= 2)
    def _():
        nall_ref[...] = nb_ref[...]
        call_ref[...] = cb_ref[...]

    normed = nall_ref[...]
    gate = dot(normed, wg_ref[...])
    up = dot(normed, wu_ref[...])
    sig = jax.nn.sigmoid(gate)
    silu = gate * sig
    act = (silu * up).astype(BF)
    act_ref[...] = act
    grad_act = dot(call_ref[...], wd_ref[...])
    grad_gate = (grad_act * up * sig * (1.0 + gate * (1.0 - sig))).astype(BF)
    grad_up = (grad_act * silu).astype(BF)
    gg_ref[...] = grad_gate
    gu_ref[...] = grad_up
    back = (dot(grad_gate, wgt_ref[...]) + dot(grad_up, wut_ref[...])).astype(BF)
    down = dot(act, wdt_ref[...]).astype(BF)

    @pl.when(step < 2)
    def _():
        xa_ref[...] = back
        da_ref[...] = down

    @pl.when(step >= 2)
    def _():
        xb_ref[...] = back
        db_ref[...] = down


def feed_call(order, na, nb, ca, cb, weights, into):
    rows, model = na.shape
    half = rows // 2
    units = weights[0].shape[1]
    total = 4 * rows
    one = lambda shape: pl.BlockSpec(shape, lambda i: (0, 0))
    pair = lambda which: pl.BlockSpec((half, model), lambda i: (jnp.clip(i - 2 * which, 0, 1), 0))
    spot = lambda i: 2 * jnp.where(i < 2, order[0], order[1]) + i % 2
    place = lambda wide: pl.BlockSpec((half, wide), lambda i: (spot(i), 0))
    extra = [] if into is None else list(into)
    shape = lambda r, c: jax.ShapeDtypeStruct((r, c), BF)
    return pl.pallas_call(
        feed_kernel,
        grid=(4,),
        in_specs=[pair(0), pair(1), pair(0), pair(1)]
        + [one(w.shape) for w in weights]
        + [pl.BlockSpec(memory_space=pl.ANY)] * len(extra),
        out_specs=[place(units)] * 3 + [place(model)] * 2 + [pair(0), pair(1), pair(0), pair(1)],
        out_shape=[shape(total, units)] * 3 + [shape(total, model)] * 2 + [shape(rows, model)] * 4,
        input_output_aliases={10 + k: k for k in range(len(extra))},
        compiler_params=params(),
        cost_estimate=cost(6 * 2 * 2 * rows * model * units, 20_000_000),
        name="feed",
    )(na, nb, ca, cb, *weights, *extra)


LANES = 256
CHUNK = 1024


def hash_kernel(tables, base_ref, pack_ref, out_ref):
    table = base_ref[0] + pl.program_id(0)
    places = out_ref.shape[1]
    count = pack_ref.shape[1] // CHUNK

    def body(n, total):
        cut = pl.ds(pl.multiple_of(n * CHUNK, CHUNK), CHUNK)
        ids = pack_ref[pl.ds(table, 1), cut].astype(jnp.int32) - base_ref[1]
        weights = pack_ref[pl.ds(table + tables, 1), cut]
        high = lax.broadcasted_iota(jnp.int32, (places, CHUNK), 0) == (ids >> 8)
        low = lax.broadcasted_iota(jnp.int32, (LANES, CHUNK), 0) == (ids & (LANES - 1))
        high = jnp.where(high, 1.0, 0.0).astype(BF)
        low = jnp.where(low, weights, 0.0).astype(BF)
        return total + lax.dot_general(
            high, low, (((1,), (1,)), ((), ())), preferred_element_type=F32
        )

    total = lax.fori_loop(0, count, body, jnp.zeros((places, LANES), F32))
    out_ref[0] = total.astype(BF)


def hash_call(pack, tables, core, seq, places):
    mine = tables // 2
    return pl.pallas_call(
        functools.partial(hash_kernel, tables),
        grid_spec=pltpu.PrefetchScalarGridSpec(
            num_scalar_prefetch=1,
            grid=(mine,),
            in_specs=[whole(pack.shape)],
            out_specs=pl.BlockSpec((1, places, LANES), lambda i, sc: (i, 0, 0)),
        ),
        out_shape=jax.ShapeDtypeStruct((mine, places, LANES), BF),
        compiler_params=params(),
        cost_estimate=cost(20_000_000_000, 2_000_000),
        name="hash_sums",
    )(jnp.stack([core * mine, seq * places * LANES]).astype(jnp.int32), pack)


def spread_kernel(sc, em_ref, om_ref, es_ref, os_ref, out_ref, flat_ref):
    mine, places = em_ref.shape[1], em_ref.shape[2]
    odd = (pl.program_id(0) ^ sc[1]) % 2

    def put(m_ref, s_ref):
        for k in range(mine):
            for ref, first in ((m_ref, sc[0] * mine), (s_ref, (1 - sc[0]) * mine)):
                at = pl.multiple_of((first + k) * places, 8)
                flat_ref[pl.ds(at, places)] = ref[0, k].astype(F32)

    @pl.when(odd == 0)
    def _():
        put(em_ref, es_ref)

    @pl.when(odd == 1)
    def _():
        put(om_ref, os_ref)

    def body(n, carry):
        for u in range(8):
            row = n * 8 + u
            out_ref[:, pl.ds(pl.multiple_of(row * LANES, LANES), LANES)] = jnp.concatenate(
                [flat_ref[pl.ds(k * places + row, 1), :] for k in range(2 * mine)], axis=0
            )
        return carry

    lax.fori_loop(0, places // 8, body, 0)


def spread_call(even_mine, odd_mine, even_sib, odd_sib, core, seq, hash_rows):
    halves, mine, places, lanes = even_mine.shape
    piece = pl.BlockSpec((1, mine, places, lanes), lambda i, sc: ((i ^ sc[1]) // 2, 0, 0, 0))
    return pl.pallas_call(
        spread_kernel,
        grid_spec=pltpu.PrefetchScalarGridSpec(
            num_scalar_prefetch=1,
            grid=(2 * halves,),
            in_specs=[piece] * 4,
            out_specs=pl.BlockSpec((2 * mine, places * lanes), lambda i, sc: (0, i)),
            scratch_shapes=[pltpu.VMEM((2 * mine * places, lanes), F32)],
        ),
        out_shape=jax.ShapeDtypeStruct((2 * mine, hash_rows), F32),
        compiler_params=params(),
        cost_estimate=cost(1_000_000, 24_000_000),
        name="hash_spread",
    )(jnp.stack([core, seq]).astype(jnp.int32), even_mine, odd_mine, even_sib, odd_sib)


HASH_ROWS = 500002


def hash_tables(hash_ids, hash_weights, core, seq):
    tables = hash_ids.shape[0]
    seq_count = lax.axis_size("seq")
    per_seq = -(-HASH_ROWS // seq_count)
    places = -(-per_seq // (LANES * 8)) * 8
    blank = jnp.zeros((16 - 2 * tables, hash_ids.shape[1]), F32)
    pack = jnp.concatenate([hash_ids.astype(F32), hash_weights, blank], axis=0)
    pack = lax.all_gather(pack, ("seq", "tp"), axis=1, tiled=True)
    mine = hash_call(pack, tables, core, seq, places)
    even = jnp.stack([mine] + [flip(mine, "seq", 2 * j) for j in range(1, seq_count // 2)])
    odd = flip(even, "seq", 1)
    return spread_call(
        even, odd, flip(even, "tp", 1), flip(odd, "tp", 1), core, seq, HASH_ROWS
    )


def contract_rows(left, right):
    return lax.dot_general(
        left, right, (((0,), (0,)), ((), ())), preferred_element_type=F32
    )


def scatter_weights(grad, seq):
    count = lax.axis_size("seq")
    rows, wide = grad.shape
    parts = grad.astype(BF).reshape(count // 2, 2, rows // count, wide)
    bit = seq % 2
    keep = lax.dynamic_index_in_dim(parts, bit, 1, keepdims=False)
    send = lax.dynamic_index_in_dim(parts, 1 - bit, 1, keepdims=False)
    half = (keep.astype(F32) + flip(send, "seq", 1).astype(F32)).astype(BF)
    place = seq // 2
    total = lax.dynamic_index_in_dim(half, place, 0, keepdims=False).astype(F32)
    for j in range(1, count // 2):
        piece = lax.dynamic_index_in_dim(half, place ^ j, 0, keepdims=False)
        total = total + flip(piece, "seq", 2 * j).astype(F32)
    return total


def shards(
    latents_in,
    gain_one,
    w_qkv,
    w_out,
    gain_two,
    w_gate,
    w_up,
    w_down,
    cotangent,
    doc_lengths,
    valid_lengths,
    hash_ids,
    hash_weights,
):
    local_rows, model_width = latents_in.shape
    local_width = w_qkv.shape[2]
    rank = lax.axis_index("tp")
    seq = lax.axis_index("seq")
    core = rank % 2
    lengths, valid = doc_lengths[0], valid_lengths[0]
    start_one = lengths[0]
    start_two = lengths[0] + lengths[1]
    sc = jnp.stack(
        [rank, start_one, start_two, valid[0], start_one + valid[1], start_two + valid[2]]
    ).astype(jnp.int32)

    row_data = latents_in.astype(F32)
    normed, scale_one = norm_rows(row_data, gain_one)
    one = gather_rows(normed.astype(BF))
    qkv_weight = w_qkv.reshape(model_width, 3 * local_width)
    qkv = qkv_call(sc, 0, one[0], one[1], qkv_weight, None)
    qkv = qkv_call(sc, 2, one[2], one[3], qkv_weight, qkv)
    wo_t = w_out.T
    heads_out, lse, part_three, part_two = attend_call(sc, 2, qkv, wo_t, None, None)
    far = scatter_far(part_two, part_three)
    heads_out, lse, part_one, part_zero = attend_call(sc, 0, qkv, wo_t, heads_out, lse)
    hidden = row_data + scatter_sum(part_zero, part_one, far)
    normed_two, scale_two = norm_rows(hidden, gain_two)
    two = gather_rows(normed_two.astype(BF))
    cot = gather_rows(cotangent)
    weights = (w_gate, w_up, w_down, w_gate.T, w_up.T, w_down.T)
    *kept, down_zero, down_one, back_zero, back_one = feed_call(
        (0, 1), two[0], two[1], cot[0], cot[1], weights, None
    )
    *kept, down_three, down_two, back_three, back_two = feed_call(
        (3, 2), two[3], two[2], cot[3], cot[2], weights, kept
    )
    act, grad_gate, grad_up, two_all, cot_all = kept
    grad_normed_two = scatter_sum(back_zero, back_one, scatter_far(back_two, back_three))
    grad_hidden_norm, grad_gain_two = norm_back(hidden, scale_two, gain_two, grad_normed_two)
    grad_hidden = cotangent.astype(F32) + grad_hidden_norm
    branch = gather_rows(grad_hidden.astype(BF))
    early = attend_back_call(sc, 0, branch[0], branch[1], w_out, qkv, heads_out, lse, None)
    mixed = attend_back_call(sc, 2, branch[2], branch[3], w_out, qkv, heads_out, lse, early)
    qkv_weight_t = qkv_weight.T
    parts = [
        dot(mixed[r * local_rows : (r + 1) * local_rows], qkv_weight_t).astype(BF)
        for r in range(4)
    ]
    grad_normed = scatter_sum(parts[0], parts[1], scatter_far(parts[2], parts[3]))
    grad_rows_norm, grad_gain_one = norm_back(row_data, scale_one, gain_one, grad_normed)
    grad_latents = grad_hidden + grad_rows_norm

    down_total = scatter_weights(contract_rows(cot_all, act), seq)
    gate_total = scatter_weights(contract_rows(two_all, grad_gate), seq)
    up_total = scatter_weights(contract_rows(two_all, grad_up), seq)
    out_total = scatter_weights(contract_rows(jnp.concatenate(branch, axis=0), heads_out), seq)
    qkv_total = scatter_weights(contract_rows(jnp.concatenate(one, axis=0), mixed), seq)
    qkv_total = qkv_total.reshape(-1, 3, local_width)

    result = hidden + scatter_sum(down_zero, down_one, scatter_far(down_two, down_three))
    latents_out = result.astype(BF)
    gain_one_total, gain_two_total = lax.psum((grad_gain_one, grad_gain_two), ("seq", "tp"))
    hash_counts = hash_tables(hash_ids, hash_weights, core, seq)
    return (
        latents_out,
        grad_latents,
        gain_one_total,
        qkv_total,
        out_total,
        gain_two_total,
        gate_total,
        up_total,
        down_total,
        hash_counts,
    )


def solution(mesh):
    in_specs = (
        P(("seq", "tp"), None),
        P(),
        P(None, None, "tp"),
        P(None, "tp"),
        P(),
        P(None, "tp"),
        P(None, "tp"),
        P(None, "tp"),
        P(("seq", "tp"), None),
        P("seq", None),
        P("seq", None),
        P(None, ("seq", "tp")),
        P(None, ("seq", "tp")),
    )
    out_specs = (
        P(("seq", "tp"), None),
        P(("seq", "tp"), None),
        P(),
        P("seq", None, "tp"),
        P("seq", "tp"),
        P(),
        P("seq", "tp"),
        P("seq", "tp"),
        P("seq", "tp"),
        P(),
    )
    return jax.shard_map(shards, mesh=mesh, in_specs=in_specs, out_specs=out_specs, check_vma=False)
```

time: 904 us -> 609 us (0.67)
  waiting for transfers between devices: 514 us -> 156 us
  Pallas kernels: 0 us -> 178 us
  matrix products: 175 us -> 38.9 us
  starting transfers between devices: 0.79 us -> 72 us
  other arithmetic: 97.4 us -> 35.5 us
    reduce_scatter x6 -> x0, waiting for transfers between devices: 369 us -> none  [the longest x1 90.9 us: shards(): lax.psum_scatter(grad_w_qkv.astype(jnp.bfloat16), 'seq', scatter_dimensio...]
    pallas_call x0 -> x10, Pallas kernels: none -> 178 us  [the longest x2 42.9 us: attend_back_call(): pl.pallas_call(functools.partial(attend_back_kernel, first, last, heads),...]
    ppermute x0 -> x50, waiting for transfers between devices: none -> 156 us  [flip(): return lax.ppermute(x, axis, [(i, i ^ bits) for i in range(count)])]
    dot_general x34 -> x4, matrix products: 149 us -> 13.5 us  [dot(): lax.dot_general(a, b, (((1,), (0,)), ((), ())), preferred_element_type=F32)]
    all_gather x4 -> x1, waiting for transfers between devices: 97.7 us -> 0.01 us  [hash_tables(): pack = lax.all_gather(pack, ('seq', 'tp'), axis=1, tiled=True)]
    ppermute x0 -> x50, starting transfers between devices: none -> 71.9 us  [flip(): return lax.ppermute(x, axis, [(i, i ^ bits) for i in range(count)])]
    unnamed x17 -> x1, waiting for transfers between devices: 46.6 us -> 0.02 us
    convert_element_type x13, other arithmetic: 41.9 us -> 17.9 us  [the longest x4 6.67 us: scatter_far(): (part_two.astype(F32) + flip(part_three, 'tp', 1).astype(F32)).astype(BF)]
  transfers between devices with their start and end apart: 14 -> 51, of which waited for: 11 -> 15; matrix products, arithmetic and copies ran while one was open for 25% -> 17% of each run, Pallas kernels for 0% -> 26%
where the time goes in v1:
time: 609 us; the launch traced here: 597 us
  Pallas kernels  178 us (29%)
  waiting for transfers between devices  156 us (26%)
  starting transfers between devices  72 us (12%)
  local copies, waits for them, and re-layouts  57.7 us (9%)
  blocking collectives  40.4 us (7%)
  matrix products  38.9 us (6%)
  other arithmetic  35.5 us (6%)
  between operations  18.3 us (3%)
    ppermute x50, waiting for transfers between devices, flip(): return lax.ppermute(x, axis, [(i, i ^ bits) for i in range(count)])  156 us
    ppermute x50, starting transfers between devices, flip(): return lax.ppermute(x, axis, [(i, i ^ bits) for i in range(count)])  71.9 us
    pallas_call x2, Pallas kernels, attend_back_call(): pl.pallas_call(functools.partial(attend_back_kernel, first, last, heads),...  42.9 us
    psum x1, blocking collectives, shards(): lax.psum((grad_gain_one, grad_gain_two), ('seq', 'tp'))  40.4 us
    pallas_call x2, Pallas kernels, feed_call(): pl.pallas_call(feed_kernel, grid=(4,), in_specs=[pair(0), pair(1), pair(0...  39.2 us
    pallas_call x2, Pallas kernels, attend_call(): pl.pallas_call(functools.partial(attend_kernel, first, heads), grid_spec=...  36.4 us
    pallas_call x1, Pallas kernels, spread_call(): pl.pallas_call(spread_kernel, grid_spec=pltpu.PrefetchScalarGridSpec(num_...  26.2 us
    dot_general x5, matrix products, contract_rows(): lax.dot_general(left, right, (((0,), (0,)), ((), ())), preferred_element_...  25.3 us
  transfers between devices with their start and end apart: 51, of which 15 were waited for; matrix products, arithmetic and copies ran while one was open for 17% of the time, Pallas kernels for 26%

profile of v1, /device:TPU:0, one launch (start us, length us, event | category | flops | bytes accessed | tf_op | source)
XLA Modules:
  0.0 596.9 jit_solution(14702213473509719318)
XLA Ops:
  13.4 23.3 %collective-permute-done.a_ref = bf16[512,1024]{1,0:T(8,128)(2,1)} collective-permute-done((bf16[512,1024]{1,0:T(8,128)(2,1)S(1)}, bf16[512,1024]{1,0:T(8,128)(2,1)}, u32[]{:S(2)}, u32[]{:S(2)}) %collective-permute-start) | collective-permute-done | bytes 1048608 | tf_op jit(solution)/shard_map/ppermute | solution.py:21
  60.2 19.4 %attend.2 = (bf16[2048,256]{1,0:T(8,128)(2,1)}, f32[8,2048]{1,0:T(8,128)}, bf16[512,1024]{1,0:T(8,128)(2,1)}, bf16[512,1024]{1,0:T(8,128)(2,1)}) custom-call(s32[6]{0:T(128)} %stack.52.sc, bf16[2048,768]{1,0:T(8,128)(2,1)} %qkv.3.qkv_ref, bf16[256,1024]{1,0:T(8,128)(2,1)} %bitcast.135), custom_call_target="tpu_custom_call" | custom-call | flops 6000000000 | bytes 8000000 | tf_op jit(solution)/shard_map/attend/pallas_call | solution.py:195
  80.6 17.0 %attend.3 = (bf16[2048,256]{1,0:T(8,128)(2,1)}, f32[8,2048]{1,0:T(8,128)}, bf16[512,1024]{1,0:T(8,128)(2,1)}, bf16[512,1024]{1,0:T(8,128)(2,1)}) custom-call(s32[6]{0:T(128)} %stack.52.sc, bf16[2048,768]{1,0:T(8,128)(2,1)} %qkv.3.qkv_ref, bf16[256,1024]{1,0:T(8,128)(2,1)} %bitcast.136, ...), custom_call_target="tpu_custom_call", output_to_operand_aliasing={{0}: (3, {}), {1}: (4, {})} | custom-call | flops 6000000000 | bytes 8000000 | tf_op jit(solution)/shard_map/attend/pallas_call | solution.py:195
  99.9 21.2 %hash_sums.1 = bf16[3,248,256]{2,1,0:T(8,128)(2,1)} custom-call(s32[2]{0:T(128)} %pad_add_fusion.1.base_ref, f32[16,16384]{1,0:T(8,128)} %all-gather.2.cloned.1.call-done.pack_ref), custom_call_target="tpu_custom_call" | custom-call | flops 20000000000 | bytes 2000000 | tf_op jit(solution)/shard_map/hash_sums/pallas_call | solution.py:464
  121.1 9.3 %collective-permute-start.45 = (bf16[3,248,256]{2,1,0:T(8,128)(2,1)}, bf16[3,248,256]{2,1,0:T(8,128)(2,1)S(1)}, u32[]{:S(2)}, u32[]{:S(2)}) collective-permute-start(bf16[3,248,256]{2,1,0:T(8,128)(2,1)} %hash_sums.1), channel_id=1, source_target_pairs={{0,16},{4,20},{8,24},{12,28},{16,0},{20,4},{24,8},{28,12},{1,17},{... | collective-permute-start | bytes 1142792 | tf_op jit(solution)/shard_map/ppermute | solution.py:21
  130.4 9.5 %collective-permute-done.44 = bf16[3,248,256]{2,1,0:T(8,128)(2,1)S(1)} collective-permute-done((bf16[3,248,256]{2,1,0:T(8,128)(2,1)}, bf16[3,248,256]{2,1,0:T(8,128)(2,1)S(1)}, u32[]{:S(2)}, u32[]{:S(2)}) %collective-permute-start.44) | collective-permute-done | bytes 380960 | tf_op jit(solution)/shard_map/ppermute | solution.py:21
  139.9 16.8 %collective-permute-done.45 = bf16[3,248,256]{2,1,0:T(8,128)(2,1)S(1)} collective-permute-done((bf16[3,248,256]{2,1,0:T(8,128)(2,1)}, bf16[3,248,256]{2,1,0:T(8,128)(2,1)S(1)}, u32[]{:S(2)}, u32[]{:S(2)}) %collective-permute-start.45) | collective-permute-done | bytes 380960 | tf_op jit(solution)/shard_map/ppermute | solution.py:21
  166.1 27.1 %collective-permute-done.47.om_ref = bf16[4,3,248,256]{3,2,1,0:T(8,128)(2,1)} collective-permute-done((bf16[4,3,248,256]{3,2,1,0:T(8,128)(2,1)}, bf16[4,3,248,256]{3,2,1,0:T(8,128)(2,1)}, u32[]{:S(2)}, u32[]{:S(2)}) %collective-permute-start.47) | collective-permute-done | bytes 1523744 | tf_op jit(solution)/shard_map/ppermute | solution.py:21
  193.7 13.5 %collective-permute-done.9.nb_ref = bf16[512,1024]{1,0:T(8,128)(2,1)} collective-permute-done((bf16[512,1024]{1,0:T(8,128)(2,1)}, bf16[512,1024]{1,0:T(8,128)(2,1)}, u32[]{:S(2)}, u32[]{:S(2)}) %collective-permute-start.9) | collective-permute-done | bytes 1048608 | tf_op jit(solution)/shard_map/ppermute | solution.py:21
  215.6 19.7 %feed.2 = (bf16[2048,704]{1,0:T(8,128)(2,1)}, bf16[2048,704]{1,0:T(8,128)(2,1)}, bf16[2048,704]{1,0:T(8,128)(2,1)}, bf16[2048,1024]{1,0:T(8,128)(2,1)}, bf16[204...) custom-call(bf16[512,1024]{1,0:T(8,128)(2,1)} %multiply_convert_fusi, ...), custom_call_target="tpu_custom_call" | custom-call | flops 8858370048 | bytes 20000000 | tf_op jit(solution)/shard_map/feed/pallas_call | solution.py:422
  235.9 26.2 %hash_spread.1 = f32[6,500002]{1,0:T(8,128)} custom-call(s32[2]{0:T(128)} %pad_add_fusion.sc, bf16[4,3,248,256]{3,2,1,0:T(8,128)(2,1)} %pad_maximum_fusion.em_ref, bf16[4,3,248,256]{3,2,1,0:T(8,128)(2,1)} %collective-permute-done.47.om_ref, bf16[4,3,248,256]{3,2,1,0:T(8,128)(2,1)} %collective-permute-done.48.es_ref, ...), custom_call_target="tpu_custom_call" | custom-call | flops 1000000 | bytes 24000000 | tf_op jit(solution)/shard_map/hash_spread/pallas_call | solution.py:511
  262.1 19.5 %feed.3 = (bf16[2048,704]{1,0:T(8,128)(2,1)}, bf16[2048,704]{1,0:T(8,128)(2,1)}, bf16[2048,704]{1,0:T(8,128)(2,1)}, bf16[2048,1024]{1,0:T(8,128)(2,1)}, bf16[204...) custom-call(bf16[512,1024]{1,0:T(8,128)(2,1)} %collective-permute-do, ...), custom_call_target="tpu_custom_call", output_to_operand_aliasing={{0}: (10, {}), {1}: (11, {}), {2}: (12, {}), {3}: (13, {}),... | custom-call | flops 8858370048 | bytes 20000000 | tf_op jit(solution)/shard_map/feed/pallas_call | solution.py:422
  281.6 7.5 %convolution_convert_fusion = bf16[1024,704]{0,1:T(8,128)(2,1)} fusion(bf16[2048,1024]{1,0:T(8,128)(2,1)} %get-tuple-element.66, bf16[2048,704]{1,0:T(8,128)(2,1)} %get-tuple-element.67), kind=kOutput, calls=%fused_computation.45 | convolution fusion | flops 2953510912 | bytes 8519680 | tf_op jit(solution)/shard_map/dot_general | solution.py:547
  344.0 8.0 %collective-permute-start.41 = (bf16[128,704]{0,1:T(8,128)(2,1)S(1)}, bf16[128,704]{0,1:T(8,128)(2,1)S(1)}, u32[]{:S(2)}, u32[]{:S(2)}) collective-permute-start(bf16[128,704]{0,1:T(8,128)(2,1)S(1)} %get-tuple-element.100), channel_id=1, source_target_pairs={{0,8},{4,12},{8,0},{12,4},{16,24},{20,28},{24,16},{28,20},{1,9},{5... | collective-permute-start | bytes 540680 | tf_op jit(solution)/shard_map/ppermute | solution.py:21
  357.3 8.9 %collective-permute-start.42 = (bf16[128,704]{0,1:T(8,128)(2,1)S(1)}, bf16[128,704]{0,1:T(8,128)(2,1)S(1)}, u32[]{:S(2)}, u32[]{:S(2)}) collective-permute-start(bf16[128,704]{0,1:T(8,128)(2,1)S(1)} %get-tuple-element.102), channel_id=1, source_target_pairs={{0,16},{4,20},{8,24},{12,28},{16,0},{20,4},{24,8},{28,12},{1,17},{... | collective-permute-start | bytes 540680 | tf_op jit(solution)/shard_map/ppermute | solution.py:21
  370.0 8.8 %collective-permute-done.14 = bf16[512,1024]{1,0:T(8,128)(2,1)S(1)} collective-permute-done((bf16[512,1024]{1,0:T(8,128)(2,1)S(1)}, bf16[512,1024]{1,0:T(8,128)(2,1)S(1)}, u32[]{:S(2)}, u32[]{:S(2)}) %collective-permute-start.14) | collective-permute-done | bytes 1048608 | tf_op jit(solution)/shard_map/ppermute | solution.py:21
  384.3 8.0 %collective-permute-start.37 = (bf16[128,704]{0,1:T(8,128)(2,1)S(1)}, bf16[128,704]{0,1:T(8,128)(2,1)S(1)}, u32[]{:S(2)}, u32[]{:S(2)}) collective-permute-start(bf16[128,704]{0,1:T(8,128)(2,1)S(1)} %get-tuple-element.103), channel_id=1, source_target_pairs={{0,8},{4,12},{8,0},{12,4},{16,24},{20,28},{24,16},{28,20},{1,9},{5... | collective-permute-start | bytes 540680 | tf_op jit(solution)/shard_map/ppermute | solution.py:21
  400.5 7.8 %collective-permute-done.38 = bf16[128,704]{0,1:T(8,128)(2,1)S(1)} collective-permute-done((bf16[128,704]{0,1:T(8,128)(2,1)S(1)}, bf16[128,704]{0,1:T(8,128)(2,1)S(1)}, u32[]{:S(2)}, u32[]{:S(2)}) %collective-permute-start.38) | collective-permute-done | bytes 180256 | tf_op jit(solution)/shard_map/ppermute | solution.py:21
  411.6 12.2 %collective-permute-done.34 = bf16[128,704]{0,1:T(8,128)(2,1)S(1)} collective-permute-done((bf16[128,704]{0,1:T(8,128)(2,1)S(1)}, bf16[128,704]{0,1:T(8,128)(2,1)S(1)}, u32[]{:S(2)}, u32[]{:S(2)}) %collective-permute-start.34) | collective-permute-done | bytes 180256 | tf_op jit(solution)/shard_map/ppermute | solution.py:21
  425.6 19.3 %attend_back.2 = (bf16[1024,256]{1,0:T(8,128)(2,1)}, f32[2048,256]{1,0:T(8,128)}, f32[2048,256]{1,0:T(8,128)}) custom-call(s32[6]{0:T(128)} %stack.52.sc, bf16[512,1024]{1,0:T(8,128)(2,1)} %copy-done.13, bf16[512,1024]{1,0:T(8,128)(2,1)} %copy-done.33, bf16[1024,256]{1,0:T(8,128)(2,1)} %wo_ref.3, bf16[2048,768]{1,0:T(8,128)(2,1)} %qkv.3.qkv_ref, ...), custom_call_target="tpu_custom_call" | custom-call | flops 12000000000 | bytes 12000000 | tf_op jit(solution)/shard_map/attend_back/pallas_call | solution.py:355
  445.9 23.6 %attend_back.3 = bf16[2048,768]{1,0:T(8,128)(2,1)} custom-call(s32[6]{0:T(128)} %stack.52.sc, bf16[512,1024]{1,0:T(8,128)(2,1)} %copy-done.32, bf16[512,1024]{1,0:T(8,128)(2,1)} %copy-done.34, bf16[1024,256]{1,0:T(8,128)(2,1)} %wo_ref.3, bf16[2048,768]{1,0:T(8,128)(2,1)} %qkv.3.qkv_ref, bf16[2048,256]{1,0:T(8,128)(2,1)} %get-tuple-element.58.heads_ref, ...), custom_call_target="tpu_custom_call" | custom-call | flops 12000000000 | bytes 12000000 | tf_op jit(solution)/shard_map/attend_back/pallas_call | solution.py:355
  499.3 10.6 %collective-permute-done.28 = bf16[4,128,256]{2,1,0:T(8,128)(2,1)S(1)} collective-permute-done((bf16[4,128,256]{2,1,0:T(8,128)(2,1)S(1)}, bf16[4,128,256]{2,1,0:T(8,128)(2,1)S(1)}, u32[]{:S(2)}, u32[]{:S(2)}) %collective-permute-start.28) | collective-permute-done | bytes 262176 | tf_op jit(solution)/shard_map/ppermute | solution.py:21
  530.1 9.0 %collective-permute-done.26 = bf16[128,768]{0,1:T(8,128)(2,1)S(1)} collective-permute-done((bf16[128,768]{0,1:T(8,128)(2,1)S(1)}, bf16[128,768]{0,1:T(8,128)(2,1)S(1)}, u32[]{:S(2)}, u32[]{:S(2)}) %collective-permute-start.26) | collective-permute-done | bytes 196640 | tf_op jit(solution)/shard_map/ppermute | solution.py:21
  545.1 40.4 %all-reduce = (f32[1024]{0:T(1024)}, f32[1024]{0:T(1024)}) all-reduce(f32[1024]{0:T(1024)S(1)} %get-tuple-element.80, f32[1024]{0:T(1024)S(1)} %get-tuple-element.78), channel_id=1, replica_groups=mesh['seq'=8,'tp'=4] {'seq','tp'}, use_global_device_ids=true, to_apply=%region_5.6 | all-reduce | flops 2048 | bytes 16384 | tf_op jit(solution)/shard_map/psum | solution.py:641
  (238 shorter events, 192.1 us)
Async XLA Ops:
  7.2 92.7 %all-gather.2.cloned.1.call-start = ((), (), s32[]{:S(2)}) async-start(), calls=%async_computation | async-start | bytes 1081344 | tf_op jit(solution)/shard_map/all_gather | solution.py:537
  13.4 34.3 %collective-permute-start.2 = (bf16[512,1024]{1,0:T(8,128)(2,1)S(1)}, bf16[512,1024]{1,0:T(8,128)(2,1)}, u32[]{:S(2)}, u32[]{:S(2)}) collective-permute-start(bf16[512,1024]{1,0:T(8,128)(2,1)S(1)} %fusion.18.a_ref), channel_id=1, source_target_pairs={{0,1},{1,0},{2,3},{3,2},{4,5},{5,4},{6,7},{7,6},{8,9},{9,8},{10,11... | collective-permute-start | bytes 3145736 | tf_op jit(solution)/shard_map/ppermute | solution.py:21
  97.6 62.0 %collective-permute-start.3 = (bf16[512,1024]{1,0:T(8,128)(2,1)}, bf16[512,1024]{1,0:T(8,128)(2,1)}, u32[]{:S(2)}, u32[]{:S(2)}) collective-permute-start(bf16[512,1024]{1,0:T(8,128)(2,1)} %get-tuple-element.42), channel_id=1, source_target_pairs={{0,1},{1,0},{2,3},{3,2},{4,5},{5,4},{6,7},{7,6},{8,9},{9,8},{10,11... | collective-permute-start | bytes 3145736 | tf_op jit(solution)/shard_map/ppermute | solution.py:21
  98.0 61.6 %collective-permute-start.5 = (bf16[512,1024]{1,0:T(8,128)(2,1)S(1)}, bf16[512,1024]{1,0:T(8,128)(2,1)S(1)}, u32[]{:S(2)}, u32[]{:S(2)}) collective-permute-start(bf16[512,1024]{1,0:T(8,128)(2,1)S(1)} %add_convert_fusion.4), channel_id=1, source_target_pairs={{0,2},{1,3},{2,0},{3,1},{4,6},{5,7},{6,4},{7,5},{8,10},{9,11},{10,... | collective-permute-start | bytes 3145736 | tf_op jit(solution)/shard_map/ppermute | solution.py:21
  121.1 35.6 %collective-permute-start.45 = (bf16[3,248,256]{2,1,0:T(8,128)(2,1)}, bf16[3,248,256]{2,1,0:T(8,128)(2,1)S(1)}, u32[]{:S(2)}, u32[]{:S(2)}) collective-permute-start(bf16[3,248,256]{2,1,0:T(8,128)(2,1)} %hash_sums.1), channel_id=1, source_target_pairs={{0,16},{4,20},{8,24},{12,28},{16,0},{20,4},{24,8},{28,12},{1,17},{... | collective-permute-start | bytes 1142792 | tf_op jit(solution)/shard_map/ppermute | solution.py:21
  159.0 34.1 %collective-permute-start.47 = (bf16[4,3,248,256]{3,2,1,0:T(8,128)(2,1)}, bf16[4,3,248,256]{3,2,1,0:T(8,128)(2,1)}, u32[]{:S(2)}, u32[]{:S(2)}) collective-permute-start(bf16[4,3,248,256]{3,2,1,0:T(8,128)(2,1)} %pad_maximum_fusion.em_ref), channel_id=1, source_target_pairs={{0,4},{4,0},{8,12},{12,8},{16,20},{20,16},{24,28},{28,24},{1,5},{5... | collective-permute-start | bytes 4571144 | tf_op jit(solution)/shard_map/ppermute | solution.py:21
  159.1 34.1 %collective-permute-start.11 = (bf16[512,1024]{1,0:T(8,128)(2,1)S(1)}, bf16[512,1024]{1,0:T(8,128)(2,1)}, u32[]{:S(2)}, u32[]{:S(2)}) collective-permute-start(bf16[512,1024]{1,0:T(8,128)(2,1)S(1)} %copy-done.10), channel_id=1, source_target_pairs={{0,2},{1,3},{2,0},{3,1},{4,6},{5,7},{6,4},{7,5},{8,10},{9,11},{10,... | collective-permute-start | bytes 3145736 | tf_op jit(solution)/shard_map/ppermute | solution.py:21
  164.1 43.1 %collective-permute-start.9 = (bf16[512,1024]{1,0:T(8,128)(2,1)}, bf16[512,1024]{1,0:T(8,128)(2,1)}, u32[]{:S(2)}, u32[]{:S(2)}) collective-permute-start(bf16[512,1024]{1,0:T(8,128)(2,1)} %multiply_convert_fusion.na_ref), channel_id=1, source_target_pairs={{0,2},{1,3},{2,0},{3,1},{4,6},{5,7},{6,4},{7,5},{8,10},{9,11},{10,... | collective-permute-start | bytes 3145736 | tf_op jit(solution)/shard_map/ppermute | solution.py:21
  165.6 50.0 %collective-permute-start.6 = (bf16[512,1024]{1,0:T(8,128)(2,1)}, bf16[512,1024]{1,0:T(8,128)(2,1)}, u32[]{:S(2)}, u32[]{:S(2)}) collective-permute-start(bf16[512,1024]{1,0:T(8,128)(2,1)} %multiply_convert_fusion.na_ref), channel_id=1, source_target_pairs={{0,1},{1,0},{2,3},{3,2},{4,5},{5,4},{6,7},{7,6},{8,9},{9,8},{10,11... | collective-permute-start | bytes 3145736 | tf_op jit(solution)/shard_map/ppermute | solution.py:21
  165.6 70.2 %collective-permute-start.48 = (bf16[4,3,248,256]{3,2,1,0:T(8,128)(2,1)}, bf16[4,3,248,256]{3,2,1,0:T(8,128)(2,1)}, u32[]{:S(2)}, u32[]{:S(2)}) collective-permute-start(bf16[4,3,248,256]{3,2,1,0:T(8,128)(2,1)} %pad_maximum_fusion.em_ref), channel_id=1, source_target_pairs={{0,1},{1,0},{2,3},{3,2},{4,5},{5,4},{6,7},{7,6},{8,9},{9,8},{10,11... | collective-permute-start | bytes 4571144 | tf_op jit(solution)/shard_map/ppermute | solution.py:21
  193.2 42.7 %collective-permute-start.49 = (bf16[4,3,248,256]{3,2,1,0:T(8,128)(2,1)}, bf16[4,3,248,256]{3,2,1,0:T(8,128)(2,1)}, u32[]{:S(2)}, u32[]{:S(2)}) collective-permute-start(bf16[4,3,248,256]{3,2,1,0:T(8,128)(2,1)} %collective-permute-done.47.om_ref), channel_id=1, source_target_pairs={{0,1},{1,0},{2,3},{3,2},{4,5},{5,4},{6,7},{7,6},{8,9},{9,8},{10,11... | collective-permute-start | bytes 4571144 | tf_op jit(solution)/shard_map/ppermute | solution.py:21
  193.2 68.9 %collective-permute-start.12 = (bf16[512,1024]{1,0:T(8,128)(2,1)}, bf16[512,1024]{1,0:T(8,128)(2,1)}, u32[]{:S(2)}, u32[]{:S(2)}) collective-permute-start(bf16[512,1024]{1,0:T(8,128)(2,1)} %collective-permute-done.11.cb_ref), channel_id=1, source_target_pairs={{0,1},{1,0},{2,3},{3,2},{4,5},{5,4},{6,7},{7,6},{8,9},{9,8},{10,11... | collective-permute-start | bytes 3145736 | tf_op jit(solution)/shard_map/ppermute | solution.py:21
  207.2 54.9 %collective-permute-start.10 = (bf16[512,1024]{1,0:T(8,128)(2,1)}, bf16[512,1024]{1,0:T(8,128)(2,1)}, u32[]{:S(2)}, u32[]{:S(2)}) collective-permute-start(bf16[512,1024]{1,0:T(8,128)(2,1)} %collective-permute-done.9.nb_ref), channel_id=1, source_target_pairs={{0,1},{1,0},{2,3},{3,2},{4,5},{5,4},{6,7},{7,6},{8,9},{9,8},{10,11... | collective-permute-start | bytes 3145736 | tf_op jit(solution)/shard_map/ppermute | solution.py:21
  235.3 108.7 %collective-permute-start.15 = (bf16[512,1024]{1,0:T(8,128)(2,1)}, bf16[512,1024]{1,0:T(8,128)(2,1)}, u32[]{:S(2)}, u32[]{:S(2)}) collective-permute-start(bf16[512,1024]{1,0:T(8,128)(2,1)} %get-tuple-element.55), channel_id=1, source_target_pairs={{0,1},{1,0},{2,3},{3,2},{4,5},{5,4},{6,7},{7,6},{8,9},{9,8},{10,11... | collective-permute-start | bytes 3145736 | tf_op jit(solution)/shard_map/ppermute | solution.py:21
  301.3 36.6 %collective-permute-start.40 = (bf16[4,128,704]{1,2,0:T(8,128)(2,1)}, bf16[4,128,704]{1,2,0:T(8,128)(2,1)}, u32[]{:S(2)}, u32[]{:S(2)}) collective-permute-start(bf16[4,128,704]{1,2,0:T(8,128)(2,1)} %bitcast.117), channel_id=1, source_target_pairs={{0,4},{4,0},{8,12},{12,8},{16,20},{20,16},{24,28},{28,24},{1,5},{5... | collective-permute-start | bytes 2162696 | tf_op jit(solution)/shard_map/ppermute | solution.py:21
  337.9 40.9 %collective-permute-start.14 = (bf16[512,1024]{1,0:T(8,128)(2,1)S(1)}, bf16[512,1024]{1,0:T(8,128)(2,1)S(1)}, u32[]{:S(2)}, u32[]{:S(2)}) collective-permute-start(bf16[512,1024]{1,0:T(8,128)(2,1)S(1)} %add_convert_fusion.3), channel_id=1, source_target_pairs={{0,2},{1,3},{2,0},{3,1},{4,6},{5,7},{6,4},{7,5},{8,10},{9,11},{10,... | collective-permute-start | bytes 3145736 | tf_op jit(solution)/shard_map/ppermute | solution.py:21
  340.9 42.8 %collective-permute-start.32 = (bf16[4,128,704]{1,2,0:T(8,128)(2,1)S(1)}, bf16[4,128,704]{1,2,0:T(8,128)(2,1)S(1)}, u32[]{:S(2)}, u32[]{:S(2)}) collective-permute-start(bf16[4,128,704]{1,2,0:T(8,128)(2,1)S(1)} %bitcast.134), channel_id=1, source_target_pairs={{0,4},{4,0},{8,12},{12,8},{16,20},{20,16},{24,28},{28,24},{1,5},{5... | collective-permute-start | bytes 2162696 | tf_op jit(solution)/shard_map/ppermute | solution.py:21
  344.0 40.3 %collective-permute-start.41 = (bf16[128,704]{0,1:T(8,128)(2,1)S(1)}, bf16[128,704]{0,1:T(8,128)(2,1)S(1)}, u32[]{:S(2)}, u32[]{:S(2)}) collective-permute-start(bf16[128,704]{0,1:T(8,128)(2,1)S(1)} %get-tuple-element.100), channel_id=1, source_target_pairs={{0,8},{4,12},{8,0},{12,4},{16,24},{20,28},{24,16},{28,20},{1,9},{5... | collective-permute-start | bytes 540680 | tf_op jit(solution)/shard_map/ppermute | solution.py:21
  357.3 34.9 %collective-permute-start.42 = (bf16[128,704]{0,1:T(8,128)(2,1)S(1)}, bf16[128,704]{0,1:T(8,128)(2,1)S(1)}, u32[]{:S(2)}, u32[]{:S(2)}) collective-permute-start(bf16[128,704]{0,1:T(8,128)(2,1)S(1)} %get-tuple-element.102), channel_id=1, source_target_pairs={{0,16},{4,20},{8,24},{12,28},{16,0},{20,4},{24,8},{28,12},{1,17},{... | collective-permute-start | bytes 540680 | tf_op jit(solution)/shard_map/ppermute | solution.py:21
  383.2 41.4 %collective-permute-start.18 = (bf16[512,1024]{1,0:T(8,128)(2,1)S(1)}, bf16[512,1024]{1,0:T(8,128)(2,1)S(1)}, u32[]{:S(2)}, u32[]{:S(2)}) collective-permute-start(bf16[512,1024]{1,0:T(8,128)(2,1)S(1)} %get-tuple-element.84.ga_ref), channel_id=1, source_target_pairs={{0,2},{1,3},{2,0},{3,1},{4,6},{5,7},{6,4},{7,5},{8,10},{9,11},{10,... | collective-permute-start | bytes 3145736 | tf_op jit(solution)/shard_map/ppermute | solution.py:21
  383.7 40.9 %collective-permute-start.20 = (bf16[512,1024]{1,0:T(8,128)(2,1)S(1)}, bf16[512,1024]{1,0:T(8,128)(2,1)S(1)}, u32[]{:S(2)}, u32[]{:S(2)}) collective-permute-start(bf16[512,1024]{1,0:T(8,128)(2,1)S(1)} %get-tuple-element.84.ga_ref), channel_id=1, source_target_pairs={{0,1},{1,0},{2,3},{3,2},{4,5},{5,4},{6,7},{7,6},{8,9},{9,8},{10,11... | collective-permute-start | bytes 3145736 | tf_op jit(solution)/shard_map/ppermute | solution.py:21
  483.9 34.3 %collective-permute-start.24 = (bf16[4,128,768]{1,2,0:T(8,128)(2,1)}, bf16[4,128,768]{1,2,0:T(8,128)(2,1)}, u32[]{:S(2)}, u32[]{:S(2)}) collective-permute-start(bf16[4,128,768]{1,2,0:T(8,128)(2,1)} %bitcast.133), channel_id=1, source_target_pairs={{0,4},{4,0},{8,12},{12,8},{16,20},{20,16},{24,28},{28,24},{1,5},{5... | collective-permute-start | bytes 2359304 | tf_op jit(solution)/shard_map/ppermute | solution.py:21
  495.1 45.0 %collective-permute-start.21 = (bf16[512,1024]{1,0:T(8,128)(2,1)}, bf16[512,1024]{1,0:T(8,128)(2,1)}, u32[]{:S(2)}, u32[]{:S(2)}) collective-permute-start(bf16[512,1024]{1,0:T(8,128)(2,1)} %convolution_convert_fusion.5), channel_id=1, source_target_pairs={{0,1},{1,0},{2,3},{3,2},{4,5},{5,4},{6,7},{7,6},{8,9},{9,8},{10,11... | collective-permute-start | bytes 3145736 | tf_op jit(solution)/shard_map/ppermute | solution.py:21
  498.0 42.2 %collective-permute-start.23 = (bf16[512,1024]{1,0:T(8,128)(2,1)}, bf16[512,1024]{1,0:T(8,128)(2,1)}, u32[]{:S(2)}, u32[]{:S(2)}) collective-permute-start(bf16[512,1024]{1,0:T(8,128)(2,1)} %add_convert_fusion), channel_id=1, source_target_pairs={{0,2},{1,3},{2,0},{3,1},{4,6},{5,7},{6,4},{7,5},{8,10},{9,11},{10,... | collective-permute-start | bytes 3145736 | tf_op jit(solution)/shard_map/ppermute | solution.py:21
  (67 other events, 1090.7 us)
Sparse Core Ops, SparseCore 0:
  37.6 55.4 all-gather.1

commit v2 on v1

v2 whole, which is shorter than its diff:
```python
import functools

import jax
import jax.numpy as jnp
from jax import lax
from jax.experimental import pallas as pl
from jax.experimental.pallas import tpu as pltpu
from jax.sharding import PartitionSpec as P

HEAD_DIM = 64
HASH_ROWS = 500002
EPSILON = 1e-05
MASKED = -1e30
BF = jnp.bfloat16
F32 = jnp.float32
QB = 256
LANES = 256
STEPS = 4
VMEM_BYTES = 60 * 1024 * 1024
MESH = pl.DeviceIdType.MESH


def flip(x, axis, bits):
    count = lax.axis_size(axis)
    return lax.ppermute(x, axis, [(i, i ^ bits) for i in range(count)])


def dot(a, b):
    return lax.dot_general(a, b, (((1,), (0,)), ((), ())), preferred_element_type=F32)


def dot_nt(a, b):
    return lax.dot_general(a, b, (((1,), (1,)), ((), ())), preferred_element_type=F32)


def dot_tn(a, b):
    return lax.dot_general(a, b, (((0,), (0,)), ((), ())), preferred_element_type=F32)


def cost(flops, moved):
    return pl.CostEstimate(flops=flops, bytes_accessed=moved, transcendentals=0)


def params(**more):
    return pltpu.CompilerParams(vmem_limit_bytes=VMEM_BYTES, **more)


def whole(shape):
    return pl.BlockSpec(shape, lambda i, sc: (0,) * len(shape))


VM = pl.BlockSpec(memory_space=pltpu.VMEM)
ANY = pl.BlockSpec(memory_space=pl.ANY)


def places():
    me = lax.axis_index("tp")
    core = lax.rem(me, 2)
    sib = me + 1 - 2 * core
    far = lax.rem(me + 2, 4)
    return me, sib, far, lax.rem(sib + 2, 4), core


def push(src, dst, send, recv, where):
    return pltpu.make_async_remote_copy(
        src_ref=src,
        dst_ref=dst,
        send_sem=send,
        recv_sem=recv,
        device_id={"seq": where[0], "tp": where[1]},
        device_id_type=MESH,
    )


def greet(others):
    barrier = pltpu.get_barrier_semaphore()
    for seq, tp in others:
        pl.semaphore_signal(
            barrier, inc=1, device_id={"seq": seq, "tp": tp}, device_id_type=MESH
        )
    pl.semaphore_wait(barrier, len(others))


def chunk(k, size):
    return pl.ds(pl.multiple_of(k * size, size), size)


def norm_rows(row_data, gain):
    scaling = lax.rsqrt(jnp.mean(row_data * row_data, axis=-1, keepdims=True) + EPSILON)
    return (row_data * scaling * gain, scaling)


def norm_back(row_data, scaling, gain, grad_norm):
    weighted = grad_norm * gain
    inner_mean = jnp.mean(weighted * row_data, axis=-1, keepdims=True)
    grad_rows = scaling * weighted - row_data * scaling * scaling * scaling * inner_mean
    grad_gain = jnp.sum(grad_norm * row_data * scaling, axis=0, keepdims=True)
    return (grad_rows, grad_gain)


def front_kernel(
    seq_count, tables, x_ref, gain_ref, w_ref, pair_ref, n_ref, qkv_ref, hash_ref,
    pack_ref, sum_ref, snd, rcv, psnd, prcv,
):
    me, sib, far, _, core = places()
    seq = lax.axis_index("seq")
    near = seq + 1 - 2 * lax.rem(seq, 2)
    parity, place, half = lax.rem(seq, 2), seq // 2, seq_count // 2
    level = [lax.rem(seq + 2 * j, seq_count) for j in range(1, half)]
    greet([(seq, sib), (seq, far), (near, me)] + [(s, me) for s in level])
    rows = x_ref.shape[0]
    size = rows // STEPS

    pack_ref[parity, place, me] = pair_ref[core]
    mine = pack_ref.at[parity, place, me]
    stage_sib = push(pair_ref.at[1 - core], mine, psnd.at[0], prcv.at[0], (seq, sib))
    stage_sib.start()
    both = pack_ref.at[parity, place, pl.ds(me - core, 2)]
    stage_far = push(both, both, psnd.at[1], prcv.at[1], (seq, far))
    four = pack_ref.at[parity, place]
    stage_level = [
        push(four, four, psnd.at[2 + j], prcv.at[2 + j], (s, me)) for j, s in enumerate(level)
    ]
    plane = pack_ref.at[parity]
    stage_near = push(plane, plane, psnd.at[half + 1], prcv.at[half + 1], (near, me))

    def own(kind, k, to, block):
        part = n_ref.at[block, chunk(k, size)]
        return push(part, part, snd.at[kind, k], rcv.at[kind, k], (seq, to))

    for k in range(STEPS):
        part = slice(k * size, (k + 1) * size)
        normed, _ = norm_rows(x_ref[part].astype(F32), gain_ref[...])
        n_ref[me, part] = normed.astype(BF)
        if k == 0:
            stage_sib.wait_recv()
            stage_far.start()
        own(1, k, far, me).start()
        own(0, k, sib, me).start()

    def project(block):
        def body(k, carry):
            part = chunk(k, rows // 2)
            qkv_ref[block, part] = dot(n_ref[block, part], w_ref[...]).astype(BF)
            return carry

        lax.fori_loop(0, 2, body, 0)

    project(me)
    stage_far.wait_recv()
    for copy in stage_level:
        copy.start()
    for k in range(STEPS):
        own(0, k, sib, me).wait_recv()
    project(sib)
    own(1, 0, far, me).wait_recv()
    own(2, 0, sib, far).start()
    for copy in stage_level:
        copy.wait_recv()
    stage_near.start()

    sum_ref[...] = jnp.zeros_like(sum_ref)
    high_rows = sum_ref.shape[1]
    first = seq * (high_rows * LANES)

    def sums(which):
        def body(n, carry):
            table, block = n // (half * 4), lax.rem(n, half * 4)
            pairs = pack_ref.at[which, block // 4, lax.rem(block, 4)]
            ids = pairs[pl.ds(table, 1)].astype(jnp.int32) - first
            weights = pairs[pl.ds(table + tables, 1)]
            high = lax.broadcasted_iota(jnp.int32, (high_rows, rows), 0) == (ids >> 8)
            low = lax.broadcasted_iota(jnp.int32, (LANES, rows), 0) == (ids & (LANES - 1))
            high = jnp.where(high, 1.0, 0.0).astype(BF)
            low = jnp.where(low, weights, 0.0).astype(BF)
            sum_ref[table] += dot_nt(high, low)
            return carry

        lax.fori_loop(0, tables * half * 4, body, 0)

    sums(parity)
    for k in range(1, STEPS):
        own(1, k, far, me).wait_recv()
        own(2, k, sib, far).start()
    stage_near.wait_recv()
    sums(1 - parity)
    hash_ref[...] = sum_ref[...].astype(BF)
    project(far)
    for k in range(STEPS):
        own(2, k, sib, far).wait_recv()
    project(lax.rem(sib + 2, 4))
    for k in range(STEPS):
        for kind in range(3):
            own(kind, k, sib, me).wait_send()
    stage_sib.wait_send()
    stage_far.wait_send()
    for copy in stage_level:
        copy.wait_send()
    stage_near.wait_send()


def front_call(x, gain, w, pairs, high_rows):
    seq_count = lax.axis_size("seq")
    rows, model = x.shape
    tables = 3
    half = seq_count // 2
    dma = pltpu.SemaphoreType.DMA
    return pl.pallas_call(
        functools.partial(front_kernel, seq_count, tables),
        in_specs=[VM] * 4,
        out_specs=[VM] * 3,
        out_shape=[
            jax.ShapeDtypeStruct((4, rows, model), BF),
            jax.ShapeDtypeStruct((4, rows, w.shape[1]), BF),
            jax.ShapeDtypeStruct((tables, high_rows, LANES), BF),
        ],
        scratch_shapes=[
            pltpu.VMEM((2, half, 4, 8, rows), F32),
            pltpu.VMEM((tables, high_rows, LANES), F32),
            dma((3, STEPS)),
            dma((3, STEPS)),
            dma((half + 2,)),
            dma((half + 2,)),
        ],
        compiler_params=params(collective_id=0, has_side_effects=True),
        cost_estimate=cost(30_000_000_000, 10_000_000),
        name="front",
    )(x, gain, w, pairs)


def doc_bounds(sc, places):
    low = jnp.where(places >= sc[2], sc[2], jnp.where(places >= sc[1], sc[1], 0))
    end = jnp.where(places >= sc[2], sc[5], jnp.where(places >= sc[1], sc[4], sc[3]))
    return low, jnp.minimum(places, end - 1)


def head_rows(x, h):
    where = lax.broadcasted_iota(jnp.int32, x.shape, 0) // HEAD_DIM
    return jnp.where(where == h, x, jnp.zeros_like(x))


def head_lanes(x, h):
    where = lax.broadcasted_iota(jnp.int32, x.shape, 1) // HEAD_DIM
    return jnp.where(where == h, x, jnp.zeros_like(x))


def attend_kernel(heads, sc, qkv_ref, heads_ref, lse_ref, vt_ref, qt_ref, acc_ref):
    width = heads * HEAD_DIM
    step = pl.program_id(0)

    @pl.when(step == 0)
    def _():
        for n in range(qkv_ref.shape[0] // QB):
            vt_ref[:, n * QB : (n + 1) * QB] = qkv_ref[n * QB : (n + 1) * QB, 2 * width :].T

    start = pl.multiple_of(step * QB, QB)
    q_t = qkv_ref[pl.ds(start, QB), :width].T * jnp.asarray(HEAD_DIM**-0.5, BF)
    for h in range(heads):
        qt_ref[h] = head_rows(q_t, h)
    acc_ref[...] = jnp.zeros_like(acc_ref)
    places = start + lax.broadcasted_iota(jnp.int32, (1, QB), 1)
    low, high = doc_bounds(sc, places)
    low_first, _ = doc_bounds(sc, start)

    def body(kb, state):
        at = pl.multiple_of(kb * QB, QB)
        keys = qkv_ref[pl.ds(at, QB), width : 2 * width]
        value_t = vt_ref[:, pl.ds(at, QB)]
        spot = at + lax.broadcasted_iota(jnp.int32, (QB, QB), 0)
        allowed = (spot >= low) & (spot <= high)
        fresh = []
        for h in range(heads):
            top, total = state[h]
            scores = jnp.where(allowed, dot(keys, qt_ref[h]), MASKED)
            new_top = jnp.maximum(top, jnp.max(scores, axis=0, keepdims=True))
            fade = jnp.exp(top - new_top)
            probs = jnp.exp(scores - new_top)
            total = total * fade + jnp.sum(probs, axis=0, keepdims=True)
            part = slice(h * HEAD_DIM, (h + 1) * HEAD_DIM)
            acc_ref[part] = acc_ref[part] * fade + dot(value_t[part], probs.astype(BF))
            fresh.append((new_top, total))
        return tuple(fresh)

    begin = tuple(
        (jnp.full((1, QB), MASKED, F32), jnp.zeros((1, QB), F32)) for _ in range(heads)
    )
    state = lax.fori_loop(low_first // QB, start // QB + 1, body, begin)
    lse_ref[...] = jnp.zeros_like(lse_ref)
    for h in range(heads):
        top, total = state[h]
        part = slice(h * HEAD_DIM, (h + 1) * HEAD_DIM)
        acc_ref[part] = acc_ref[part] * (1.0 / total)
        lse_ref[h : h + 1] = top + jnp.log(total)
    heads_ref[...] = acc_ref[...].T.astype(BF)


def attend_call(sc, qkv):
    rows, width = qkv.shape[0], qkv.shape[1] // 3
    heads = width // HEAD_DIM
    return pl.pallas_call(
        functools.partial(attend_kernel, heads),
        grid_spec=pltpu.PrefetchScalarGridSpec(
            num_scalar_prefetch=1,
            grid=(rows // QB,),
            in_specs=[whole(qkv.shape)],
            out_specs=[
                pl.BlockSpec((QB, width), lambda i, sc: (i, 0)),
                pl.BlockSpec((8, QB), lambda i, sc: (0, i)),
            ],
            scratch_shapes=[
                pltpu.VMEM((width, rows), BF),
                pltpu.VMEM((heads, width, QB), BF),
                pltpu.VMEM((width, QB), F32),
            ],
        ),
        out_shape=[
            jax.ShapeDtypeStruct((rows, width), BF),
            jax.ShapeDtypeStruct((8, rows), F32),
        ],
        compiler_params=params(),
        cost_estimate=cost(35_000_000_000, 8_000_000),
        name="attend",
    )(sc, qkv)


def attend_back_kernel(
    heads, sc, grad_ref, wo_ref, qkv_ref, heads_ref, lse_ref, mixed_ref,
    kt_ref, qt_ref, gt_ref, qs_ref, gs_ref, dqt_ref, dk_ref, dv_ref,
):
    width = heads * HEAD_DIM
    step = pl.program_id(0)
    rows = qkv_ref.shape[0]

    @pl.when(step == 0)
    def _():
        for n in range(rows // QB):
            kt_ref[:, n * QB : (n + 1) * QB] = qkv_ref[n * QB : (n + 1) * QB, width : 2 * width].T
        dk_ref[...] = jnp.zeros_like(dk_ref)
        dv_ref[...] = jnp.zeros_like(dv_ref)

    start = pl.multiple_of(step * QB, QB)
    grad = dot(grad_ref[...], wo_ref[...]).astype(BF)
    grad_t = grad.T
    out_t = heads_ref[...].T
    product = grad_t.astype(F32) * out_t.astype(F32)
    query = qkv_ref[pl.ds(start, QB), :width] * jnp.asarray(HEAD_DIM**-0.5, BF)
    q_t = query.T
    inner = []
    for h in range(heads):
        part = slice(h * HEAD_DIM, (h + 1) * HEAD_DIM)
        inner.append(jnp.sum(product[part], axis=0, keepdims=True))
        qt_ref[h] = head_rows(q_t, h)
        gt_ref[h] = head_rows(grad_t, h)
        qs_ref[h * QB : (h + 1) * QB] = head_lanes(query, h)
        gs_ref[h * QB : (h + 1) * QB] = head_lanes(grad, h)
    dqt_ref[...] = jnp.zeros_like(dqt_ref)
    places = start + lax.broadcasted_iota(jnp.int32, (1, QB), 1)
    low, high = doc_bounds(sc, places)
    low_first, _ = doc_bounds(sc, start)

    def body(kb, carry):
        at = pl.multiple_of(kb * QB, QB)
        keys = qkv_ref[pl.ds(at, QB), width : 2 * width]
        values = qkv_ref[pl.ds(at, QB), 2 * width :]
        spot = at + lax.broadcasted_iota(jnp.int32, (QB, QB), 0)
        allowed = (spot >= low) & (spot <= high)
        all_probs, all_grads = [], []
        for h in range(heads):
            part = slice(h * HEAD_DIM, (h + 1) * HEAD_DIM)
            scores = jnp.where(allowed, dot(keys, qt_ref[h]), MASKED)
            probs = jnp.exp(scores - lse_ref[h : h + 1])
            grad_probs = dot(values, gt_ref[h])
            grad_scores = (probs * (grad_probs - inner[h])).astype(BF)
            all_probs.append(probs.astype(BF))
            all_grads.append(grad_scores)
            dqt_ref[part] += dot(kt_ref[part, pl.ds(at, QB)], grad_scores)
        dv_ref[pl.ds(at, QB)] += dot(jnp.concatenate(all_probs, axis=1), gs_ref[...])
        dk_ref[pl.ds(at, QB)] += dot(jnp.concatenate(all_grads, axis=1), qs_ref[...])
        return carry

    lax.fori_loop(low_first // QB, start // QB + 1, body, 0)
    dq = (dqt_ref[...] * HEAD_DIM**-0.5).T.astype(BF)
    mixed_ref[pl.ds(start, QB), :width] = dq

    @pl.when(step == pl.num_programs(0) - 1)
    def _():
        mixed_ref[:, width : 2 * width] = dk_ref[...].astype(BF)
        mixed_ref[:, 2 * width :] = dv_ref[...].astype(BF)


def attend_back_call(sc, grad, wo, qkv, heads_out, lse):
    rows, width = qkv.shape[0], qkv.shape[1] // 3
    heads = width // HEAD_DIM
    model = wo.shape[0]
    return pl.pallas_call(
        functools.partial(attend_back_kernel, heads),
        grid_spec=pltpu.PrefetchScalarGridSpec(
            num_scalar_prefetch=1,
            grid=(rows // QB,),
            in_specs=[
                pl.BlockSpec((QB, model), lambda i, sc: (i, 0)),
                whole(wo.shape),
                whole(qkv.shape),
                pl.BlockSpec((QB, width), lambda i, sc: (i, 0)),
                pl.BlockSpec((8, QB), lambda i, sc: (0, i)),
            ],
            out_specs=whole((rows, 3 * width)),
            scratch_shapes=[
                pltpu.VMEM((width, rows), BF),
                pltpu.VMEM((heads, width, QB), BF),
                pltpu.VMEM((heads, width, QB), BF),
                pltpu.VMEM((heads * QB, width), BF),
                pltpu.VMEM((heads * QB, width), BF),
                pltpu.VMEM((width, QB), F32),
                pltpu.VMEM((rows, width), F32),
                pltpu.VMEM((rows, width), F32),
            ],
        ),
        out_shape=jax.ShapeDtypeStruct((rows, 3 * width), BF),
        compiler_params=params(),
        cost_estimate=cost(45_000_000_000, 12_000_000),
        name="attend_back",
    )(sc, grad, wo, qkv, heads_out, lse)


def middle_kernel(
    seq_count, heads_ref, wo_ref, x_ref, gain_ref, c0, c1, c2, c3, wg_ref, wu_ref, wd_ref,
    rest_ref, fardown_ref, grad_ref, gain_out, branch_ref,
    keep_ref, got_ref,
    n_ref, act_ref, gg_ref, gu_ref, g0_ref, g1s_ref, g1r_ref, d0_ref, d1s_ref, d1r_ref,
    d3s_ref, d3r_ref, as_ref, ar_ref, ys_ref, yr_ref, bs_ref, br_ref, gb_ref, dw_ref,
    snd, rcv, xsnd, xrcv, loc, wloc,
):
    me, sib, far, farsib, core = places()
    seq = lax.axis_index("seq")
    near = seq + 1 - 2 * lax.rem(seq, 2)
    greet([(seq, sib), (seq, far), (near, me)])
    rows, model = x_ref.shape
    size = rows // STEPS
    half = seq_count // 2
    units = keep_ref.shape[-1]

    def copy(kind, k, src, dst, to):
        return push(
            src.at[chunk(k, size)], dst.at[chunk(k, size)], snd.at[kind, k], rcv.at[kind, k], (seq, to)
        )

    def block_copy(kind, k, ref, block, to):
        part = ref.at[block, chunk(k, size)]
        return push(part, part, snd.at[kind, k], rcv.at[kind, k], (seq, to))

    proj_a = lambda k: copy(0, k, as_ref, ar_ref, sib)
    proj_y = lambda k: copy(1, k, ys_ref, yr_ref, far)
    proj_b = lambda k: copy(2, k, bs_ref, br_ref, sib)
    two_sib = lambda k: block_copy(3, k, n_ref, me, sib)
    two_far = lambda k: block_copy(4, k, n_ref, me, far)
    two_on = lambda k: block_copy(5, k, n_ref, far, sib)
    back_one = lambda k: copy(6, k, g1s_ref, g1r_ref, sib)
    down_one = lambda k: copy(7, k, d1s_ref, d1r_ref, sib)
    back_a = lambda k: copy(8, k, as_ref, ar_ref, sib)
    back_y = lambda k: copy(9, k, ys_ref, yr_ref, far)
    down_three = lambda k: copy(10, k, d3s_ref, d3r_ref, sib)
    branch_on = lambda k: block_copy(13, k, branch_ref, far, sib)

    def branch_out(kind, k, to):
        return push(
            gb_ref.at[chunk(k, size)], branch_ref.at[me, chunk(k, size)],
            snd.at[kind, k], rcv.at[kind, k], (seq, to),
        )

    def branch_home(k):
        return pltpu.make_async_copy(
            gb_ref.at[chunk(k, size)], branch_ref.at[me, chunk(k, size)], loc.at[k]
        )

    def each(body, count=STEPS):
        lax.fori_loop(0, count, lambda k, c: (body(k), c)[1], 0)

    def project(block, k):
        return dot(heads_ref[block, chunk(k, size)], wo_ref[...])

    def send_three(k):
        as_ref[chunk(k, size)] = project(farsib, k).astype(BF)
        proj_a(k).start()

    def send_two(k):
        part = project(far, k)
        proj_a(k).wait_recv()
        ys_ref[chunk(k, size)] = (part + ar_ref[chunk(k, size)].astype(F32)).astype(BF)
        proj_y(k).start()

    def send_one(k):
        bs_ref[chunk(k, size)] = project(sib, k).astype(BF)
        proj_b(k).start()

    each(send_three)
    each(send_two)
    each(send_one)

    def feed(k, block_a, block_b, ca, cb):
        part = chunk(k, size)
        normed = jnp.concatenate([n_ref[block_a, part], n_ref[block_b, part]], axis=0)
        cot = jnp.concatenate([ca[part], cb[part]], axis=0)
        gate = dot(normed, wg_ref[...])
        up = dot(normed, wu_ref[...])
        sig = jax.nn.sigmoid(gate)
        silu = gate * sig
        act = (silu * up).astype(BF)
        grad_act = dot(cot, wd_ref[...])
        grad_gate = (grad_act * up * sig * (1.0 + gate * (1.0 - sig))).astype(BF)
        grad_up = (grad_act * silu).astype(BF)
        for ref, value in ((act_ref, act), (gg_ref, grad_gate), (gu_ref, grad_up)):
            ref[block_a, part] = value[:size]
            ref[block_b, part] = value[size:]
        back = dot_nt(grad_gate, wg_ref[...]) + dot_nt(grad_up, wu_ref[...])
        return back, dot_nt(act, wd_ref[...])

    def own_chunk(k):
        part = chunk(k, size)
        total = x_ref[part].astype(F32) + project(me, k)
        proj_b(k).wait_recv()
        proj_y(k).wait_recv()
        hidden = total + br_ref[part].astype(F32) + yr_ref[part].astype(F32)
        rest_ref[part] = hidden
        normed, _ = norm_rows(hidden, gain_ref[...])
        n_ref[me, part] = normed.astype(BF)
        two_far(k).start()
        two_sib(k).start()
        two_sib(k).wait_recv()
        back, down = feed(k, me, sib, c0, c1)
        g0_ref[part] = back[:size].astype(BF)
        g1s_ref[part] = back[size:].astype(BF)
        back_one(k).start()
        d0_ref[part] = down[:size].astype(BF)
        d1s_ref[part] = down[size:].astype(BF)
        down_one(k).start()

    each(own_chunk)

    def settle(k):
        proj_a(k).wait_send()
        proj_y(k).wait_send()

    each(settle)

    def far_sum(k):
        part = chunk(k, size)
        back_a(k).wait_recv()
        ys_ref[part] = (ys_ref[part].astype(F32) + ar_ref[part].astype(F32)).astype(BF)
        back_y(k).start()

    def far_chunk(k):
        part = chunk(k, size)
        two_far(k).wait_recv()
        two_on(k).start()

        @pl.when(k > 0)
        def _():
            far_sum(k - 1)

        two_on(k).wait_recv()
        back, down = feed(k, far, farsib, c2, c3)
        as_ref[part] = back[size:].astype(BF)
        back_a(k).start()
        ys_ref[part] = back[:size].astype(BF)
        d3s_ref[part] = down[size:].astype(BF)
        down_three(k).start()
        fardown_ref[part] = down[:size].astype(BF)

    each(far_chunk)
    far_sum(STEPS - 1)

    parity = lax.rem(seq, 2)
    piece = model // seq_count

    def weight_home(w, b):
        return pltpu.make_async_copy(
            dw_ref.at[w, 0, b], keep_ref.at[b, w], wloc.at[w, b]
        )

    def weight_away(w, b):
        return push(
            dw_ref.at[w, 1, b], got_ref.at[b, w], xsnd.at[w, b], xrcv.at[w, b], (near, me)
        )

    def weight_tile(w, k):
        cots = (c0, c1, c2, c3)
        order = (me, sib, far, farsib)
        right = (act_ref, gg_ref, gu_ref)[w]
        span = model // STEPS
        total = None
        for r in range(4):
            cols = chunk(k, span)
            left = cots[r][:, cols] if w == 0 else n_ref[order[r], :, cols]
            term = dot_tn(left, right[order[r]])
            total = term if total is None else total + term
        total = total[:, :units].astype(BF).reshape(span // (2 * piece), 2, piece, units)
        return total

    def weights_step(k):
        per = model // STEPS // (2 * piece)
        for w in range(3):
            tile = weight_tile(w, k)
            for j in range(per):
                b = k * per + j

                @pl.when(parity == 0)
                def _():
                    dw_ref[w, 0, b] = tile[j, 0]
                    dw_ref[w, 1, b] = tile[j, 1]

                @pl.when(parity == 1)
                def _():
                    dw_ref[w, 0, b] = tile[j, 1]
                    dw_ref[w, 1, b] = tile[j, 0]

                weight_home(w, b).start()
                weight_away(w, b).start()

    gain_out[...] = jnp.zeros_like(gain_out)

    def back_chunk(k):
        weights_step(k)
        part = chunk(k, size)
        back_one(k).wait_recv()
        back_y(k).wait_recv()
        grad_norm = g0_ref[part].astype(F32) + g1r_ref[part].astype(F32) + yr_ref[part].astype(F32)
        hidden = rest_ref[part]
        _, scaling = norm_rows(hidden, gain_ref[...])
        grad_rows, grad_gain = norm_back(hidden, scaling, gain_ref[...], grad_norm)
        grad = c0[part].astype(F32) + grad_rows
        grad_ref[part] = grad
        gain_out[...] += grad_gain
        gb_ref[part] = grad.astype(BF)
        branch_out(12, k, far).start()
        branch_out(11, k, sib).start()
        branch_home(k).start()

    each(back_chunk)

    def finish(k):
        part = chunk(k, size)
        down_one(k).wait_recv()
        down_three(k).wait_recv()
        rest_ref[part] += d0_ref[part].astype(F32) + d1r_ref[part].astype(F32)
        fardown_ref[part] = (fardown_ref[part].astype(F32) + d3r_ref[part].astype(F32)).astype(BF)
        branch_out(12, k, far).wait_recv()
        branch_on(k).start()

    each(finish)

    def close(k):
        branch_out(11, k, sib).wait_recv()
        branch_on(k).wait_recv()
        branch_home(k).wait()
        for made in (
            proj_b, two_sib, two_far, two_on, back_one, down_one, back_a, back_y, down_three, branch_on,
        ):
            made(k).wait_send()
        branch_out(11, k, sib).wait_send()
        branch_out(12, k, far).wait_send()

    each(close)

    def close_weights(b):
        for w in range(3):
            weight_home(w, b).wait()
            weight_away(w, b).wait_recv()
            weight_away(w, b).wait_send()

    each(close_weights, half)


def middle_call(heads_out, wo_t, x, gain, cots, weights, units):
    seq_count = lax.axis_size("seq")
    rows, model = x.shape
    half = seq_count // 2
    piece = model // seq_count
    wide = weights[0].shape[1]
    dma = pltpu.SemaphoreType.DMA
    shape = jax.ShapeDtypeStruct
    part = shape((half, 3, piece, units), BF)
    rows_bf = pltpu.VMEM((rows, model), BF)
    return pl.pallas_call(
        functools.partial(middle_kernel, seq_count),
        in_specs=[VM] * 11,
        out_specs=[VM] * 4 + [ANY] * 3,
        out_shape=[
            shape((rows, model), F32),
            shape((rows, model), BF),
            shape((rows, model), F32),
            shape((1, model), F32),
            shape((4, rows, model), BF),
        ]
        + [part] * 2,
        scratch_shapes=[pltpu.VMEM((4, rows, model), BF)]
        + [pltpu.VMEM((4, rows, wide), BF)] * 3
        + [rows_bf] * 15
        + [pltpu.VMEM((3, 2, half, piece, units), BF)]
        + [
            dma((14, STEPS)),
            dma((14, STEPS)),
            dma((3, half)),
            dma((3, half)),
            dma((STEPS,)),
            dma((3, half)),
        ],
        compiler_params=params(collective_id=1, has_side_effects=True),
        cost_estimate=cost(100_000_000_000, 30_000_000),
        name="middle",
    )(heads_out, wo_t, x, gain, *cots, *weights)


def last_kernel(
    seq_count, mixed_ref, w_ref, x_ref, gain_ref, grad_ref, n_ref, heads_ref, branch_ref, gain_in,
    out_ref, wqkv_ref, wout_ref, gains_ref,
    as_ref, ar_ref, ys_ref, yr_ref, bs_ref, br_ref, dw_ref, got_ref, sum_ref, zr_ref, gs_ref, gr_ref,
    snd, rcv, xsnd, xrcv, zsnd, zrcv, gsnd, grcv,
):
    me, sib, far, farsib, core = places()
    seq = lax.axis_index("seq")
    parity, place, half = lax.rem(seq, 2), seq // 2, seq_count // 2
    near = seq + 1 - 2 * parity
    level = [lax.rem(seq + 2 * j, seq_count) for j in range(1, half)]
    greet([(seq, sib), (seq, far), (near, me)] + [(s, me) for s in level])
    rows, model = x_ref.shape
    size = rows // STEPS
    piece = model // seq_count
    wide = mixed_ref.shape[-1]

    def copy(kind, k, src, dst, to):
        return push(
            src.at[chunk(k, size)], dst.at[chunk(k, size)], snd.at[kind, k], rcv.at[kind, k], (seq, to)
        )

    back_a = lambda k: copy(0, k, as_ref, ar_ref, sib)
    back_y = lambda k: copy(1, k, ys_ref, yr_ref, far)
    back_b = lambda k: copy(2, k, bs_ref, br_ref, sib)

    def near_copy(b):
        return push(dw_ref.at[1, b], got_ref.at[b], xsnd.at[b], xrcv.at[b], (near, me))

    def level_copy(j):
        b = lax.rem(place + j, half)
        return push(sum_ref.at[b], zr_ref.at[j], zsnd.at[j], zrcv.at[j], (level[j - 1], me))

    def each(body, count=STEPS):
        lax.fori_loop(0, count, lambda k, c: (body(k), c)[1], 0)

    def project(block, k):
        return dot_nt(mixed_ref[block, chunk(k, size)], w_ref[...])

    def send_three(k):
        as_ref[chunk(k, size)] = project(farsib, k).astype(BF)
        back_a(k).start()

    def send_two(k):
        part = project(far, k)
        back_a(k).wait_recv()
        ys_ref[chunk(k, size)] = (part + ar_ref[chunk(k, size)].astype(F32)).astype(BF)
        back_y(k).start()

    def send_one(k):
        bs_ref[chunk(k, size)] = project(sib, k).astype(BF)
        back_b(k).start()

    span = model // STEPS
    per = span // (2 * piece)

    def weights_step(k):
        cols = chunk(k, span)
        to_qkv, to_out = None, None
        for r in range(4):
            term = dot_tn(n_ref[r, :, cols], mixed_ref[r])
            to_qkv = term if to_qkv is None else to_qkv + term
            term = dot_tn(branch_ref[r, :, cols], heads_ref[r])
            to_out = term if to_out is None else to_out + term
        for ref_at, value in ((slice(0, wide), to_qkv), (slice(wide, None), to_out)):
            tile = value.astype(BF).reshape(per, 2, piece, value.shape[1])
            for j in range(per):
                b = k * per + j

                @pl.when(parity == 0)
                def _():
                    dw_ref[0, b, :, ref_at] = tile[j, 0]
                    dw_ref[1, b, :, ref_at] = tile[j, 1]

                @pl.when(parity == 1)
                def _():
                    dw_ref[0, b, :, ref_at] = tile[j, 1]
                    dw_ref[1, b, :, ref_at] = tile[j, 0]

        for j in range(per):
            near_copy(k * per + j).start()

    each(send_three)
    each(send_two)
    each(weights_step)
    each(send_one)

    gs_ref[...] = jnp.zeros_like(gs_ref)

    def own_chunk(k):
        part = chunk(k, size)
        total = project(me, k)
        x = x_ref[part].astype(F32)
        _, scaling = norm_rows(x, gain_ref[...])
        back_b(k).wait_recv()
        back_y(k).wait_recv()
        grad_norm = total + br_ref[part].astype(F32) + yr_ref[part].astype(F32)
        grad_rows, grad_gain = norm_back(x, scaling, gain_ref[...], grad_norm)
        out_ref[part] = grad_ref[part] + grad_rows
        gs_ref[0, 0:1] += grad_gain

    def near_sum(b):
        near_copy(b).wait_recv()
        sum_ref[b] = (dw_ref[0, b].astype(F32) + got_ref[b].astype(F32)).astype(BF)

    def both(k):
        own_chunk(k)
        for j in range(half // STEPS):
            near_sum(k * (half // STEPS) + j)

    each(both)
    for j in range(1, half):
        level_copy(j).start()

    gs_ref[0, 1:2] = gain_in[...]
    others = [(seq, sib), (seq, far), (near, me)]

    def gain_copy(n, slot, to):
        return push(gs_ref.at[n], gr_ref.at[slot], gsnd.at[slot], grcv.at[slot], to)

    for n, to in enumerate(others):
        gain_copy(n, n, to).start()
        gain_copy(n, n, to).wait_recv()
        gs_ref[n + 1] = gs_ref[n] + gr_ref[n]
    for j in range(1, half):
        gain_copy(3, 2 + j, (level[j - 1], me)).start()
    gains = gs_ref[3]
    for j in range(1, half):
        gain_copy(3, 2 + j, (level[j - 1], me)).wait_recv()
        gains = gains + gr_ref[2 + j]
    gains_ref[...] = gains

    total = sum_ref[place].astype(F32)
    for j in range(1, half):
        level_copy(j).wait_recv()
        total = total + zr_ref[j].astype(F32)
    wqkv_ref[...] = total[:, :wide]
    wout_ref[...] = total[:, wide:]

    def close(k):
        for made in (back_a, back_y, back_b):
            made(k).wait_send()

    each(close)
    each(lambda b: near_copy(b).wait_send(), half)
    for n, to in enumerate(others):
        gain_copy(n, n, to).wait_send()
    for j in range(1, half):
        gain_copy(3, 2 + j, (level[j - 1], me)).wait_send()
        level_copy(j).wait_send()


def last_call(mixed, w, x, gain, grad, normed, heads_out, branch, gain_two):
    seq_count = lax.axis_size("seq")
    rows, model = x.shape
    half = seq_count // 2
    piece = model // seq_count
    wide, width = mixed.shape[-1], heads_out.shape[-1]
    dma = pltpu.SemaphoreType.DMA
    shape = jax.ShapeDtypeStruct
    rows_bf = pltpu.VMEM((rows, model), BF)
    pieces = pltpu.VMEM((half, piece, wide + width), BF)
    return pl.pallas_call(
        functools.partial(last_kernel, seq_count),
        in_specs=[VM] * 9,
        out_specs=[VM] * 4,
        out_shape=[
            shape((rows, model), F32),
            shape((piece, wide), F32),
            shape((piece, width), F32),
            shape((8, model), F32),
        ],
        scratch_shapes=[rows_bf] * 6
        + [pltpu.VMEM((2, half, piece, wide + width), BF), pieces, pieces, pieces]
        + [pltpu.VMEM((4, 8, model), F32), pltpu.VMEM((half + 2, 8, model), F32)]
        + [
            dma((3, STEPS)),
            dma((3, STEPS)),
            dma((half,)),
            dma((half,)),
            dma((half,)),
            dma((half,)),
            dma((half + 2,)),
            dma((half + 2,)),
        ],
        compiler_params=params(collective_id=2, has_side_effects=True),
        cost_estimate=cost(60_000_000_000, 30_000_000),
        name="last",
    )(mixed, w, x, gain, grad, normed, heads_out, branch, gain_two)


def spread_kernel(sc, em_ref, om_ref, es_ref, os_ref, out_ref, flat_ref):
    mine, places = em_ref.shape[1], em_ref.shape[2]
    odd = (pl.program_id(0) ^ sc[1]) % 2

    def put(m_ref, s_ref):
        for k in range(mine):
            for ref, first in ((m_ref, sc[0] * mine), (s_ref, (1 - sc[0]) * mine)):
                at = pl.multiple_of((first + k) * places, 8)
                flat_ref[pl.ds(at, places)] = ref[0, k].astype(F32)

    @pl.when(odd == 0)
    def _():
        put(em_ref, es_ref)

    @pl.when(odd == 1)
    def _():
        put(om_ref, os_ref)

    def body(n, carry):
        for u in range(8):
            row = n * 8 + u
            out_ref[:, pl.ds(pl.multiple_of(row * LANES, LANES), LANES)] = jnp.concatenate(
                [flat_ref[pl.ds(k * places + row, 1), :] for k in range(2 * mine)], axis=0
            )
        return carry

    lax.fori_loop(0, places // 8, body, 0)


def spread_call(even_mine, odd_mine, even_sib, odd_sib, core, seq, hash_rows):
    halves, mine, places, lanes = even_mine.shape
    piece = pl.BlockSpec((1, mine, places, lanes), lambda i, sc: ((i ^ sc[1]) // 2, 0, 0, 0))
    return pl.pallas_call(
        spread_kernel,
        grid_spec=pltpu.PrefetchScalarGridSpec(
            num_scalar_prefetch=1,
            grid=(2 * halves,),
            in_specs=[piece] * 4,
            out_specs=pl.BlockSpec((2 * mine, places * lanes), lambda i, sc: (0, i)),
            scratch_shapes=[pltpu.VMEM((2 * mine * places, lanes), F32)],
        ),
        out_shape=jax.ShapeDtypeStruct((2 * mine, hash_rows), F32),
        compiler_params=params(),
        cost_estimate=cost(1_000_000, 24_000_000),
        name="hash_spread",
    )(jnp.stack([core, seq]).astype(jnp.int32), even_mine, odd_mine, even_sib, odd_sib)


def spread_tables(mine, core, seq):
    seq_count = lax.axis_size("seq")
    even = jnp.stack([mine] + [flip(mine, "seq", 2 * j) for j in range(1, seq_count // 2)])
    odd = flip(even, "seq", 1)
    return spread_call(
        even, odd, flip(even, "tp", 1), flip(odd, "tp", 1), core, seq, HASH_ROWS
    )


def shards(
    latents_in,
    gain_one,
    w_qkv,
    w_out,
    gain_two,
    w_gate,
    w_up,
    w_down,
    cotangent,
    doc_lengths,
    valid_lengths,
    hash_ids,
    hash_weights,
):
    local_rows, model_width = latents_in.shape
    local_width = w_qkv.shape[2]
    group_rows = 4 * local_rows
    units = w_gate.shape[1]
    rank = lax.axis_index("tp")
    seq = lax.axis_index("seq")
    core = rank % 2
    seq_count = lax.axis_size("seq")
    lengths, valid = doc_lengths[0], valid_lengths[0]
    start_one = lengths[0]
    start_two = lengths[0] + lengths[1]
    sc = jnp.stack(
        [rank, start_one, start_two, valid[0], start_one + valid[1], start_two + valid[2]]
    ).astype(jnp.int32)
    gain_one, gain_two = gain_one[None], gain_two[None]

    tables = hash_ids.shape[0] // 2
    blank = jnp.zeros((8 - 2 * tables, local_rows), F32)
    pairs = jnp.stack(
        [
            jnp.concatenate(
                [
                    hash_ids[c * tables : (c + 1) * tables].astype(F32),
                    hash_weights[c * tables : (c + 1) * tables],
                    blank,
                ]
            )
            for c in range(2)
        ]
    )
    per_seq = -(-HASH_ROWS // seq_count)
    high_rows = -(-per_seq // (LANES * 8)) * 8

    qkv_weight = w_qkv.reshape(model_width, 3 * local_width)
    normed, qkv, sums = front_call(latents_in, gain_one, qkv_weight, pairs, high_rows)
    sums, cotangent_late = lax.optimization_barrier((sums, cotangent))
    qkv = qkv.reshape(group_rows, 3 * local_width)
    heads_out, lse = attend_call(sc, qkv)
    cot_far = flip(cotangent_late, "tp", 2)
    cots = [cotangent, flip(cotangent_late, "tp", 1), cot_far, flip(cot_far, "tp", 1)]

    pad = -units % 256
    weights = [jnp.pad(w, ((0, 0), (0, pad))) for w in (w_gate, w_up, w_down)]
    heads_four = heads_out.reshape(4, local_rows, local_width)
    rest, far_down, grad_hidden, gain_two_part, branch, keep, got = middle_call(
        heads_four, w_out.T, latents_in, gain_two, cots, weights, units
    )
    down_far = flip(far_down, "tp", 2)
    half_sum = (keep.astype(F32) + got.astype(F32)).astype(BF)
    place = seq // 2
    pieces = [
        lax.dynamic_index_in_dim(half_sum, place ^ j, 0, keepdims=False)
        for j in range(seq_count // 2)
    ]
    arrived = [flip(pieces[j], "seq", 2 * j) for j in range(1, seq_count // 2)]
    mixed = attend_back_call(
        sc, branch.reshape(group_rows, model_width), w_out, qkv, heads_out, lse
    )
    grad_latents, qkv_total, out_total, gains = last_call(
        mixed.reshape(4, local_rows, -1), qkv_weight, latents_in, gain_one, grad_hidden,
        normed, heads_four, branch, gain_two_part,
    )
    qkv_total = qkv_total.reshape(-1, 3, local_width)
    total = pieces[0].astype(F32)
    for piece in arrived:
        total = total + piece.astype(F32)
    latents_out = (rest + down_far.astype(F32)).astype(BF)
    hash_counts = spread_tables(sums, core, seq)
    return (
        latents_out,
        grad_latents,
        gains[0],
        qkv_total,
        out_total,
        gains[1],
        total[1],
        total[2],
        total[0],
        hash_counts,
    )


def solution(mesh):
    in_specs = (
        P(("seq", "tp"), None),
        P(),
        P(None, None, "tp"),
        P(None, "tp"),
        P(),
        P(None, "tp"),
        P(None, "tp"),
        P(None, "tp"),
        P(("seq", "tp"), None),
        P("seq", None),
        P("seq", None),
        P(None, ("seq", "tp")),
        P(None, ("seq", "tp")),
    )
    out_specs = (
        P(("seq", "tp"), None),
        P(("seq", "tp"), None),
        P(),
        P("seq", None, "tp"),
        P("seq", "tp"),
        P(),
        P("seq", "tp"),
        P("seq", "tp"),
        P("seq", "tp"),
        P(),
    )
    return jax.shard_map(shards, mesh=mesh, in_specs=in_specs, out_specs=out_specs, check_vma=False)
```

time: 609 us -> 415 us (0.68); the launches traced: 597 us -> 411 us
  Pallas kernels: 178 us -> 326 us
  waiting for transfers between devices: 156 us -> 25.3 us
  starting transfers between devices: 72 us -> 12.1 us
  blocking collectives: 40.4 us -> 0 us
  matrix products: 38.9 us -> 0 us
  local copies, waits for them, and re-layouts: 57.7 us -> 32.6 us
  other arithmetic: 35.5 us -> 10.6 us
  between operations: 18.3 us -> 4.09 us
    pallas_call x9 -> x5, Pallas kernels: 152 us -> 300 us  [the longest x1 117 us: middle_call(): pl.pallas_call(functools.partial(middle_kernel, seq_count), in_specs=[VM]...]
    ppermute x50 -> x13, waiting for transfers between devices: 156 us -> 25.3 us  [flip(): return lax.ppermute(x, axis, [(i, i ^ bits) for i in range(count)])]
    ppermute x50 -> x13, starting transfers between devices: 71.9 us -> 12.1 us  [flip(): return lax.ppermute(x, axis, [(i, i ^ bits) for i in range(count)])]
    psum x1 -> x0, blocking collectives: 40.4 us -> none  [shards(): lax.psum((grad_gain_one, grad_gain_two), ('seq', 'tp'))]
    dot_general x9 -> x0, matrix products: 38.9 us -> none  [the longest x5 25.3 us: contract_rows(): lax.dot_general(left, right, (((0,), (0,)), ((), ())), preferred_element_...]
    dynamic_slice x8 -> x4, local copies, waits for them, and re-layouts: 20.8 us -> 5.15 us  [shards(): lax.dynamic_index_in_dim(half_sum, place ^ j, 0, keepdims=False)]
    reshape x3 -> x0, local copies, waits for them, and re-layouts: 14.8 us -> none  [scatter_weights(): parts = grad.astype(BF).reshape(count // 2, 2, rows // count, wide)]
    convert_element_type x13 -> x3, other arithmetic: 17.9 us -> 5.56 us  [the longest x1 3 us: shards(): half_sum = (keep.astype(F32) + got.astype(F32)).astype(BF)]
  transfers between devices with their start and end apart: 51 -> 13, of which waited for: 15 -> 2; matrix products, arithmetic and copies ran while one was open for 17% -> 9% of each run, Pallas kernels for 26% -> 60%
where the time goes in v2:
time: 415 us; the launch traced here: 411 us
  Pallas kernels  326 us (79%)
  local copies, waits for them, and re-layouts  32.6 us (8%)
  waiting for transfers between devices  25.3 us (6%)
  starting transfers between devices  12.1 us (3%)
  other arithmetic  10.6 us (3%)
    pallas_call x1, Pallas kernels, middle_call(): pl.pallas_call(functools.partial(middle_kernel, seq_count), in_specs=[VM]...  117 us
    pallas_call x1, Pallas kernels, last_call(): pl.pallas_call(functools.partial(last_kernel, seq_count), in_specs=[VM] *...  67.2 us
    pallas_call x1, Pallas kernels, front_call(): pl.pallas_call(functools.partial(front_kernel, seq_count, tables), in_spe...  52.3 us
    pallas_call x1, Pallas kernels, attend_back_call(): pl.pallas_call(functools.partial(attend_back_kernel, heads), grid_spec=pl...  34.4 us
    pallas_call x1, Pallas kernels, attend_call(): pl.pallas_call(functools.partial(attend_kernel, heads), grid_spec=pltpu.P...  28.9 us
    pallas_call x1, Pallas kernels, spread_call(): pl.pallas_call(spread_kernel, grid_spec=pltpu.PrefetchScalarGridSpec(num_...  26.4 us
    ppermute x13, waiting for transfers between devices, flip(): return lax.ppermute(x, axis, [(i, i ^ bits) for i in range(count)])  25.3 us
    ppermute x13, starting transfers between devices, flip(): return lax.ppermute(x, axis, [(i, i ^ bits) for i in range(count)])  12.1 us
  transfers between devices with their start and end apart: 13, of which 2 were waited for; matrix products, arithmetic and copies ran while one was open for 9% of the time, Pallas kernels for 60%

profile of v2, /device:TPU:0, one launch (start us, length us, event | category | flops | bytes accessed | tf_op | source)
XLA Modules:
  0.0 411.2 jit_solution(16885756672095178348)
XLA Ops:
  0.6 1.7 copy.59
  2.4 1.6 copy.60.w_ref
  4.8 52.3 %front.1 = (bf16[4,512,1024]{2,1,0:T(8,128)(2,1)}, bf16[4,512,768]{2,1,0:T(8,128)(2,1)}, bf16[3,248,256]{2,1,0:T(8,128)(2,1)}) custom-call(bf16[512,1024]{1,0:T(8,128)(2,1)} %x_ref.5, f32[1,1024]{1,0:T(1,128)} %bitcast.51, bf16[1024,768]{1,0:T(8,128)(2,1)} %copy.60.w_ref, f32[2,8,512]{2,1,0:T(8,128)} %pad_maximum_fusion.1.pair_ref), custom_call_target="tpu_custom_call" | custom-call | flops 30000001024 | bytes 10000000 | tf_op jit(solution)/shard_map/front/pallas_call | solution.py:208
  57.7 2.5 collective-permute-start.9
  60.1 1.9 collective-permute-start.7
  65.9 1.9 stack.52.sc
  67.8 3.7 collective-permute-done.9
  71.5 21.5 %collective-permute-done.8 = bf16[3,248,256]{2,1,0:T(8,128)(2,1)S(1)} collective-permute-done((bf16[3,248,256]{2,1,0:T(8,128)(2,1)}, bf16[3,248,256]{2,1,0:T(8,128)(2,1)S(1)}, u32[]{:S(2)}, u32[]{:S(2)}) %collective-permute-start.8) | collective-permute-done | bytes 380960 | tf_op jit(solution)/shard_map/ppermute | solution.py:25
  93.1 2.4 pad_maximum_fusion.em_ref
  95.5 1.5 collective-permute-start.10
  97.0 28.9 %attend.1 = (bf16[2048,256]{1,0:T(8,128)(2,1)}, f32[8,2048]{1,0:T(8,128)}) custom-call(s32[6]{0:T(128)} %stack.52.sc, bf16[2048,768]{1,0:T(8,128)(2,1)} %bitcast.54), custom_call_target="tpu_custom_call" | custom-call | flops 35000000512 | bytes 8000000 | tf_op jit(solution)/shard_map/attend/pallas_call | solution.py:300
  127.6 1.7 copy.63
  130.6 1.3 pad.11.wu_ref
  135.8 117.2 %middle.1 = (f32[512,1024]{1,0:T(8,128)}, bf16[512,1024]{1,0:T(8,128)(2,1)}, f32[512,1024]{1,0:T(8,128)}, f32[1,1024]{1,0:T(1,128)}, bf16[4,512,1024]{2,1,0:T(8,...) custom-call(bf16[4,512,256]{2,1,0:T(8,128)(2,1)} %bitcast.57, bf16[256,1024]{1,0:T(8,128)(2,1)} %bitcast.43, ...), custom_call_target="tpu_custom_call" | custom-call | flops 99999997952 | bytes 30000000 | tf_op jit(solution)/shard_map/middle/pallas_call | solution.py:684
  253.7 3.0 add_convert_fusion
  257.7 2.1 copy.71
  259.8 1.4 collective-permute-start.6
  262.2 34.4 %attend_back.1 = bf16[2048,768]{1,0:T(8,128)(2,1)} custom-call(s32[6]{0:T(128)} %stack.52.sc, bf16[2048,1024]{1,0:T(8,128)(2,1)} %bitcast.53, bf16[1024,256]{1,0:T(8,128)(2,1)} %wo_ref.1, bf16[2048,768]{1,0:T(8,128)(2,1)} %bitcast.55, bf16[2048,256]{1,0:T(8,128)(2,1)} %get-tuple-element.29.heads_ref, f32[8,2048]{1,0:T(8,128)} %get-tuple-element.35.lse_ref), custom_call_target="tpu_custom_call" | custom-call | flops 44999999488 | bytes 12000000 | tf_op jit(solution)/shard_map/attend_back/pallas_call | solution.py:395
  297.7 3.0 collective-permute-start.4
  300.7 67.2 %last.1 = (f32[512,1024]{1,0:T(8,128)}, f32[128,768]{1,0:T(8,128)}, f32[128,256]{1,0:T(8,128)}, f32[8,1024]{1,0:T(8,128)}) custom-call(bf16[4,512,768]{2,1,0:T(8,128)(2,1)} %bitcast.56, bf16[1024,768]{1,0:T(8,128)(2,1)} %copy.60.w_ref, bf16[512,1024]{1,0:T(8,128)(2,1)} %x_ref.5, f32[1,1024]{1,0:T(1,128)} %bitcast.52, ...), custom_call_target="tpu_custom_call" | custom-call | flops 60000002048 | bytes 30000000 | tf_op jit(solution)/shard_map/last/pallas_call | solution.py:876
  370.0 1.4 fusion.2
  374.0 2.1 copy.68
  380.3 2.5 add_convert_fusion.1
  382.8 26.4 %hash_spread.1 = f32[6,500002]{1,0:T(8,128)} custom-call(s32[2]{0:T(128)} %pad_add_fusion.sc, bf16[4,3,248,256]{3,2,1,0:T(8,128)(2,1)} %pad_maximum_fusion.em_ref, bf16[4,3,248,256]{3,2,1,0:T(8,128)(2,1)} %collective-permute-done.10.om_ref, bf16[4,3,248,256]{3,2,1,0:T(8,128)(2,1)} %collective-permute-done.11.es_ref, ...), custom_call_target="tpu_custom_call" | custom-call | flops 1000000 | bytes 24000000 | tf_op jit(solution)/shard_map/hash_spread/pallas_call | solution.py:937
  (66 shorter events, 23.3 us)
Async XLA Ops:
  2.4 1.6 copy-start.6
  2.4 1.6 copy-start.7
  4.8 57.3 %copy-start.8 = (s32[1,3]{1,0:T(1,128)S(1)}, s32[1,3]{1,0:T(1,128)}, u32[]{:S(2)}) copy-start(s32[1,3]{1,0:T(1,128)} %param.23) | copy-start | bytes 40
  4.8 57.3 %copy-start.9 = (s32[1,3]{1,0:T(1,128)S(1)}, s32[1,3]{1,0:T(1,128)}, u32[]{:S(2)}) copy-start(s32[1,3]{1,0:T(1,128)} %param.22) | copy-start | bytes 40
  57.1 39.9 %collective-permute-start.1 = (bf16[512,1024]{1,0:T(8,128)(2,1)}, bf16[512,1024]{1,0:T(8,128)(2,1)}, u32[]{:S(2)}, u32[]{:S(2)}) collective-permute-start(bf16[512,1024]{1,0:T(8,128)(2,1)} %c0.1), channel_id=1, source_target_pairs={{0,2},{1,3},{2,0},{3,1},{4,6},{5,7},{6,4},{7,5},{8,10},{9,11},{10,... | collective-permute-start | bytes 3145736 | tf_op jit(solution)/shard_map/ppermute | solution.py:25
  57.7 13.8 %collective-permute-start.9 = (bf16[3,248,256]{2,1,0:T(8,128)(2,1)}, bf16[3,248,256]{2,1,0:T(8,128)(2,1)S(1)}, u32[]{:S(2)}, u32[]{:S(2)}) collective-permute-start(bf16[3,248,256]{2,1,0:T(8,128)(2,1)} %get-tuple-element.45), channel_id=1, source_target_pairs={{0,24},{4,28},{8,16},{12,20},{16,8},{20,12},{24,0},{28,4},{1,25},{... | collective-permute-start | bytes 1142792 | tf_op jit(solution)/shard_map/ppermute | solution.py:25
  60.1 32.9 %collective-permute-start.8 = (bf16[3,248,256]{2,1,0:T(8,128)(2,1)}, bf16[3,248,256]{2,1,0:T(8,128)(2,1)S(1)}, u32[]{:S(2)}, u32[]{:S(2)}) collective-permute-start(bf16[3,248,256]{2,1,0:T(8,128)(2,1)} %get-tuple-element.45), channel_id=1, source_target_pairs={{0,16},{4,20},{8,24},{12,28},{16,0},{20,4},{24,8},{28,12},{1,17},{... | collective-permute-start | bytes 1142792 | tf_op jit(solution)/shard_map/ppermute | solution.py:25
  60.1 32.9 %collective-permute-start.7 = (bf16[3,248,256]{2,1,0:T(8,128)(2,1)}, bf16[3,248,256]{2,1,0:T(8,128)(2,1)S(1)}, u32[]{:S(2)}, u32[]{:S(2)}) collective-permute-start(bf16[3,248,256]{2,1,0:T(8,128)(2,1)} %get-tuple-element.45), channel_id=1, source_target_pairs={{0,8},{4,12},{8,0},{12,4},{16,24},{20,28},{24,16},{28,20},{1,9},{5... | collective-permute-start | bytes 1142792 | tf_op jit(solution)/shard_map/ppermute | solution.py:25
  62.1 73.7 %collective-permute-start = (bf16[512,1024]{1,0:T(8,128)(2,1)}, bf16[512,1024]{1,0:T(8,128)(2,1)}, u32[]{:S(2)}, u32[]{:S(2)}) collective-permute-start(bf16[512,1024]{1,0:T(8,128)(2,1)} %c0.1), channel_id=1, source_target_pairs={{0,1},{1,0},{2,3},{3,2},{4,5},{5,4},{6,7},{7,6},{8,9},{9,8},{10,11... | collective-permute-start | bytes 3145736 | tf_op jit(solution)/shard_map/ppermute | solution.py:25
  95.5 40.3 %collective-permute-start.10 = (bf16[4,3,248,256]{3,2,1,0:T(8,128)(2,1)}, bf16[4,3,248,256]{3,2,1,0:T(8,128)(2,1)}, u32[]{:S(2)}, u32[]{:S(2)}) collective-permute-start(bf16[4,3,248,256]{3,2,1,0:T(8,128)(2,1)} %pad_maximum_fusion.em_ref), channel_id=1, source_target_pairs={{0,4},{4,0},{8,12},{12,8},{16,20},{20,16},{24,28},{28,24},{1,5},{5... | collective-permute-start | bytes 4571144 | tf_op jit(solution)/shard_map/ppermute | solution.py:25
  97.0 38.8 %collective-permute-start.2 = (bf16[512,1024]{1,0:T(8,128)(2,1)}, bf16[512,1024]{1,0:T(8,128)(2,1)}, u32[]{:S(2)}, u32[]{:S(2)}) collective-permute-start(bf16[512,1024]{1,0:T(8,128)(2,1)} %collective-permute-done.1.c2), channel_id=1, source_target_pairs={{0,1},{1,0},{2,3},{3,2},{4,5},{5,4},{6,7},{7,6},{8,9},{9,8},{10,11... | collective-permute-start | bytes 3145736 | tf_op jit(solution)/shard_map/ppermute | solution.py:25
  97.0 28.9 %copy-start.4 = (bf16[1024,256]{1,0:T(8,128)(2,1)S(1)}, bf16[1024,256]{1,0:T(8,128)(2,1)}, u32[]{:S(2)}) copy-start(bf16[1024,256]{1,0:T(8,128)(2,1)} %wo_ref.1) | copy-start | bytes 1572868
  97.0 30.0 %copy-start.2 = (bf16[1024,704]{0,1:T(8,128)(2,1)S(1)}, bf16[1024,704]{0,1:T(8,128)(2,1)}, u32[]{:S(2)}) copy-start(bf16[1024,704]{0,1:T(8,128)(2,1)} %param.18) | copy-start | bytes 4325380
  130.6 1.9 copy-start.3
  135.3 247.6 %collective-permute-start.11 = (bf16[4,3,248,256]{3,2,1,0:T(8,128)(2,1)}, bf16[4,3,248,256]{3,2,1,0:T(8,128)(2,1)}, u32[]{:S(2)}, u32[]{:S(2)}) collective-permute-start(bf16[4,3,248,256]{3,2,1,0:T(8,128)(2,1)} %pad_maximum_fusion.em_ref), channel_id=1, source_target_pairs={{0,1},{1,0},{2,3},{3,2},{4,5},{5,4},{6,7},{7,6},{8,9},{9,8},{10,11... | collective-permute-start | bytes 4571144 | tf_op jit(solution)/shard_map/ppermute | solution.py:25
  135.7 247.1 %collective-permute-start.12 = (bf16[4,3,248,256]{3,2,1,0:T(8,128)(2,1)}, bf16[4,3,248,256]{3,2,1,0:T(8,128)(2,1)}, u32[]{:S(2)}, u32[]{:S(2)}) collective-permute-start(bf16[4,3,248,256]{3,2,1,0:T(8,128)(2,1)} %collective-permute-done.10.om_ref), channel_id=1, source_target_pairs={{0,1},{1,0},{2,3},{3,2},{4,5},{5,4},{6,7},{7,6},{8,9},{9,8},{10,11... | collective-permute-start | bytes 4571144 | tf_op jit(solution)/shard_map/ppermute | solution.py:25
  253.0 127.3 %collective-permute-start.3 = (bf16[512,1024]{1,0:T(8,128)(2,1)}, bf16[512,1024]{1,0:T(8,128)(2,1)}, u32[]{:S(2)}, u32[]{:S(2)}) collective-permute-start(bf16[512,1024]{1,0:T(8,128)(2,1)} %get-tuple-element.33), channel_id=1, source_target_pairs={{0,2},{1,3},{2,0},{3,1},{4,6},{5,7},{6,4},{7,5},{8,10},{9,11},{10,... | collective-permute-start | bytes 3145736 | tf_op jit(solution)/shard_map/ppermute | solution.py:25
  259.8 37.9 %collective-permute-start.6 = (bf16[3,128,704]{1,2,0:T(8,128)(2,1)}, bf16[3,128,704]{1,2,0:T(8,128)(2,1)}, u32[]{:S(2)}, u32[]{:S(2)}) collective-permute-start(bf16[3,128,704]{1,2,0:T(8,128)(2,1)} %bitcast.42), channel_id=1, source_target_pairs={{0,24},{4,28},{8,16},{12,20},{16,8},{20,12},{24,0},{28,4},{1,25},{... | collective-permute-start | bytes 1622024 | tf_op jit(solution)/shard_map/ppermute | solution.py:25
  262.2 110.6 %collective-permute-start.5 = (bf16[3,128,704]{1,2,0:T(8,128)(2,1)}, bf16[3,128,704]{1,2,0:T(8,128)(2,1)}, u32[]{:S(2)}, u32[]{:S(2)}) collective-permute-start(bf16[3,128,704]{1,2,0:T(8,128)(2,1)} %bitcast.41), channel_id=1, source_target_pairs={{0,16},{4,20},{8,24},{12,28},{16,0},{20,4},{24,8},{28,12},{1,17},{... | collective-permute-start | bytes 1622024 | tf_op jit(solution)/shard_map/ppermute | solution.py:25
  297.7 76.4 %collective-permute-start.4 = (bf16[3,128,704]{1,2,0:T(8,128)(2,1)}, bf16[3,128,704]{1,2,0:T(8,128)(2,1)}, u32[]{:S(2)}, u32[]{:S(2)}) collective-permute-start(bf16[3,128,704]{1,2,0:T(8,128)(2,1)} %bitcast.20), channel_id=1, source_target_pairs={{0,8},{4,12},{8,0},{12,4},{16,24},{20,28},{24,16},{28,20},{1,9},{5... | collective-permute-start | bytes 1622024 | tf_op jit(solution)/shard_map/ppermute | solution.py:25
  377.6 2.7 copy-start
  382.8 26.4 %copy-start.1 = (f32[512,1024]{1,0:T(8,128)S(1)}, f32[512,1024]{1,0:T(8,128)}, u32[]{:S(2)}) copy-start(f32[512,1024]{1,0:T(8,128)} %get-tuple-element.118) | copy-start | bytes 6291460
  409.2 1.3 copy-start.5

commit v3 on v2

v3 whole, which is shorter than its diff:
```python
import functools

import jax
import jax.numpy as jnp
from jax import lax
from jax.experimental import pallas as pl
from jax.experimental.pallas import tpu as pltpu
from jax.sharding import PartitionSpec as P

HEAD_DIM = 64
HASH_ROWS = 500002
EPSILON = 1e-05
MASKED = -1e30
BF = jnp.bfloat16
F32 = jnp.float32
QB = 256
LANES = 256
STEPS = 4
VMEM_BYTES = 60 * 1024 * 1024
MESH = pl.DeviceIdType.MESH


def flip(x, axis, bits):
    count = lax.axis_size(axis)
    return lax.ppermute(x, axis, [(i, i ^ bits) for i in range(count)])


def dot(a, b):
    return lax.dot_general(a, b, (((1,), (0,)), ((), ())), preferred_element_type=F32)


def dot_nt(a, b):
    return lax.dot_general(a, b, (((1,), (1,)), ((), ())), preferred_element_type=F32)


def dot_tn(a, b):
    return lax.dot_general(a, b, (((0,), (0,)), ((), ())), preferred_element_type=F32)


def cost(flops, moved):
    return pl.CostEstimate(flops=flops, bytes_accessed=moved, transcendentals=0)


def params(**more):
    return pltpu.CompilerParams(vmem_limit_bytes=VMEM_BYTES, **more)


def whole(shape):
    return pl.BlockSpec(shape, lambda i, sc: (0,) * len(shape))


VM = pl.BlockSpec(memory_space=pltpu.VMEM)
ANY = pl.BlockSpec(memory_space=pl.ANY)


def places():
    me = lax.axis_index("tp")
    core = lax.rem(me, 2)
    sib = me + 1 - 2 * core
    far = lax.rem(me + 2, 4)
    return me, sib, far, lax.rem(sib + 2, 4), core


def push(src, dst, send, recv, where):
    return pltpu.make_async_remote_copy(
        src_ref=src,
        dst_ref=dst,
        send_sem=send,
        recv_sem=recv,
        device_id={"seq": where[0], "tp": where[1]},
        device_id_type=MESH,
    )


def greet(others):
    barrier = pltpu.get_barrier_semaphore()
    for seq, tp in others:
        pl.semaphore_signal(
            barrier, inc=1, device_id={"seq": seq, "tp": tp}, device_id_type=MESH
        )
    pl.semaphore_wait(barrier, len(others))


def each(body, count):
    lax.fori_loop(0, count, lambda k, c: (body(k), c)[1], 0)


def chunk(k, size):
    return pl.ds(pl.multiple_of(k * size, size), size)


def norm_rows(row_data, gain):
    scaling = lax.rsqrt(jnp.mean(row_data * row_data, axis=-1, keepdims=True) + EPSILON)
    return (row_data * scaling * gain, scaling)


def norm_back(row_data, scaling, gain, grad_norm):
    weighted = grad_norm * gain
    inner_mean = jnp.mean(weighted * row_data, axis=-1, keepdims=True)
    grad_rows = scaling * weighted - row_data * scaling * scaling * scaling * inner_mean
    grad_gain = jnp.sum(grad_norm * row_data * scaling, axis=0, keepdims=True)
    return (grad_rows, grad_gain)


def front_kernel(
    seq_count, tables, x_ref, gain_ref, w_ref, pair_ref, n_out, qkv_out, hash_ref,
    n_ref, qkv_ref, pack_ref, sum_ref, snd, rcv, psnd, prcv, loc,
):
    me, sib, far, farsib, core = places()
    seq = lax.axis_index("seq")
    near = seq + 1 - 2 * lax.rem(seq, 2)
    parity, place, half = lax.rem(seq, 2), seq // 2, seq_count // 2
    level = [lax.rem(seq + 2 * j, seq_count) for j in range(1, half)]
    greet([(seq, sib), (seq, far), (near, me)] + [(s, me) for s in level])
    rows = x_ref.shape[0]
    size = rows // STEPS

    pack_ref[parity, place, me] = pair_ref[core]
    mine = pack_ref.at[parity, place, me]
    stage_sib = push(pair_ref.at[1 - core], mine, psnd.at[0], prcv.at[0], (seq, sib))
    stage_sib.start()
    both = pack_ref.at[parity, place, pl.ds(me - core, 2)]
    stage_far = push(both, both, psnd.at[1], prcv.at[1], (seq, far))
    four = pack_ref.at[parity, place]
    stage_level = [
        push(four, four, psnd.at[2 + j], prcv.at[2 + j], (s, me)) for j, s in enumerate(level)
    ]
    plane = pack_ref.at[parity]
    stage_near = push(plane, plane, psnd.at[half + 1], prcv.at[half + 1], (near, me))

    def own(kind, k, to, block):
        part = n_ref.at[block, chunk(k, size)]
        return push(part, part, snd.at[kind, k], rcv.at[kind, k], (seq, to))

    for k in range(STEPS):
        part = slice(k * size, (k + 1) * size)
        normed, _ = norm_rows(x_ref[part].astype(F32), gain_ref[...])
        n_ref[me, part] = normed.astype(BF)
        if k == 0:
            stage_sib.wait_recv()
            stage_far.start()
        own(1, k, far, me).start()
        own(0, k, sib, me).start()

    width = w_ref.shape[2]

    def project(block, k, length):
        part = chunk(k, length)
        for c in range(3):
            qkv_ref[block, part, c * width : (c + 1) * width] = dot(
                n_ref[block, part], w_ref[c]
            ).astype(BF)

    def homes(block):
        return [
            pltpu.make_async_copy(n_ref.at[block], n_out.at[block], loc.at[0, block]),
            pltpu.make_async_copy(qkv_ref.at[block], qkv_out.at[block], loc.at[1, block]),
        ]

    each(lambda k: project(me, k, rows // 2), 2)
    for copy in homes(me):
        copy.start()
    stage_far.wait_recv()
    for copy in stage_level:
        copy.start()
    for k in range(STEPS):
        own(0, k, sib, me).wait_recv()
    each(lambda k: project(sib, k, rows // 2), 2)
    for copy in homes(sib):
        copy.start()

    def far_chunk(k):
        own(1, k, far, me).wait_recv()
        own(2, k, sib, far).start()
        project(far, k, size)

    def farsib_chunk(k):
        own(2, k, sib, far).wait_recv()
        project(farsib, k, size)

    far_chunk(0)
    for copy in stage_level:
        copy.wait_recv()
    stage_near.start()

    sum_ref[...] = jnp.zeros_like(sum_ref)
    high_rows = sum_ref.shape[1]
    first = seq * (high_rows * LANES)

    def sums(which):
        def body(b):
            for table in range(tables):
                line = lambda row: jnp.concatenate(
                    [pack_ref[which, b, t, row : row + 1] for t in range(4)], axis=1
                )
                ids = line(table).astype(jnp.int32) - first
                weights = line(table + tables)
                high = lax.broadcasted_iota(jnp.int32, (high_rows, 4 * rows), 0) == (ids >> 8)
                low = lax.broadcasted_iota(jnp.int32, (LANES, 4 * rows), 0) == (ids & (LANES - 1))
                high = jnp.where(high, 1.0, 0.0).astype(BF)
                low = jnp.where(low, weights, 0.0).astype(BF)
                sum_ref[table] += dot_nt(high, low)

        each(body, half)

    sums(parity)
    each(lambda k: far_chunk(k + 1), STEPS - 2)
    each(farsib_chunk, STEPS - 1)
    stage_near.wait_recv()
    sums(1 - parity)
    far_chunk(STEPS - 1)
    for copy in homes(far):
        copy.start()
    hash_ref[...] = sum_ref[...].astype(BF)
    farsib_chunk(STEPS - 1)
    for copy in homes(farsib):
        copy.start()
    for k in range(STEPS):
        for kind in range(3):
            own(kind, k, sib, me).wait_send()
    stage_sib.wait_send()
    stage_far.wait_send()
    for copy in stage_level:
        copy.wait_send()
    stage_near.wait_send()
    for block in (me, sib, far, farsib):
        for copy in homes(block):
            copy.wait()


def front_call(x, gain, w, pairs, high_rows):
    seq_count = lax.axis_size("seq")
    rows, model = x.shape
    width = w.shape[0] * w.shape[2]
    tables = 3
    half = seq_count // 2
    dma = pltpu.SemaphoreType.DMA
    return pl.pallas_call(
        functools.partial(front_kernel, seq_count, tables),
        in_specs=[VM] * 4,
        out_specs=[ANY] * 2 + [VM],
        out_shape=[
            jax.ShapeDtypeStruct((4, rows, model), BF),
            jax.ShapeDtypeStruct((4, rows, width), BF),
            jax.ShapeDtypeStruct((tables, high_rows, LANES), BF),
        ],
        scratch_shapes=[
            pltpu.VMEM((4, rows, model), BF),
            pltpu.VMEM((4, rows, width), BF),
            pltpu.VMEM((2, half, 4, 8, rows), F32),
            pltpu.VMEM((tables, high_rows, LANES), F32),
            dma((3, STEPS)),
            dma((3, STEPS)),
            dma((half + 2,)),
            dma((half + 2,)),
            dma((2, 4)),
        ],
        compiler_params=params(collective_id=0, has_side_effects=True),
        cost_estimate=cost(1_000_000, 1_000_000),
        name="front",
    )(x, gain, w, pairs)


def doc_bounds(sc, places):
    low = jnp.where(places >= sc[2], sc[2], jnp.where(places >= sc[1], sc[1], 0))
    end = jnp.where(places >= sc[2], sc[5], jnp.where(places >= sc[1], sc[4], sc[3]))
    return low, jnp.minimum(places, end - 1)


def head_rows(x, h):
    where = lax.broadcasted_iota(jnp.int32, x.shape, 0) // HEAD_DIM
    return jnp.where(where == h, x, jnp.zeros_like(x))


def attend_kernel(heads, sc, qkv_ref, heads_ref, lse_ref, vt_ref, qt_ref, acc_ref, score_ref):
    width = heads * HEAD_DIM
    step = pl.program_id(0)

    @pl.when(step == 0)
    def _():
        for n in range(qkv_ref.shape[0] // QB):
            vt_ref[:, n * QB : (n + 1) * QB] = qkv_ref[n * QB : (n + 1) * QB, 2 * width :].T

    start = pl.multiple_of(step * QB, QB)
    q_t = qkv_ref[pl.ds(start, QB), :width].T * jnp.asarray(HEAD_DIM**-0.5, BF)
    for h in range(heads):
        qt_ref[:, h * QB : (h + 1) * QB] = head_rows(q_t, h)
    acc_ref[...] = jnp.zeros_like(acc_ref)
    places = start + lax.broadcasted_iota(jnp.int32, (1, QB), 1)
    low, high = doc_bounds(sc, places)
    low_first, _ = doc_bounds(sc, start)

    def body(kb, state):
        at = pl.multiple_of(kb * QB, QB)
        keys = qkv_ref[pl.ds(at, QB), width : 2 * width]
        value_t = vt_ref[:, pl.ds(at, QB)]
        spot = at + lax.broadcasted_iota(jnp.int32, (QB, QB), 0)
        allowed = (spot >= low) & (spot <= high)
        score_ref[...] = dot(keys, qt_ref[...])
        fresh = []
        for h in range(heads):
            top, total = state[h]
            scores = jnp.where(allowed, score_ref[:, h * QB : (h + 1) * QB], MASKED)
            new_top = jnp.maximum(top, jnp.max(scores, axis=0, keepdims=True))
            fade = jnp.exp(top - new_top)
            probs = jnp.exp(scores - new_top)
            total = total * fade + jnp.sum(probs, axis=0, keepdims=True)
            part = slice(h * HEAD_DIM, (h + 1) * HEAD_DIM)
            acc_ref[part] = acc_ref[part] * fade + dot(value_t[part], probs.astype(BF))
            fresh.append((new_top, total))
        return tuple(fresh)

    begin = tuple(
        (jnp.full((1, QB), MASKED, F32), jnp.zeros((1, QB), F32)) for _ in range(heads)
    )
    state = lax.fori_loop(low_first // QB, start // QB + 1, body, begin)
    lse_ref[...] = jnp.zeros_like(lse_ref)
    for h in range(heads):
        top, total = state[h]
        part = slice(h * HEAD_DIM, (h + 1) * HEAD_DIM)
        acc_ref[part] = acc_ref[part] * (1.0 / total)
        lse_ref[h : h + 1] = top + jnp.log(total)
    heads_ref[...] = acc_ref[...].T.astype(BF)


def attend_call(sc, qkv):
    rows, width = qkv.shape[0], qkv.shape[1] // 3
    heads = width // HEAD_DIM
    return pl.pallas_call(
        functools.partial(attend_kernel, heads),
        grid_spec=pltpu.PrefetchScalarGridSpec(
            num_scalar_prefetch=1,
            grid=(rows // QB,),
            in_specs=[whole(qkv.shape)],
            out_specs=[
                pl.BlockSpec((QB, width), lambda i, sc: (i, 0)),
                pl.BlockSpec((8, QB), lambda i, sc: (0, i)),
            ],
            scratch_shapes=[
                pltpu.VMEM((width, rows), BF),
                pltpu.VMEM((width, heads * QB), BF),
                pltpu.VMEM((width, QB), F32),
                pltpu.VMEM((QB, heads * QB), F32),
            ],
        ),
        out_shape=[
            jax.ShapeDtypeStruct((rows, width), BF),
            jax.ShapeDtypeStruct((8, rows), F32),
        ],
        compiler_params=params(),
        cost_estimate=cost(60_000_000_000, 8_000_000),
        name="attend",
    )(sc, qkv)


def attend_back_kernel(
    heads, sc, grad_ref, wo_ref, qkv_ref, heads_ref, lse_ref, mixed_ref,
    kt_ref, qt_ref, gt_ref, qs_ref, gs_ref, dqt_ref, dk_ref, dv_ref, score_ref, prob_ref,
):
    width = heads * HEAD_DIM
    step = pl.program_id(0)
    rows = qkv_ref.shape[0]

    @pl.when(step == 0)
    def _():
        for n in range(rows // QB):
            kt_ref[:, n * QB : (n + 1) * QB] = qkv_ref[n * QB : (n + 1) * QB, width : 2 * width].T
        dk_ref[...] = jnp.zeros_like(dk_ref)
        dv_ref[...] = jnp.zeros_like(dv_ref)

    start = pl.multiple_of(step * QB, QB)
    grad = dot(grad_ref[...], wo_ref[...]).astype(BF)
    grad_t = grad.T
    out_t = heads_ref[...].T
    product = grad_t.astype(F32) * out_t.astype(F32)
    query = qkv_ref[pl.ds(start, QB), :width] * jnp.asarray(HEAD_DIM**-0.5, BF)
    q_t = query.T
    inner = []
    for h in range(heads):
        part = slice(h * HEAD_DIM, (h + 1) * HEAD_DIM)
        inner.append(jnp.sum(product[part], axis=0, keepdims=True))
        qt_ref[:, h * QB : (h + 1) * QB] = head_rows(q_t, h)
        gt_ref[:, h * QB : (h + 1) * QB] = head_rows(grad_t, h)
    qs_ref[...] = q_t
    gs_ref[...] = grad_t
    dqt_ref[...] = jnp.zeros_like(dqt_ref)
    places = start + lax.broadcasted_iota(jnp.int32, (1, QB), 1)
    low, high = doc_bounds(sc, places)
    low_first, _ = doc_bounds(sc, start)

    def body(kb, carry):
        at = pl.multiple_of(kb * QB, QB)
        keys = qkv_ref[pl.ds(at, QB), width : 2 * width]
        values = qkv_ref[pl.ds(at, QB), 2 * width :]
        spot = at + lax.broadcasted_iota(jnp.int32, (QB, QB), 0)
        allowed = (spot >= low) & (spot <= high)
        score_ref[...] = dot(keys, qt_ref[...])
        prob_ref[...] = dot(values, gt_ref[...])
        for h in range(heads):
            part = slice(h * HEAD_DIM, (h + 1) * HEAD_DIM)
            lanes = slice(h * QB, (h + 1) * QB)
            scores = jnp.where(allowed, score_ref[:, lanes], MASKED)
            probs = jnp.exp(scores - lse_ref[h : h + 1])
            grad_scores = (probs * (prob_ref[:, lanes] - inner[h])).astype(BF)
            dqt_ref[part] += dot(kt_ref[part, pl.ds(at, QB)], grad_scores)
            dv_ref[part, pl.ds(at, QB)] += dot_nt(gs_ref[part], probs.astype(BF))
            dk_ref[part, pl.ds(at, QB)] += dot_nt(qs_ref[part], grad_scores)
        return carry

    lax.fori_loop(low_first // QB, start // QB + 1, body, 0)
    dq = (dqt_ref[...] * HEAD_DIM**-0.5).T.astype(BF)
    mixed_ref[pl.ds(start, QB), :width] = dq

    @pl.when(step == pl.num_programs(0) - 1)
    def _():
        for n in range(rows // QB):
            part = slice(n * QB, (n + 1) * QB)
            mixed_ref[part, width : 2 * width] = dk_ref[:, part].T.astype(BF)
            mixed_ref[part, 2 * width :] = dv_ref[:, part].T.astype(BF)


def attend_back_call(sc, grad, wo, qkv, heads_out, lse):
    rows, width = qkv.shape[0], qkv.shape[1] // 3
    heads = width // HEAD_DIM
    model = wo.shape[0]
    return pl.pallas_call(
        functools.partial(attend_back_kernel, heads),
        grid_spec=pltpu.PrefetchScalarGridSpec(
            num_scalar_prefetch=1,
            grid=(rows // QB,),
            in_specs=[
                pl.BlockSpec((QB, model), lambda i, sc: (i, 0)),
                whole(wo.shape),
                whole(qkv.shape),
                pl.BlockSpec((QB, width), lambda i, sc: (i, 0)),
                pl.BlockSpec((8, QB), lambda i, sc: (0, i)),
            ],
            out_specs=whole((rows, 3 * width)),
            scratch_shapes=[
                pltpu.VMEM((width, rows), BF),
                pltpu.VMEM((width, heads * QB), BF),
                pltpu.VMEM((width, heads * QB), BF),
                pltpu.VMEM((width, QB), BF),
                pltpu.VMEM((width, QB), BF),
                pltpu.VMEM((width, QB), F32),
                pltpu.VMEM((width, rows), F32),
                pltpu.VMEM((width, rows), F32),
                pltpu.VMEM((QB, heads * QB), F32),
                pltpu.VMEM((QB, heads * QB), F32),
            ],
        ),
        out_shape=jax.ShapeDtypeStruct((rows, 3 * width), BF),
        compiler_params=params(),
        cost_estimate=cost(90_000_000_000, 12_000_000),
        name="attend_back",
    )(sc, grad, wo, qkv, heads_out, lse)


def middle_kernel(
    seq_count, heads_ref, wo_ref, x_ref, gain_ref, c0, c2, wg_in, wu_in, wd_in, table_in, *refs
):
    half = seq_count // 2
    rest_ref, fardown_ref, grad_ref, gain_out, keep_out, send_out, branch_ref, table_ref = refs[:8]
    piece_refs, refs = refs[8 : 8 + half], refs[8 + half :]
    (
        c1, c3, n_ref, wg_ref, wu_ref, wd_ref, act_ref, gg_ref, gu_ref,
        g0_ref, g1s_ref, g1r_ref, d0_ref, d1s_ref, d1r_ref,
        as_ref, ar_ref, ys_ref, yr_ref, bs_ref, br_ref, gb_ref,
        stay_ref, away_ref, got_ref, up_ref, upgot_ref,
        snd, rcv, xsnd, xrcv, zsnd, zrcv, tsnd, trcv, loc, wloc,
    ) = refs
    me, sib, far, farsib, core = places()
    seq = lax.axis_index("seq")
    parity, place = lax.rem(seq, 2), seq // 2
    near = seq + 1 - 2 * parity
    level = [lax.rem(seq + 2 * j, seq_count) for j in range(1, half)]

    loads = [
        pltpu.make_async_copy(w_in, w_ref.at[: w_in.shape[0]], wloc.at[n])
        for n, (w_in, w_ref) in enumerate(((wg_in, wg_ref), (wu_in, wu_ref), (wd_in, wd_ref)))
    ]
    for load in loads:
        load.start()
    greet([(seq, sib), (seq, far), (near, me)] + [(s, me) for s in level])
    rows, model = x_ref.shape
    size = rows // STEPS
    units = wg_in.shape[0]
    long = rows // 2
    kinds = iter(range(100))

    def maker(src, dst, to, length=size):
        kind = next(kinds)

        def made(k):
            part = chunk(k, length)
            return push(src.at[part], dst.at[part], snd.at[kind, k], rcv.at[kind, k], (seq, to))

        return made

    proj_a = maker(as_ref, ar_ref, sib)
    proj_y = maker(ys_ref, yr_ref, far)
    proj_b = maker(bs_ref, br_ref, sib)
    two_sib = maker(n_ref.at[me], n_ref.at[me], sib)
    two_far = maker(n_ref.at[me], n_ref.at[me], far)
    two_on = maker(n_ref.at[far], n_ref.at[far], sib)
    back_one = maker(g1s_ref, g1r_ref, sib, long)
    down_one = maker(d1s_ref, d1r_ref, sib, long)
    back_a = maker(as_ref, ar_ref, sib, long)
    back_y = maker(ys_ref, yr_ref, far)
    down_three = maker(bs_ref, br_ref, sib, long)
    branch_sib = maker(gb_ref, branch_ref.at[me], sib)
    branch_far = maker(gb_ref, branch_ref.at[me], far)
    branch_on = maker(branch_ref.at[far], branch_ref.at[far], sib)
    cot_one = maker(c0, c1, sib, long)
    cot_three = maker(c2, c3, sib, long)

    def branch_home(k):
        part = chunk(k, size)
        return pltpu.make_async_copy(gb_ref.at[part], branch_ref.at[me, part], loc.at[k])

    table_home = pltpu.make_async_copy(table_in, table_ref.at[parity, place, core], wloc.at[3])

    def table_level(j):
        return push(
            table_in, table_ref.at[parity, place, core], tsnd.at[0, j], trcv.at[0, j], (level[j - 1], me)
        )

    def table_near(j):
        spot = table_ref.at[parity, lax.rem(place + half - j, half), core]
        return push(table_in if j == 0 else spot, spot, tsnd.at[1, j], trcv.at[1, j], (near, me))

    def table_sib(same, j):
        which = parity if same else 1 - parity
        spot = table_ref.at[which, lax.rem(place + half - j, half), core]
        kind = 2 if same else 3
        src = table_in if same and j == 0 else spot
        return push(src, spot, tsnd.at[kind, j], trcv.at[kind, j], (seq, sib))

    table_home.start()
    for j in range(1, half):
        table_level(j).start()
    table_near(0).start()
    table_sib(True, 0).start()
    for k in range(2):
        cot_one(k).start()
        cot_three(k).start()

    def project(block, k):
        return dot_nt(heads_ref[block, chunk(k, size)], wo_ref[...])

    def send_three(k):
        as_ref[chunk(k, size)] = project(farsib, k).astype(BF)
        proj_a(k).start()

    def send_two(k):
        part = project(far, k)
        proj_a(k).wait_recv()
        ys_ref[chunk(k, size)] = (part + ar_ref[chunk(k, size)].astype(F32)).astype(BF)
        proj_y(k).start()

    def send_one(k):
        bs_ref[chunk(k, size)] = project(sib, k).astype(BF)
        proj_b(k).start()

    each(send_three, STEPS)
    each(send_two, STEPS)
    each(send_one, STEPS)
    wide = act_ref.shape[0]
    if wide > units:
        for ref in (act_ref, gg_ref, gu_ref, wg_ref, wu_ref, wd_ref):
            ref[units:] = jnp.zeros((wide - units, ref.shape[1]), BF)
    for load in loads:
        load.wait()
    for k in range(2):
        cot_one(k).wait_recv()
        cot_three(k).wait_recv()

    def feed(m, block_a, block_b, ca, cb):
        part = chunk(m, long)
        normed = jnp.concatenate([n_ref[block_a, part], n_ref[block_b, part]], axis=0)
        cot = jnp.concatenate([ca[part], cb[part]], axis=0)
        gate = dot_nt(wg_ref[:units], normed)
        up = dot_nt(wu_ref[:units], normed)
        sig = jax.nn.sigmoid(gate)
        silu = gate * sig
        act = (silu * up).astype(BF)
        grad_act = dot_nt(wd_ref[:units], cot)
        grad_gate = (grad_act * up * sig * (1.0 + gate * (1.0 - sig))).astype(BF)
        grad_up = (grad_act * silu).astype(BF)
        lanes = [
            pl.ds(pl.multiple_of(block * rows + m * long, long), long) for block in (block_a, block_b)
        ]
        for ref, value in ((act_ref, act), (gg_ref, grad_gate), (gu_ref, grad_up)):
            ref[:units, lanes[0]] = value[:, :long]
            ref[:units, lanes[1]] = value[:, long:]
        pair = lambda ref: jnp.concatenate([ref[:, lanes[0]], ref[:, lanes[1]]], axis=1)
        back = dot_tn(pair(gg_ref), wg_ref[...]) + dot_tn(pair(gu_ref), wu_ref[...])
        return back, dot_tn(pair(act_ref), wd_ref[...])

    def own_chunk(k):
        part = chunk(k, size)
        total = x_ref[part].astype(F32) + project(me, k)
        proj_b(k).wait_recv()
        proj_y(k).wait_recv()
        hidden = total + br_ref[part].astype(F32) + yr_ref[part].astype(F32)
        rest_ref[part] = hidden
        normed, _ = norm_rows(hidden, gain_ref[...])
        n_ref[me, part] = normed.astype(BF)
        two_far(k).start()
        two_sib(k).start()

    def own_half(m):
        own_chunk(2 * m)
        own_chunk(2 * m + 1)
        two_sib(2 * m).wait_recv()
        two_sib(2 * m + 1).wait_recv()
        part = chunk(m, long)
        back, down = feed(m, me, sib, c0, c1)
        g0_ref[part] = back[:long].astype(BF)
        g1s_ref[part] = back[long:].astype(BF)
        back_one(m).start()
        d0_ref[part] = down[:long].astype(BF)
        d1s_ref[part] = down[long:].astype(BF)
        down_one(m).start()

    each(own_half, 2)
    for j in range(1, half):
        table_level(j).wait_recv()
        table_near(j).start()
        table_sib(True, j).start()

    def settle(k):
        proj_a(k).wait_send()
        proj_y(k).wait_send()
        proj_b(k).wait_send()

    each(settle, STEPS)

    def far_sum(k):
        part = chunk(k, size)
        ys_ref[part] = (ys_ref[part].astype(F32) + ar_ref[part].astype(F32)).astype(BF)
        back_y(k).start()

    def far_half(m):
        for k in (2 * m, 2 * m + 1):
            two_far(k).wait_recv()
            two_on(k).start()
        for k in (2 * m, 2 * m + 1):
            two_on(k).wait_recv()
        part = chunk(m, long)
        back, down = feed(m, far, farsib, c2, c3)
        as_ref[part] = back[long:].astype(BF)
        back_a(m).start()
        ys_ref[part] = back[:long].astype(BF)
        bs_ref[part] = down[long:].astype(BF)
        down_three(m).start()
        fardown_ref[part] = down[:long].astype(BF)
        back_a(m).wait_recv()
        far_sum(2 * m)
        far_sum(2 * m + 1)

    each(far_half, 2)
    for j in range(half):
        table_near(j).wait_recv()
        table_sib(False, j).start()

    piece = model // seq_count
    span = model // STEPS
    per = half // STEPS
    upright = piece % 128 == 0

    def weight_away(w, b):
        return push(
            away_ref.at[w, b], got_ref.at[w, b], xsnd.at[w, b], xrcv.at[w, b], (near, me)
        )

    def up_away(j):
        b = lax.rem(place + j, half)
        return push(
            up_ref.at[b], upgot_ref.at[j - 1], zsnd.at[j], zrcv.at[j],
            (lax.rem(seq + 2 * j, seq_count), me),
        )

    def weight_tile(w, k):
        cots = (c0, c1, c2, c3)
        order = (me, sib, far, farsib)
        left = (act_ref, gg_ref, gu_ref)[w]
        total = None
        for r in range(4):
            cols = chunk(k, span)
            right = cots[r][:, cols] if w == 0 else n_ref[order[r], :, cols]
            lanes = pl.ds(pl.multiple_of(order[r] * rows, rows), rows)
            term = dot(left[:units, lanes], right)
            total = term if total is None else total + term
        return total.astype(BF)

    def weights_step(kk):
        k = lax.rem(place // per + 1 + kk, STEPS)
        for w in range(3):
            tile = weight_tile(w, k)
            tile = tile if upright else tile.T
            for n in range(per):
                b = k * per + n
                take = lambda i: slice(i * piece, (i + 1) * piece)
                even = tile[:, take(2 * n)] if upright else tile[take(2 * n)]
                odd = tile[:, take(2 * n + 1)] if upright else tile[take(2 * n + 1)]
                if w == 2:
                    up_ref[b, 0] = even
                    up_ref[b, 1] = odd

                    @pl.when(b != place)
                    def _():
                        up_away(lax.rem(b + half - place, half)).start()
                else:

                    @pl.when(parity == 0)
                    def _():
                        stay_ref[w, b] = even
                        away_ref[w, b] = odd

                    @pl.when(parity == 1)
                    def _():
                        stay_ref[w, b] = odd
                        away_ref[w, b] = even

                    weight_away(w, b).start()

    gain_out[...] = jnp.zeros_like(gain_out)

    def back_chunk(k):
        weights_step(k)
        part = chunk(k, size)
        back_y(k).wait_recv()
        grad_norm = g0_ref[part].astype(F32) + g1r_ref[part].astype(F32) + yr_ref[part].astype(F32)
        hidden = rest_ref[part]
        _, scaling = norm_rows(hidden, gain_ref[...])
        grad_rows, grad_gain = norm_back(hidden, scaling, gain_ref[...], grad_norm)
        grad = c0[part].astype(F32) + grad_rows
        grad_ref[part] = grad
        gain_out[...] += grad_gain
        gb_ref[part] = grad.astype(BF)
        branch_far(k).start()
        branch_sib(k).start()
        branch_home(k).start()

    for m in range(2):
        back_one(m).wait_recv()
    each(back_chunk, STEPS)

    for m in range(2):
        down_one(m).wait_recv()
        down_three(m).wait_recv()

    def finish(k):
        part = chunk(k, size)
        rest_ref[part] += d0_ref[part].astype(F32) + d1r_ref[part].astype(F32)
        fardown_ref[part] = (fardown_ref[part].astype(F32) + br_ref[part].astype(F32)).astype(BF)
        branch_far(k).wait_recv()
        branch_on(k).start()

    each(finish, STEPS)

    for j in range(half):
        b = lax.rem(place + j, half)
        for w in range(2):
            weight_away(w, b).wait_recv()
            piece_refs[j][w] = (stay_ref[w, b].astype(F32) + got_ref[w, b].astype(F32)).astype(BF)

    def up_sum(which):
        total = up_ref[place, which].astype(F32)
        for j in range(1, half):
            total = total + upgot_ref[j - 1, which].astype(F32)
        return total.astype(BF)

    for j in range(1, half):
        up_away(j).wait_recv()
    keep_out[...] = up_sum(parity)
    send_out[...] = up_sum(1 - parity)

    def close(k):
        branch_sib(k).wait_recv()
        branch_on(k).wait_recv()
        branch_home(k).wait()
        for made in (two_sib, two_far, two_on, back_y, branch_sib, branch_far, branch_on):
            made(k).wait_send()

    each(close, STEPS)
    for m in range(2):
        for made in (back_one, down_one, back_a, down_three, cot_one, cot_three):
            made(m).wait_send()
    table_home.wait()
    for j in range(half):
        table_sib(True, j).wait_recv()
        table_sib(False, j).wait_recv()
        table_near(j).wait_send()
        table_sib(True, j).wait_send()
        table_sib(False, j).wait_send()
        for w in range(2):
            weight_away(w, j).wait_send()
    for j in range(1, half):
        table_level(j).wait_send()
        up_away(j).wait_send()


def middle_call(heads_out, wo, x, gain, cot, cot_far, weights, tables):
    seq_count = lax.axis_size("seq")
    rows, model = x.shape
    half = seq_count // 2
    piece = model // seq_count
    units = weights[0].shape[0]
    wide = units + -units % 256
    block = (units, piece) if piece % 128 == 0 else (piece, units)
    dma = pltpu.SemaphoreType.DMA
    shape = jax.ShapeDtypeStruct
    vm = pltpu.VMEM
    rows_bf = vm((rows, model), BF)
    return pl.pallas_call(
        functools.partial(middle_kernel, seq_count),
        in_specs=[VM] * 6 + [ANY] * 4,
        out_specs=[VM] * 6 + [ANY] * 2 + [VM] * half,
        out_shape=[
            shape((rows, model), F32),
            shape((rows, model), BF),
            shape((rows, model), F32),
            shape((1, model), F32),
            shape(block, BF),
            shape(block, BF),
            shape((4, rows, model), BF),
            shape((2, half, 2) + tables.shape, BF),
        ]
        + [shape((2,) + block, BF)] * half,
        scratch_shapes=[rows_bf, rows_bf, vm((4, rows, model), BF)]
        + [vm((wide, model), BF)] * 3
        + [vm((wide, 4 * rows), BF)] * 3
        + [rows_bf] * 13
        + [vm((2, half) + block, BF)] * 3
        + [vm((half, 2) + block, BF), vm((half - 1, 2) + block, BF)]
        + [dma((16, STEPS))] * 2
        + [dma((2, half))] * 2
        + [dma((half,))] * 2
        + [dma((4, half))] * 2
        + [dma((STEPS,)), dma((4,))],
        compiler_params=params(collective_id=1, has_side_effects=True),
        cost_estimate=cost(100_000_000_000, 30_000_000),
        name="middle",
    )(heads_out, wo, x, gain, cot, cot_far, *weights, tables)


def last_kernel(
    seq_count, mixed_in, w_in, x_in, gain_ref, grad_in, n_in, heads_in, branch_in, gain_in,
    out_ref, wqkv_ref, wout_ref, gains_ref,
    mixed_ref, w_ref, x_ref, grad_ref, n_ref, heads_ref, branch_ref,
    as_ref, ar_ref, ys_ref, yr_ref, bs_ref, br_ref, dw_ref, got_ref, sum_ref, zr_ref, gs_ref, gr_ref,
    snd, rcv, xsnd, xrcv, zsnd, zrcv, gsnd, grcv, loc,
):
    me, sib, far, farsib, core = places()
    seq = lax.axis_index("seq")
    parity, place, half = lax.rem(seq, 2), seq // 2, seq_count // 2
    near = seq + 1 - 2 * parity
    level = [lax.rem(seq + 2 * j, seq_count) for j in range(1, half)]
    loads = [
        pltpu.make_async_copy(src, dst, loc.at[n])
        for n, (src, dst) in enumerate(
            (
                (mixed_in, mixed_ref), (w_in, w_ref), (n_in, n_ref), (branch_in, branch_ref),
                (heads_in, heads_ref), (x_in, x_ref), (grad_in, grad_ref),
            )
        )
    ]
    for load in loads:
        load.start()
    greet([(seq, sib), (seq, far), (near, me)] + [(s, me) for s in level])
    rows, model = x_ref.shape
    size = rows // STEPS
    piece = model // seq_count
    wide = mixed_ref.shape[-1]

    def copy(kind, k, src, dst, to):
        return push(
            src.at[chunk(k, size)], dst.at[chunk(k, size)], snd.at[kind, k], rcv.at[kind, k], (seq, to)
        )

    back_a = lambda k: copy(0, k, as_ref, ar_ref, sib)
    back_y = lambda k: copy(1, k, ys_ref, yr_ref, far)
    back_b = lambda k: copy(2, k, bs_ref, br_ref, sib)

    def near_copy(b):
        return push(dw_ref.at[1, b], got_ref.at[b], xsnd.at[b], xrcv.at[b], (near, me))

    def level_copy(j):
        b = lax.rem(place + j, half)
        return push(
            sum_ref.at[b], zr_ref.at[j], zsnd.at[j], zrcv.at[j], (lax.rem(seq + 2 * j, seq_count), me)
        )

    width = w_ref.shape[2]

    def project(block, k):
        part = chunk(k, size)
        terms = [
            dot_nt(mixed_ref[block, part, c * width : (c + 1) * width], w_ref[c]) for c in range(3)
        ]
        return terms[0] + terms[1] + terms[2]

    def send_three(k):
        as_ref[chunk(k, size)] = project(farsib, k).astype(BF)
        back_a(k).start()

    def send_two(k):
        part = project(far, k)
        back_a(k).wait_recv()
        ys_ref[chunk(k, size)] = (part + ar_ref[chunk(k, size)].astype(F32)).astype(BF)
        back_y(k).start()

    def send_one(k):
        bs_ref[chunk(k, size)] = project(sib, k).astype(BF)
        back_b(k).start()

    span = model // STEPS
    per = half // STEPS

    def weights_step(kk):
        k = lax.rem(place // per + 1 + kk, STEPS)
        cols = chunk(k, span)
        to_qkv, to_out = None, None
        for r in range(4):
            term = dot_tn(n_ref[r, :, cols], mixed_ref[r])
            to_qkv = term if to_qkv is None else to_qkv + term
            term = dot_tn(branch_ref[r, :, cols], heads_ref[r])
            to_out = term if to_out is None else to_out + term
        for ref_at, value in ((slice(0, wide), to_qkv), (slice(wide, None), to_out)):
            tile = value.astype(BF).reshape(per, 2, piece, value.shape[1])
            for j in range(per):
                b = k * per + j

                @pl.when(parity == 0)
                def _():
                    dw_ref[0, b, :, ref_at] = tile[j, 0]
                    dw_ref[1, b, :, ref_at] = tile[j, 1]

                @pl.when(parity == 1)
                def _():
                    dw_ref[0, b, :, ref_at] = tile[j, 1]
                    dw_ref[1, b, :, ref_at] = tile[j, 0]

        for j in range(per):
            near_copy(k * per + j).start()

    for load in loads[:2]:
        load.wait()
    each(send_three, STEPS)
    each(send_two, STEPS)
    for load in loads[2:5]:
        load.wait()
    each(weights_step, STEPS)
    each(send_one, STEPS)
    for load in loads[5:]:
        load.wait()

    gs_ref[...] = jnp.zeros_like(gs_ref)

    def own_chunk(k):
        part = chunk(k, size)
        total = project(me, k)
        x = x_ref[part].astype(F32)
        _, scaling = norm_rows(x, gain_ref[...])
        back_b(k).wait_recv()
        back_y(k).wait_recv()
        grad_norm = total + br_ref[part].astype(F32) + yr_ref[part].astype(F32)
        grad_rows, grad_gain = norm_back(x, scaling, gain_ref[...], grad_norm)
        out_ref[part] = grad_ref[part] + grad_rows
        gs_ref[0, 0:1] += grad_gain

    def near_sum(b):
        near_copy(b).wait_recv()
        sum_ref[b] = (dw_ref[0, b].astype(F32) + got_ref[b].astype(F32)).astype(BF)

        @pl.when(b != place)
        def _():
            level_copy(lax.rem(b + half - place, half)).start()

    def both(kk):
        k = lax.rem(place // per + 1 + kk, STEPS)
        own_chunk(kk)
        for n in range(per):
            near_sum(k * per + n)

    each(both, STEPS)

    gs_ref[0, 1:2] = gain_in[...]
    others = [(seq, sib), (seq, far), (near, me)]

    def gain_copy(n, slot, to):
        return push(gs_ref.at[n], gr_ref.at[slot], gsnd.at[slot], grcv.at[slot], to)

    for n, to in enumerate(others):
        gain_copy(n, n, to).start()
        gain_copy(n, n, to).wait_recv()
        gs_ref[n + 1] = gs_ref[n] + gr_ref[n]
    for j in range(1, half):
        gain_copy(3, 2 + j, (level[j - 1], me)).start()
    gains = gs_ref[3]
    for j in range(1, half):
        gain_copy(3, 2 + j, (level[j - 1], me)).wait_recv()
        gains = gains + gr_ref[2 + j]
    gains_ref[...] = gains

    total = sum_ref[place].astype(F32)
    for j in range(1, half):
        level_copy(j).wait_recv()
        total = total + zr_ref[j].astype(F32)
    for c in range(3):
        wqkv_ref[c] = total[:, c * width : (c + 1) * width]
    wout_ref[...] = total[:, wide:]

    def close(k):
        for made in (back_a, back_y, back_b):
            made(k).wait_send()

    each(close, STEPS)
    each(lambda b: near_copy(b).wait_send(), half)
    for n, to in enumerate(others):
        gain_copy(n, n, to).wait_send()
    for j in range(1, half):
        gain_copy(3, 2 + j, (level[j - 1], me)).wait_send()
        level_copy(j).wait_send()


def last_call(mixed, w, x, gain, grad, normed, heads_out, branch, gain_two):
    seq_count = lax.axis_size("seq")
    rows, model = x.shape
    half = seq_count // 2
    piece = model // seq_count
    wide, width = mixed.shape[-1], heads_out.shape[-1]
    dma = pltpu.SemaphoreType.DMA
    shape = jax.ShapeDtypeStruct
    rows_bf = pltpu.VMEM((rows, model), BF)
    pieces = pltpu.VMEM((half, piece, wide + width), BF)
    return pl.pallas_call(
        functools.partial(last_kernel, seq_count),
        in_specs=[ANY] * 3 + [VM] + [ANY] * 4 + [VM],
        out_specs=[VM] * 4,
        out_shape=[
            shape((rows, model), F32),
            shape((3, piece, width), F32),
            shape((piece, width), F32),
            shape((8, model), F32),
        ],
        scratch_shapes=[
            pltpu.VMEM(a.shape, a.dtype) for a in (mixed, w, x, grad, normed, heads_out, branch)
        ]
        + [rows_bf] * 6
        + [pltpu.VMEM((2, half, piece, wide + width), BF), pieces, pieces, pieces]
        + [pltpu.VMEM((4, 8, model), F32), pltpu.VMEM((half + 2, 8, model), F32)]
        + [
            dma((3, STEPS)),
            dma((3, STEPS)),
            dma((half,)),
            dma((half,)),
            dma((half,)),
            dma((half,)),
            dma((half + 2,)),
            dma((half + 2,)),
            dma((7,)),
        ],
        compiler_params=params(collective_id=2, has_side_effects=True),
        cost_estimate=cost(1_000_000, 1_000_000),
        name="last",
    )(mixed, w, x, gain, grad, normed, heads_out, branch, gain_two)


def spread_kernel(in_ref, out_ref, flat_ref):
    tables, high_rows = in_ref.shape[2], in_ref.shape[3]
    for n in range(tables):
        for side in range(2):
            flat_ref[side, n * high_rows : (n + 1) * high_rows] = in_ref[
                0, 0, n, :, side * 128 : (side + 1) * 128
            ].astype(F32)

    def body(n, carry):
        for u in range(8):
            row = n * 8 + u
            for side in range(2):
                at = pl.multiple_of(row * LANES + side * 128, 128)
                out_ref[:, pl.ds(at, 128)] = flat_ref[side, pl.ds(row, tables, stride=high_rows)]
        return carry

    lax.fori_loop(0, high_rows // 8, body, 0)


def spread_call(tables, hash_rows):
    parities, half, count, high_rows, lanes = tables.shape
    return pl.pallas_call(
        spread_kernel,
        grid=(parities * half,),
        in_specs=[pl.BlockSpec((1, 1, count, high_rows, lanes), lambda i: (i % 2, i // 2, 0, 0, 0))],
        out_specs=pl.BlockSpec((count, high_rows * lanes), lambda i: (0, i)),
        out_shape=jax.ShapeDtypeStruct((count, hash_rows), F32),
        scratch_shapes=[pltpu.VMEM((2, count * high_rows, 128), F32)],
        compiler_params=params(),
        cost_estimate=cost(1_000_000, 24_000_000),
        name="hash_spread",
    )(tables)


def shards(
    latents_in,
    gain_one,
    w_qkv,
    w_out,
    gain_two,
    w_gate,
    w_up,
    w_down,
    cotangent,
    doc_lengths,
    valid_lengths,
    hash_ids,
    hash_weights,
):
    local_rows, model_width = latents_in.shape
    local_width = w_qkv.shape[2]
    group_rows = 4 * local_rows
    units = w_gate.shape[1]
    rank = lax.axis_index("tp")
    seq = lax.axis_index("seq")
    core = rank % 2
    seq_count = lax.axis_size("seq")
    lengths, valid = doc_lengths[0], valid_lengths[0]
    start_one = lengths[0]
    start_two = lengths[0] + lengths[1]
    sc = jnp.stack(
        [rank, start_one, start_two, valid[0], start_one + valid[1], start_two + valid[2]]
    ).astype(jnp.int32)
    gain_one, gain_two = gain_one[None], gain_two[None]

    tables = hash_ids.shape[0] // 2
    blank = jnp.zeros((8 - 2 * tables, local_rows), F32)
    pairs = jnp.stack(
        [
            jnp.concatenate(
                [
                    hash_ids[c * tables : (c + 1) * tables].astype(F32),
                    hash_weights[c * tables : (c + 1) * tables],
                    blank,
                ]
            )
            for c in range(2)
        ]
    )
    per_seq = -(-HASH_ROWS // seq_count)
    high_rows = -(-per_seq // (LANES * 8)) * 8

    qkv_weight = w_qkv.transpose(1, 0, 2)
    normed, qkv, sums = front_call(latents_in, gain_one, qkv_weight, pairs, high_rows)
    qkv, cotangent_late = lax.optimization_barrier((qkv, cotangent))
    qkv = qkv.reshape(group_rows, 3 * local_width)
    cot_far = flip(cotangent_late, "tp", 2)
    heads_out, lse = attend_call(sc, qkv)
    heads_four = heads_out.reshape(4, local_rows, local_width)
    (
        rest, far_down, grad_hidden, gain_two_part, up_keep, up_send, branch, hash_parts, *pieces
    ) = middle_call(
        heads_four, w_out, latents_in, gain_two, cotangent, cot_far,
        (w_gate.T, w_up.T, w_down.T), sums,
    )
    down_far = flip(far_down, "tp", 2)
    up_got = flip(up_send, "seq", 1)
    arrived = [
        lax.ppermute(pieces[j], "seq", [(s, (s + 2 * j) % seq_count) for s in range(seq_count)])
        for j in range(1, seq_count // 2)
    ]
    mixed = attend_back_call(
        sc, branch.reshape(group_rows, model_width), w_out, qkv, heads_out, lse
    )
    mixed, up_got, arrived, down_far = lax.optimization_barrier((mixed, up_got, arrived, down_far))
    hash_parts = hash_parts.reshape(2, seq_count // 2, 2 * tables, high_rows, LANES)
    hash_counts = spread_call(hash_parts, HASH_ROWS)
    grad_latents, qkv_total, out_total, gains = last_call(
        mixed.reshape(4, local_rows, -1), qkv_weight, latents_in, gain_one, grad_hidden,
        normed, heads_four, branch, gain_two_part,
    )
    total = pieces[0].astype(F32)
    for piece in arrived:
        total = total + piece.astype(F32)
    up_total = up_keep.astype(F32) + up_got.astype(F32)
    latents_out = (rest + down_far.astype(F32)).astype(BF)
    upright = lambda w: w.T if w.shape[0] == units else w
    return (
        latents_out,
        grad_latents,
        gains[0],
        qkv_total.transpose(1, 0, 2),
        out_total,
        gains[1],
        upright(total[1]),
        upright(up_total),
        upright(total[0]),
        hash_counts,
    )


def solution(mesh):
    in_specs = (
        P(("seq", "tp"), None),
        P(),
        P(None, None, "tp"),
        P(None, "tp"),
        P(),
        P(None, "tp"),
        P(None, "tp"),
        P(None, "tp"),
        P(("seq", "tp"), None),
        P("seq", None),
        P("seq", None),
        P(None, ("seq", "tp")),
        P(None, ("seq", "tp")),
    )
    out_specs = (
        P(("seq", "tp"), None),
        P(("seq", "tp"), None),
        P(),
        P("seq", None, "tp"),
        P("seq", "tp"),
        P(),
        P("seq", "tp"),
        P("seq", "tp"),
        P("seq", "tp"),
        P(),
    )
    return jax.shard_map(shards, mesh=mesh, in_specs=in_specs, out_specs=out_specs, check_vma=False)
```

time: 415 us -> 281 us (0.68)
  Pallas kernels: 326 us -> 253 us
  waiting for transfers between devices: 25.3 us -> 1.91 us
  local copies, waits for them, and re-layouts: 32.6 us -> 9.52 us
  other arithmetic: 10.6 us -> 3.83 us
    pallas_call x2, Pallas kernels: 93.6 us -> 62.3 us  [the longest x1 49.9 us: last_call(): pl.pallas_call(functools.partial(last_kernel, seq_count), in_specs=[ANY]...]
    ppermute x13 -> x3, waiting for transfers between devices: 25.3 us -> 1.9 us  [flip(): return lax.ppermute(x, axis, [(i, i ^ bits) for i in range(count)])]
    pallas_call x1, Pallas kernels: 52.3 us -> 37.6 us  [front_call(): pl.pallas_call(functools.partial(front_kernel, seq_count, tables), in_spe...]
    pallas_call x1, Pallas kernels: 28.9 us -> 17.3 us  [attend_call(): pl.pallas_call(functools.partial(attend_kernel, heads), grid_spec=pltpu.P...]
    ppermute x13 -> x3, starting transfers between devices: 12.1 us -> 1.63 us  [flip(): return lax.ppermute(x, axis, [(i, i ^ bits) for i in range(count)])]
    pallas_call x1, Pallas kernels: 117 us -> 109 us  [middle_call(): pl.pallas_call(functools.partial(middle_kernel, seq_count), in_specs=[VM]...]
    unnamed x31 -> x23, local copies, waits for them, and re-layouts: 12 us -> 3.73 us
    pallas_call x1, Pallas kernels: 34.4 us -> 27.4 us  [attend_back_call(): pl.pallas_call(functools.partial(attend_back_kernel, heads), grid_spec=pl...]
  transfers between devices with their start and end apart: 13 -> 6, of which waited for: 2 -> 1; matrix products, arithmetic and copies ran while one was open for 9% -> 1% of each run, Pallas kernels for 60% -> 20%
where the time goes in v3:
time: 281 us
  Pallas kernels  253 us (90%)
  local copies, waits for them, and re-layouts  9.52 us (3%)
  starting transfers between devices  8.18 us (3%)
  between operations  4 us (1%)
  other arithmetic  3.83 us (1%)
    pallas_call x1, Pallas kernels, middle_call(): pl.pallas_call(functools.partial(middle_kernel, seq_count), in_specs=[VM]...  109 us
    pallas_call x1, Pallas kernels, last_call(): pl.pallas_call(functools.partial(last_kernel, seq_count), in_specs=[ANY]...  49.9 us
    pallas_call x1, Pallas kernels, front_call(): pl.pallas_call(functools.partial(front_kernel, seq_count, tables), in_spe...  37.6 us
    pallas_call x1, Pallas kernels, attend_back_call(): pl.pallas_call(functools.partial(attend_back_kernel, heads), grid_spec=pl...  27.4 us
    pallas_call x1, Pallas kernels, attend_call(): pl.pallas_call(functools.partial(attend_kernel, heads), grid_spec=pltpu.P...  17.3 us
    pallas_call x1, Pallas kernels, spread_call(): pl.pallas_call(spread_kernel, grid=(parities * half,), in_specs=[pl.Block...  12.4 us
    ppermute x3, starting transfers between devices, shards(): lax.ppermute(pieces[j], 'seq', [(s, (s + 2 * j) % seq_count) for s in ran...  6.55 us
  transfers between devices with their start and end apart: 6, of which 1 were waited for; matrix products, arithmetic and copies ran while one was open for 1% of the time, Pallas kernels for 20%

profile of v3, /device:TPU:0, one launch (start us, length us, event | category | flops | bytes accessed | tf_op | source)
XLA Modules:
  0.0 280.6 jit_solution(10852846659961828260)
XLA Ops:
  0.7 0.8 slice_convert_fusion.1
  1.5 0.8 fusion.1
  2.5 0.6 pad_maximum_fusion.pair_ref
  3.1 37.6 %front.1 = (bf16[4,512,1024]{2,1,0:T(8,128)(2,1)}, bf16[4,512,768]{2,1,0:T(8,128)(2,1)}, bf16[3,248,256]{2,1,0:T(8,128)(2,1)}) custom-call(bf16[512,1024]{1,0:T(8,128)(2,1)} %x_in.1, f32[1,1024]{1,0:T(1,128)} %bitcast.42, bf16[3,1024,256]{2,1,0:T(8,128)(2,1)} %bitcast.34, f32[2,8,512]{2,1,0:T(8,128)} %pad_maximum_fusion.pair_ref), custom_call_target="tpu_custom_call" | custom-call | flops 1000000 | bytes 1000000 | tf_op jit(solution)/shard_map/front/pallas_call | solution.py:238
  40.7 0.6 collective-permute-start
  45.1 1.9 stack.28.sc
  47.0 17.3 %attend.1 = (bf16[2048,256]{1,0:T(8,128)(2,1)}, f32[8,2048]{1,0:T(8,128)}) custom-call(s32[6]{0:T(128)} %stack.28.sc, bf16[2048,768]{1,0:T(8,128)(2,1)} %bitcast.46), custom_call_target="tpu_custom_call" | custom-call | flops 60000002048 | bytes 8000000 | tf_op jit(solution)/shard_map/attend/pallas_call | solution.py:329
  64.3 1.9 collective-permute-done.c2
  66.2 1.0 copy-done.9
  67.2 108.5 %middle.1 = (f32[512,1024]{1,0:T(8,128)}, bf16[512,1024]{1,0:T(8,128)(2,1)}, f32[512,1024]{1,0:T(8,128)}, f32[1,1024]{1,0:T(1,128)}, bf16[704,128]{1,0:T(8,128)(...) custom-call(bf16[4,512,256]{2,1,0:T(8,128)(2,1)} %bitcast.39, ...), custom_call_target="tpu_custom_call" | custom-call | flops 99999997952 | bytes 30000000 | tf_op jit(solution)/shard_map/middle/pallas_call | solution.py:817
  175.8 0.6 collective-permute-start.1
  176.4 4.1 %collective-permute-start.2 = (bf16[2,704,128]{2,1,0:T(8,128)(2,1)}, bf16[2,704,128]{2,1,0:T(8,128)(2,1)S(1)}, u32[]{:S(2)}, u32[]{:S(2)}) collective-permute-start(bf16[2,704,128]{2,1,0:T(8,128)(2,1)} %get-tuple-element.48), channel_id=1, source_target_pairs={{0,8},{4,12},{8,16},{12,20},{16,24},{20,28},{24,0},{28,4},{1,9},{5... | collective-permute-start | bytes 1081352 | tf_op jit(solution)/shard_map/ppermute | solution.py:1170
  180.5 1.0 collective-permute-start.3
  181.5 1.4 collective-permute-start.4
  183.3 27.4 %attend_back.1 = bf16[2048,768]{1,0:T(8,128)(2,1)} custom-call(s32[6]{0:T(128)} %stack.28.sc, bf16[2048,1024]{1,0:T(8,128)(2,1)} %bitcast.37, bf16[1024,256]{1,0:T(8,128)(2,1)} %wo_ref.3, bf16[2048,768]{1,0:T(8,128)(2,1)} %bitcast.47, bf16[2048,256]{1,0:T(8,128)(2,1)} %get-tuple-element.41.heads_ref, f32[8,2048]{1,0:T(8,128)} %get-tuple-element.46.lse_ref), custom_call_target="tpu_custom_call" | custom-call | flops 89999998976 | bytes 12000000 | tf_op jit(solution)/shard_map/attend_back/pallas_call | solution.py:426
  210.8 12.4 %hash_spread.1 = f32[6,500002]{1,0:T(8,128)} custom-call(bf16[2,4,6,248,256]{4,3,2,1,0:T(8,128)(2,1)} %bitcast.36), custom_call_target="tpu_custom_call" | custom-call | flops 1000000 | bytes 24000000 | tf_op jit(solution)/shard_map/hash_spread/pallas_call | solution.py:1093
  223.2 49.9 %last.1 = (f32[512,1024]{1,0:T(8,128)}, f32[3,128,256]{2,1,0:T(8,128)}, f32[128,256]{1,0:T(8,128)}, f32[8,1024]{1,0:T(8,128)}) custom-call(bf16[4,512,768]{2,1,0:T(8,128)(2,1)} %bitcast.38, bf16[3,1024,256]{2,1,0:T(8,128)(2,1)} %bitcast.35, bf16[512,1024]{1,0:T(8,128)(2,1)} %x_in.1, f32[1,1024]{1,0:T(1,128)} %bitcast.43, ...), custom_call_target="tpu_custom_call" | custom-call | flops 1000000 | bytes 1000000 | tf_op jit(solution)/shard_map/last/pallas_call | solution.py:1039
  273.2 1.5 fusion
  274.9 0.9 slice_bitcast_fusion
  275.8 1.4 add_convert_fusion
  277.1 0.8 add_bitcast_fusion
  277.9 1.3 copy.26
  279.2 0.7 copy.27
  280.0 0.7 copy.28
  (30 shorter events, 1.4 us)
Async XLA Ops:
  0.6 40.0 %copy-start.8 = (bf16[512,1024]{1,0:T(8,128)(2,1)S(1)}, bf16[512,1024]{1,0:T(8,128)(2,1)}, u32[]{:S(2)}) copy-start(bf16[512,1024]{1,0:T(8,128)(2,1)} %c0.1) | copy-start | bytes 3145732
  0.7 40.6 %copy-start.6 = (s32[1,3]{1,0:T(1,128)S(1)}, s32[1,3]{1,0:T(1,128)}, u32[]{:S(2)}) copy-start(s32[1,3]{1,0:T(1,128)} %param.23) | copy-start | bytes 40
  0.7 40.6 %copy-start.7 = (s32[1,3]{1,0:T(1,128)S(1)}, s32[1,3]{1,0:T(1,128)}, u32[]{:S(2)}) copy-start(s32[1,3]{1,0:T(1,128)} %param.22) | copy-start | bytes 40
  40.7 25.6 %collective-permute-start = (bf16[512,1024]{1,0:T(8,128)(2,1)S(1)}, bf16[512,1024]{1,0:T(8,128)(2,1)S(1)}, u32[]{:S(2)}, u32[]{:S(2)}) collective-permute-start(bf16[512,1024]{1,0:T(8,128)(2,1)S(1)} %copy-done.8), channel_id=1, source_target_pairs={{0,2},{1,3},{2,0},{3,1},{4,6},{5,7},{6,4},{7,5},{8,10},{9,11},{10,... | collective-permute-start | bytes 3145736 | tf_op jit(solution)/shard_map/ppermute | solution.py:25
  66.2 1.0 copy-start.9
  175.8 47.4 %collective-permute-start.1 = (bf16[704,128]{1,0:T(8,128)(2,1)}, bf16[704,128]{1,0:T(8,128)(2,1)S(1)}, u32[]{:S(2)}, u32[]{:S(2)}) collective-permute-start(bf16[704,128]{1,0:T(8,128)(2,1)} %get-tuple-element.47), channel_id=1, source_target_pairs={{0,4},{4,0},{8,12},{12,8},{16,20},{20,16},{24,28},{28,24},{1,5},{5... | collective-permute-start | bytes 540680 | tf_op jit(solution)/shard_map/ppermute | solution.py:25
  176.4 46.8 %collective-permute-start.2 = (bf16[2,704,128]{2,1,0:T(8,128)(2,1)}, bf16[2,704,128]{2,1,0:T(8,128)(2,1)S(1)}, u32[]{:S(2)}, u32[]{:S(2)}) collective-permute-start(bf16[2,704,128]{2,1,0:T(8,128)(2,1)} %get-tuple-element.48), channel_id=1, source_target_pairs={{0,8},{4,12},{8,16},{12,20},{16,24},{20,28},{24,0},{28,4},{1,9},{5... | collective-permute-start | bytes 1081352 | tf_op jit(solution)/shard_map/ppermute | solution.py:1170
  180.5 42.6 %collective-permute-start.3 = (bf16[2,704,128]{2,1,0:T(8,128)(2,1)}, bf16[2,704,128]{2,1,0:T(8,128)(2,1)S(1)}, u32[]{:S(2)}, u32[]{:S(2)}) collective-permute-start(bf16[2,704,128]{2,1,0:T(8,128)(2,1)} %get-tuple-element.49), channel_id=1, source_target_pairs={{0,16},{4,20},{8,24},{12,28},{16,0},{20,4},{24,8},{28,12},{1,17},{... | collective-permute-start | bytes 1081352 | tf_op jit(solution)/shard_map/ppermute | solution.py:1170
  181.5 41.6 %collective-permute-start.4 = (bf16[2,704,128]{2,1,0:T(8,128)(2,1)}, bf16[2,704,128]{2,1,0:T(8,128)(2,1)S(1)}, u32[]{:S(2)}, u32[]{:S(2)}) collective-permute-start(bf16[2,704,128]{2,1,0:T(8,128)(2,1)} %get-tuple-element.50), channel_id=1, source_target_pairs={{0,24},{4,28},{8,0},{12,4},{16,8},{20,12},{24,16},{28,20},{1,25},{... | collective-permute-start | bytes 1081352 | tf_op jit(solution)/shard_map/ppermute | solution.py:1170
  182.9 40.2 %collective-permute-start.5 = (bf16[512,1024]{1,0:T(8,128)(2,1)}, bf16[512,1024]{1,0:T(8,128)(2,1)S(1)}, u32[]{:S(2)}, u32[]{:S(2)}) collective-permute-start(bf16[512,1024]{1,0:T(8,128)(2,1)} %get-tuple-element.51), channel_id=1, source_target_pairs={{0,2},{1,3},{2,0},{3,1},{4,6},{5,7},{6,4},{7,5},{8,10},{9,11},{10,... | collective-permute-start | bytes 3145736 | tf_op jit(solution)/shard_map/ppermute | solution.py:25
  223.2 51.5 %copy-start.3 = (bf16[2,704,128]{2,1,0:T(8,128)(2,1)S(1)}, bf16[2,704,128]{2,1,0:T(8,128)(2,1)}, u32[]{:S(2)}) copy-start(bf16[2,704,128]{2,1,0:T(8,128)(2,1)} %get-tuple-element.61) | copy-start | bytes 1081348
  273.1 2.6 copy-start
  275.8 1.4 copy-start.4
  275.8 2.1 copy-start.1
  277.9 1.3 copy-start.2
  277.9 2.1 copy-start.5

commit v4 on v3

--- a/solution.py
+++ b/solution.py
@@ -46,7 +46,7 @@
 
 
 def whole(shape):
-    return pl.BlockSpec(shape, lambda i, sc: (0,) * len(shape))
+    return pl.BlockSpec(shape, lambda i, *sc: (0,) * len(shape))
 
 
 VM = pl.BlockSpec(memory_space=pltpu.VMEM)
@@ -103,8 +103,8 @@
 
 
 def front_kernel(
-    seq_count, tables, x_ref, gain_ref, w_ref, pair_ref, n_out, qkv_out, hash_ref,
-    n_ref, qkv_ref, pack_ref, sum_ref, snd, rcv, psnd, prcv, loc,
+    seq_count, x_ref, gain_ref, w_ref, ids_ref, weights_ref, wo_ref, n_out, qkv_out, hash_ref, out_out,
+    out_ref, n_ref, qkv_ref, pair_ref, pack_ref, sum_ref, snd, rcv, psnd, prcv, osnd, orcv, loc,
 ):
     me, sib, far, farsib, core = places()
     seq = lax.axis_index("seq")
@@ -114,10 +114,17 @@
     greet([(seq, sib), (seq, far), (near, me)] + [(s, me) for s in level])
     rows = x_ref.shape[0]
     size = rows // STEPS
-
-    pack_ref[parity, place, me] = pair_ref[core]
+    tables = ids_ref.shape[0] // 2
+
+    def pairs(low):
+        ids = jnp.where(core == low, ids_ref[:tables], ids_ref[tables:]).astype(F32)
+        weights = jnp.where(core == low, weights_ref[:tables], weights_ref[tables:])
+        return jnp.concatenate([ids, weights, jnp.zeros((8 - 2 * tables, rows), F32)], axis=0)
+
+    pack_ref[parity, place, me] = pairs(0)
+    pair_ref[...] = pairs(1)
     mine = pack_ref.at[parity, place, me]
-    stage_sib = push(pair_ref.at[1 - core], mine, psnd.at[0], prcv.at[0], (seq, sib))
+    stage_sib = push(pair_ref, mine, psnd.at[0], prcv.at[0], (seq, sib))
     stage_sib.start()
     both = pack_ref.at[parity, place, pl.ds(me - core, 2)]
     stage_far = push(both, both, psnd.at[1], prcv.at[1], (seq, far))
@@ -128,6 +135,19 @@
     plane = pack_ref.at[parity]
     stage_near = push(plane, plane, psnd.at[half + 1], prcv.at[half + 1], (near, me))
 
+    out_ref[me] = wo_ref[...]
+    eighth = out_ref.at[me, place, parity]
+    out_far = push(eighth, eighth, osnd.at[0], orcv.at[0], (seq, far))
+    got_eighth = out_ref.at[far, place, parity]
+    out_level = [
+        push(got_eighth, got_eighth, osnd.at[2 + j], orcv.at[2 + j], (s, me))
+        for j, s in enumerate(level)
+    ]
+    got_plane = out_ref.at[far, :, parity]
+    out_near = push(got_plane, got_plane, osnd.at[half + 1], orcv.at[half + 1], (near, me))
+    out_sib = push(out_ref.at[me], out_ref.at[me], osnd.at[1], orcv.at[1], (seq, sib))
+    out_on = push(out_ref.at[far], out_ref.at[far], osnd.at[half + 2], orcv.at[half + 2], (seq, sib))
+
     def own(kind, k, to, block):
         part = n_ref.at[block, chunk(k, size)]
         return push(part, part, snd.at[kind, k], rcv.at[kind, k], (seq, to))
@@ -139,6 +159,8 @@
         if k == 0:
             stage_sib.wait_recv()
             stage_far.start()
+            out_far.start()
+            out_sib.start()
         own(1, k, far, me).start()
         own(0, k, sib, me).start()
 
@@ -151,6 +173,11 @@
                 n_ref[block, part], w_ref[c]
             ).astype(BF)
 
+    def out_home(block):
+        return pltpu.make_async_copy(out_ref.at[block], out_out.at[block], loc.at[2, block])
+
+    out_home(me).start()
+
     def homes(block):
         return [
             pltpu.make_async_copy(n_ref.at[block], n_out.at[block], loc.at[0, block]),
@@ -162,6 +189,9 @@
         copy.start()
     stage_far.wait_recv()
     for copy in stage_level:
+        copy.start()
+    out_far.wait_recv()
+    for copy in out_level:
         copy.start()
     for k in range(STEPS):
         own(0, k, sib, me).wait_recv()
@@ -204,14 +234,24 @@
         each(body, half)
 
     sums(parity)
+    for copy in out_level:
+        copy.wait_recv()
+    out_near.start()
     each(lambda k: far_chunk(k + 1), STEPS - 2)
     each(farsib_chunk, STEPS - 1)
     stage_near.wait_recv()
     sums(1 - parity)
+    out_near.wait_recv()
+    out_on.start()
+    out_home(far).start()
+    out_sib.wait_recv()
+    out_home(sib).start()
     far_chunk(STEPS - 1)
     for copy in homes(far):
         copy.start()
     hash_ref[...] = sum_ref[...].astype(BF)
+    out_on.wait_recv()
+    out_home(farsib).start()
     farsib_chunk(STEPS - 1)
     for copy in homes(farsib):
         copy.start()
@@ -223,47 +263,61 @@
     for copy in stage_level:
         copy.wait_send()
     stage_near.wait_send()
+    for copy in [out_far, out_near, out_sib, out_on] + out_level:
+        copy.wait_send()
+    for block in (me, sib, far, farsib):
+        out_home(block).wait()
     for block in (me, sib, far, farsib):
         for copy in homes(block):
             copy.wait()
 
 
-def front_call(x, gain, w, pairs, high_rows):
+def front_call(x, gain, w, ids, weights, wo, high_rows):
     seq_count = lax.axis_size("seq")
     rows, model = x.shape
     width = w.shape[0] * w.shape[2]
-    tables = 3
+    tables = ids.shape[0] // 2
     half = seq_count // 2
     dma = pltpu.SemaphoreType.DMA
     return pl.pallas_call(
-        functools.partial(front_kernel, seq_count, tables),
-        in_specs=[VM] * 4,
-        out_specs=[ANY] * 2 + [VM],
+        functools.partial(front_kernel, seq_count),
+        in_specs=[VM] * 6,
+        out_specs=[ANY] * 2 + [VM, ANY],
         out_shape=[
             jax.ShapeDtypeStruct((4, rows, model), BF),
             jax.ShapeDtypeStruct((4, rows, width), BF),
             jax.ShapeDtypeStruct((tables, high_rows, LANES), BF),
+            jax.ShapeDtypeStruct((4,) + wo.shape, BF),
         ],
         scratch_shapes=[
+            pltpu.VMEM((4,) + wo.shape, BF),
             pltpu.VMEM((4, rows, model), BF),
             pltpu.VMEM((4, rows, width), BF),
+            pltpu.VMEM((8, rows), F32),
             pltpu.VMEM((2, half, 4, 8, rows), F32),
             pltpu.VMEM((tables, high_rows, LANES), F32),
             dma((3, STEPS)),
             dma((3, STEPS)),
             dma((half + 2,)),
             dma((half + 2,)),
-            dma((2, 4)),
+            dma((half + 3,)),
+            dma((half + 3,)),
+            dma((3, 4)),
         ],
         compiler_params=params(collective_id=0, has_side_effects=True),
         cost_estimate=cost(1_000_000, 1_000_000),
         name="front",
-    )(x, gain, w, pairs)
+    )(x, gain, w, ids, weights, wo)
 
 
 def doc_bounds(sc, places):
-    low = jnp.where(places >= sc[2], sc[2], jnp.where(places >= sc[1], sc[1], 0))
-    end = jnp.where(places >= sc[2], sc[5], jnp.where(places >= sc[1], sc[4], sc[3]))
+    _, lengths, valid = sc
+    one = lengths[0]
+    two = one + lengths[1]
+    low = jnp.where(places >= two, two, jnp.where(places >= one, one, 0))
+    end = jnp.where(
+        places >= two, two + valid[2], jnp.where(places >= one, one + valid[1], valid[0])
+    )
     return low, jnp.minimum(places, end - 1)
 
 
@@ -272,7 +326,8 @@
     return jnp.where(where == h, x, jnp.zeros_like(x))
 
 
-def attend_kernel(heads, sc, qkv_ref, heads_ref, lse_ref, vt_ref, qt_ref, acc_ref, score_ref):
+def attend_kernel(heads, rank, lengths, valid, qkv_ref, heads_ref, lse_ref, vt_ref, qt_ref, acc_ref, score_ref):
+    sc = (rank, lengths, valid)
     width = heads * HEAD_DIM
     step = pl.program_id(0)
 
@@ -329,12 +384,12 @@
     return pl.pallas_call(
         functools.partial(attend_kernel, heads),
         grid_spec=pltpu.PrefetchScalarGridSpec(
-            num_scalar_prefetch=1,
+            num_scalar_prefetch=3,
             grid=(rows // QB,),
             in_specs=[whole(qkv.shape)],
             out_specs=[
-                pl.BlockSpec((QB, width), lambda i, sc: (i, 0)),
-                pl.BlockSpec((8, QB), lambda i, sc: (0, i)),
+                pl.BlockSpec((QB, width), lambda i, *sc: (i, 0)),
+                pl.BlockSpec((8, QB), lambda i, *sc: (0, i)),
             ],
             scratch_shapes=[
                 pltpu.VMEM((width, rows), BF),
@@ -350,13 +405,35 @@
         compiler_params=params(),
         cost_estimate=cost(60_000_000_000, 8_000_000),
         name="attend",
-    )(sc, qkv)
+    )(*sc, qkv)
+
+
+def spread(table_ref, out_ref, flat_ref):
+    parities, levels, tables, high_rows, _ = table_ref.shape
+    for piece in range(parities * levels):
+        p, q = piece % parities, piece // parities
+        for n in range(tables):
+            for side in range(2):
+                flat_ref[side, n * high_rows : (n + 1) * high_rows] = table_ref[
+                    p, q, n, :, side * 128 : (side + 1) * 128
+                ].astype(F32)
+
+        def body(n, carry):
+            for u in range(8):
+                row = n * 8 + u
+                for side in range(2):
+                    at = pl.multiple_of((piece * high_rows + row) * LANES + side * 128, 128)
+                    out_ref[:, pl.ds(at, 128)] = flat_ref[side, pl.ds(row, tables, stride=high_rows)]
+            return carry
+
+        lax.fori_loop(0, high_rows // 8, body, 0)
 
 
 def attend_back_kernel(
-    heads, sc, grad_ref, wo_ref, qkv_ref, heads_ref, lse_ref, mixed_ref,
-    kt_ref, qt_ref, gt_ref, qs_ref, gs_ref, dqt_ref, dk_ref, dv_ref, score_ref, prob_ref,
+    heads, rank, lengths, valid, grad_ref, qkv_ref, heads_ref, lse_ref, table_ref, mixed_ref, spread_ref,
+    kt_ref, qt_ref, gt_ref, qs_ref, gs_ref, dqt_ref, dk_ref, dv_ref, score_ref, prob_ref, flat_ref,
 ):
+    sc = (rank, lengths, valid)
     width = heads * HEAD_DIM
     step = pl.program_id(0)
     rows = qkv_ref.shape[0]
@@ -369,7 +446,7 @@
         dv_ref[...] = jnp.zeros_like(dv_ref)
 
     start = pl.multiple_of(step * QB, QB)
-    grad = dot(grad_ref[...], wo_ref[...]).astype(BF)
+    grad = grad_ref[...]
     grad_t = grad.T
     out_t = heads_ref[...].T
     product = grad_t.astype(F32) * out_t.astype(F32)
@@ -408,6 +485,7 @@
         return carry
 
     lax.fori_loop(low_first // QB, start // QB + 1, body, 0)
+    spread(table_ref, spread_ref, flat_ref)
     dq = (dqt_ref[...] * HEAD_DIM**-0.5).T.astype(BF)
     mixed_ref[pl.ds(start, QB), :width] = dq
 
@@ -419,23 +497,35 @@
             mixed_ref[part, 2 * width :] = dv_ref[:, part].T.astype(BF)
 
 
-def attend_back_call(sc, grad, wo, qkv, heads_out, lse):
+def attend_back_call(sc, grad, qkv, heads_out, lse, tables, hash_rows):
     rows, width = qkv.shape[0], qkv.shape[1] // 3
     heads = width // HEAD_DIM
-    model = wo.shape[0]
+    parities, levels, count, high_rows, lanes = tables.shape
+    per = parities * levels // (rows // QB)
+    if per == 1:
+        table_spec = pl.BlockSpec(
+            (1, 1, count, high_rows, lanes), lambda i, *sc: (i % 2, i // 2, 0, 0, 0)
+        )
+    else:
+        table_spec = pl.BlockSpec(
+            (2, per // 2, count, high_rows, lanes), lambda i, *sc: (0, i, 0, 0, 0)
+        )
     return pl.pallas_call(
         functools.partial(attend_back_kernel, heads),
         grid_spec=pltpu.PrefetchScalarGridSpec(
-            num_scalar_prefetch=1,
+            num_scalar_prefetch=3,
             grid=(rows // QB,),
             in_specs=[
-                pl.BlockSpec((QB, model), lambda i, sc: (i, 0)),
-                whole(wo.shape),
+                pl.BlockSpec((QB, width), lambda i, *sc: (i, 0)),
                 whole(qkv.shape),
-                pl.BlockSpec((QB, width), lambda i, sc: (i, 0)),
-                pl.BlockSpec((8, QB), lambda i, sc: (0, i)),
+                pl.BlockSpec((QB, width), lambda i, *sc: (i, 0)),
+                pl.BlockSpec((8, QB), lambda i, *sc: (0, i)),
+                table_spec,
             ],
-            out_specs=whole((rows, 3 * width)),
+            out_specs=[
+                whole((rows, 3 * width)),
+                pl.BlockSpec((count, per * high_rows * lanes), lambda i, *sc: (0, i)),
+            ],
             scratch_shapes=[
                 pltpu.VMEM((width, rows), BF),
                 pltpu.VMEM((width, heads * QB), BF),
@@ -447,28 +537,37 @@
                 pltpu.VMEM((width, rows), F32),
                 pltpu.VMEM((QB, heads * QB), F32),
                 pltpu.VMEM((QB, heads * QB), F32),
+                pltpu.VMEM((2, count * high_rows, 128), F32),
             ],
         ),
-        out_shape=jax.ShapeDtypeStruct((rows, 3 * width), BF),
+        out_shape=[
+            jax.ShapeDtypeStruct((rows, 3 * width), BF),
+            jax.ShapeDtypeStruct((count, hash_rows), F32),
+        ],
         compiler_params=params(),
         cost_estimate=cost(90_000_000_000, 12_000_000),
         name="attend_back",
-    )(sc, grad, wo, qkv, heads_out, lse)
+    )(*sc, grad, qkv, heads_out, lse, tables)
 
 
 def middle_kernel(
-    seq_count, heads_ref, wo_ref, x_ref, gain_ref, c0, c2, wg_in, wu_in, wd_in, table_in, *refs
+    seq_count, heads_ref, wo_in, x_in, gain_ref, c0_in, c2_in, wg_in, wu_in, wd_in, *refs
 ):
     half = seq_count // 2
-    rest_ref, fardown_ref, grad_ref, gain_out, keep_out, send_out, branch_ref, table_ref = refs[:8]
-    piece_refs, refs = refs[8 : 8 + half], refs[8 + half :]
+    early = half // 2 + 1
+    table_ins, refs = refs[:early], refs[early:]
+    rest_out, fardown_out, grad_out, gain_out, keep_out, send_out = refs[:6]
+    ostay_out, oaway_out, gh_out, table_ref = refs[6:10]
+    piece_refs, refs = refs[10 : 10 + half], refs[10 + half :]
     (
-        c1, c3, n_ref, wg_ref, wu_ref, wd_ref, act_ref, gg_ref, gu_ref,
+        rest_ref, grad_ref, wo_ref, c0, c1, c2, c3, x_ref,
+        ps_ref, pr_ref, py_ref, n_ref, wg_ref, wu_ref, wd_ref, act_ref, gg_ref, gu_ref,
         g0_ref, g1s_ref, g1r_ref, d0_ref, d1s_ref, d1r_ref,
-        as_ref, ar_ref, ys_ref, yr_ref, bs_ref, br_ref, gb_ref,
+        ys_ref, yr_ref, all_ref, gh_ref,
         stay_ref, away_ref, got_ref, up_ref, upgot_ref,
-        snd, rcv, xsnd, xrcv, zsnd, zrcv, tsnd, trcv, loc, wloc,
+        snd, rcv, xsnd, xrcv, zsnd, zrcv, tsnd, trcv, psnd, prcv, loc, wloc, hloc,
     ) = refs
+    fardown_ref, gb_ref, ar_ref, br_ref = x_ref, d0_ref, g1r_ref, d1r_ref
     me, sib, far, farsib, core = places()
     seq = lax.axis_index("seq")
     parity, place = lax.rem(seq, 2), seq // 2
@@ -479,10 +578,14 @@
         pltpu.make_async_copy(w_in, w_ref.at[: w_in.shape[0]], wloc.at[n])
         for n, (w_in, w_ref) in enumerate(((wg_in, wg_ref), (wu_in, wu_ref), (wd_in, wd_ref)))
     ]
-    for load in loads:
+    pairs = ((wo_in, wo_ref), (x_in, x_ref), (c0_in, c0), (c2_in, c2), (heads_ref.at[me], all_ref.at[me]))
+    first = [
+        pltpu.make_async_copy(src, dst, wloc.at[4 + n]) for n, (src, dst) in enumerate(pairs)
+    ]
+    for load in first + loads:
         load.start()
-    greet([(seq, sib), (seq, far), (near, me)] + [(s, me) for s in level])
-    rows, model = x_ref.shape
+    greet([(seq, sib), (seq, far), (seq, farsib), (near, me)] + [(s, me) for s in level])
+    rows, model = x_in.shape
     size = rows // STEPS
     units = wg_in.shape[0]
     long = rows // 2
@@ -497,79 +600,64 @@
 
         return made
 
-    proj_a = maker(as_ref, ar_ref, sib)
-    proj_y = maker(ys_ref, yr_ref, far)
-    proj_b = maker(bs_ref, br_ref, sib)
+    head_copies = [
+        maker(heads_ref.at[to], all_ref.at[me], to) for to in (far, farsib, sib)
+    ]
+    grad_copies = [maker(gh_ref.at[to], gh_out.at[me], to) for to in (far, farsib, sib)]
     two_sib = maker(n_ref.at[me], n_ref.at[me], sib)
     two_far = maker(n_ref.at[me], n_ref.at[me], far)
     two_on = maker(n_ref.at[far], n_ref.at[far], sib)
     back_one = maker(g1s_ref, g1r_ref, sib, long)
     down_one = maker(d1s_ref, d1r_ref, sib, long)
-    back_a = maker(as_ref, ar_ref, sib, long)
+    back_a = maker(g1s_ref, ar_ref, sib, long)
     back_y = maker(ys_ref, yr_ref, far)
-    down_three = maker(bs_ref, br_ref, sib, long)
-    branch_sib = maker(gb_ref, branch_ref.at[me], sib)
-    branch_far = maker(gb_ref, branch_ref.at[me], far)
-    branch_on = maker(branch_ref.at[far], branch_ref.at[far], sib)
-    cot_one = maker(c0, c1, sib, long)
-    cot_three = maker(c2, c3, sib, long)
-
-    def branch_home(k):
+    down_three = maker(d1s_ref, br_ref, sib, long)
+    cot_one = maker(c0_in, c1, sib, long)
+    cot_three = maker(c2_in, c3, sib, long)
+
+    def grad_home(k):
         part = chunk(k, size)
-        return pltpu.make_async_copy(gb_ref.at[part], branch_ref.at[me, part], loc.at[k])
-
-    table_home = pltpu.make_async_copy(table_in, table_ref.at[parity, place, core], wloc.at[3])
+        return pltpu.make_async_copy(gh_ref.at[me, part], gh_out.at[me, part], loc.at[0, k])
+
+    def table_spot(which, j):
+        return table_ref.at[which, lax.rem(place + half - j, half), core]
+
+    def table_home(j):
+        return pltpu.make_async_copy(table_ins[j], table_spot(parity, j), hloc.at[j])
 
     def table_level(j):
         return push(
-            table_in, table_ref.at[parity, place, core], tsnd.at[0, j], trcv.at[0, j], (level[j - 1], me)
+            table_ins[0], table_ref.at[parity, place, core], tsnd.at[0, j], trcv.at[0, j], (level[j - 1], me)
         )
 
     def table_near(j):
-        spot = table_ref.at[parity, lax.rem(place + half - j, half), core]
-        return push(table_in if j == 0 else spot, spot, tsnd.at[1, j], trcv.at[1, j], (near, me))
+        spot = table_spot(parity, j)
+        return push(table_ins[j] if j < early else spot, spot, tsnd.at[1, j], trcv.at[1, j], (near, me))
 
     def table_sib(same, j):
-        which = parity if same else 1 - parity
-        spot = table_ref.at[which, lax.rem(place + half - j, half), core]
+        spot = table_spot(parity if same else 1 - parity, j)
         kind = 2 if same else 3
-        src = table_in if same and j == 0 else spot
+        src = table_ins[j] if same and j < early else spot
         return push(src, spot, tsnd.at[kind, j], trcv.at[kind, j], (seq, sib))
 
-    table_home.start()
-    for j in range(1, half):
+    for k in range(STEPS):
+        for made in head_copies:
+            made(k).start()
+    for j in range(early, half):
         table_level(j).start()
-    table_near(0).start()
-    table_sib(True, 0).start()
+    for j in range(early):
+        table_home(j).start()
+        table_near(j).start()
+        table_sib(True, j).start()
     for k in range(2):
         cot_one(k).start()
         cot_three(k).start()
 
-    def project(block, k):
-        return dot_nt(heads_ref[block, chunk(k, size)], wo_ref[...])
-
-    def send_three(k):
-        as_ref[chunk(k, size)] = project(farsib, k).astype(BF)
-        proj_a(k).start()
-
-    def send_two(k):
-        part = project(far, k)
-        proj_a(k).wait_recv()
-        ys_ref[chunk(k, size)] = (part + ar_ref[chunk(k, size)].astype(F32)).astype(BF)
-        proj_y(k).start()
-
-    def send_one(k):
-        bs_ref[chunk(k, size)] = project(sib, k).astype(BF)
-        proj_b(k).start()
-
-    each(send_three, STEPS)
-    each(send_two, STEPS)
-    each(send_one, STEPS)
     wide = act_ref.shape[0]
     if wide > units:
         for ref in (act_ref, gg_ref, gu_ref, wg_ref, wu_ref, wd_ref):
             ref[units:] = jnp.zeros((wide - units, ref.shape[1]), BF)
-    for load in loads:
+    for load in first + loads:
         load.wait()
     for k in range(2):
         cot_one(k).wait_recv()
@@ -599,10 +687,11 @@
 
     def own_chunk(k):
         part = chunk(k, size)
-        total = x_ref[part].astype(F32) + project(me, k)
-        proj_b(k).wait_recv()
-        proj_y(k).wait_recv()
-        hidden = total + br_ref[part].astype(F32) + yr_ref[part].astype(F32)
+        hidden = x_ref[part].astype(F32) + dot_nt(all_ref[me, part], wo_ref[me])
+        for made in head_copies:
+            made(k).wait_recv()
+        for block in (sib, far, farsib):
+            hidden = hidden + dot_nt(all_ref[block, part], wo_ref[block])
         rest_ref[part] = hidden
         normed, _ = norm_rows(hidden, gain_ref[...])
         n_ref[me, part] = normed.astype(BF)
@@ -624,17 +713,10 @@
         down_one(m).start()
 
     each(own_half, 2)
-    for j in range(1, half):
+    for j in range(early, half):
         table_level(j).wait_recv()
         table_near(j).start()
         table_sib(True, j).start()
-
-    def settle(k):
-        proj_a(k).wait_send()
-        proj_y(k).wait_send()
-        proj_b(k).wait_send()
-
-    each(settle, STEPS)
 
     def far_sum(k):
         part = chunk(k, size)
@@ -642,17 +724,23 @@
         back_y(k).start()
 
     def far_half(m):
+        part = chunk(m, long)
+        back_one(m).wait_recv()
+        g0_ref[part] = (g0_ref[part].astype(F32) + g1r_ref[part].astype(F32)).astype(BF)
+        down_one(m).wait_recv()
+        d0_ref[part] = (d0_ref[part].astype(F32) + d1r_ref[part].astype(F32)).astype(BF)
         for k in (2 * m, 2 * m + 1):
             two_far(k).wait_recv()
             two_on(k).start()
         for k in (2 * m, 2 * m + 1):
             two_on(k).wait_recv()
-        part = chunk(m, long)
         back, down = feed(m, far, farsib, c2, c3)
-        as_ref[part] = back[long:].astype(BF)
+        back_one(m).wait_send()
+        g1s_ref[part] = back[long:].astype(BF)
         back_a(m).start()
         ys_ref[part] = back[:long].astype(BF)
-        bs_ref[part] = down[long:].astype(BF)
+        down_one(m).wait_send()
+        d1s_ref[part] = down[long:].astype(BF)
         down_three(m).start()
         fardown_ref[part] = down[:long].astype(BF)
         back_a(m).wait_recv()
@@ -660,9 +748,6 @@
         far_sum(2 * m + 1)
 
     each(far_half, 2)
-    for j in range(half):
-        table_near(j).wait_recv()
-        table_sib(False, j).start()
 
     piece = model // seq_count
     span = model // STEPS
@@ -727,38 +812,66 @@
 
     gain_out[...] = jnp.zeros_like(gain_out)
 
+    def leave(k, n, ref, out):
+        part = chunk(k, size)
+        return pltpu.make_async_copy(ref.at[part], out.at[part], loc.at[1 + n, k])
+
     def back_chunk(k):
         weights_step(k)
         part = chunk(k, size)
         back_y(k).wait_recv()
-        grad_norm = g0_ref[part].astype(F32) + g1r_ref[part].astype(F32) + yr_ref[part].astype(F32)
+        grad_norm = g0_ref[part].astype(F32) + yr_ref[part].astype(F32)
         hidden = rest_ref[part]
         _, scaling = norm_rows(hidden, gain_ref[...])
         grad_rows, grad_gain = norm_back(hidden, scaling, gain_ref[...], grad_norm)
         grad = c0[part].astype(F32) + grad_rows
         grad_ref[part] = grad
+        leave(k, 0, grad_ref, grad_out).start()
+        rest_ref[part] = hidden + d0_ref[part].astype(F32)
+        leave(k, 1, rest_ref, rest_out).start()
+        fardown_ref[part] = (fardown_ref[part].astype(F32) + br_ref[part].astype(F32)).astype(BF)
+        leave(k, 2, fardown_ref, fardown_out).start()
         gain_out[...] += grad_gain
         gb_ref[part] = grad.astype(BF)
-        branch_far(k).start()
-        branch_sib(k).start()
-        branch_home(k).start()
+        low = grad.astype(BF)
+        for block in (far, farsib, sib, me):
+            gh_ref[block, part] = dot(low, wo_ref[block]).astype(BF)
+        for made in grad_copies:
+            made(k).start()
+        grad_home(k).start()
 
     for m in range(2):
-        back_one(m).wait_recv()
+        down_three(m).wait_recv()
     each(back_chunk, STEPS)
-
-    for m in range(2):
-        down_one(m).wait_recv()
-        down_three(m).wait_recv()
-
-    def finish(k):
-        part = chunk(k, size)
-        rest_ref[part] += d0_ref[part].astype(F32) + d1r_ref[part].astype(F32)
-        fardown_ref[part] = (fardown_ref[part].astype(F32) + br_ref[part].astype(F32)).astype(BF)
-        branch_far(k).wait_recv()
-        branch_on(k).start()
-
-    each(finish, STEPS)
+    for j in range(half):
+        table_near(j).wait_recv()
+        table_sib(False, j).start()
+
+    def out_part(block):
+        return dot_tn(gb_ref[...], all_ref[block])
+
+    def out_sib(n):
+        return push(ps_ref.at[n], pr_ref.at[n], psnd.at[n], prcv.at[n], (seq, sib))
+
+    out_far = push(ps_ref.at[0], py_ref, psnd.at[2], prcv.at[2], (seq, far))
+    for n, block in enumerate((farsib, sib)):
+        ps_ref[n] = out_part(block).astype(BF)
+        out_sib(n).start()
+    total = out_part(far)
+    out_sib(0).wait_recv()
+    out_sib(0).wait_send()
+    ps_ref[0] = (total + pr_ref[0].astype(F32)).astype(BF)
+    out_far.start()
+    total = out_part(me)
+    out_sib(1).wait_recv()
+    total = total + pr_ref[1].astype(F32)
+    out_far.wait_recv()
+    pr_ref[0] = (total + py_ref[...].astype(F32)).astype(BF)
+    for j in range(half):
+        b = lax.rem(place + j, half)
+        take = lambda which: pl.ds(pl.multiple_of((2 * b + which) * piece, piece), piece)
+        ostay_out[j] = pr_ref[0, take(parity)]
+        oaway_out[j] = pr_ref[0, take(1 - parity)]
 
     for j in range(half):
         b = lax.rem(place + j, half)
@@ -778,17 +891,23 @@
     send_out[...] = up_sum(1 - parity)
 
     def close(k):
-        branch_sib(k).wait_recv()
-        branch_on(k).wait_recv()
-        branch_home(k).wait()
-        for made in (two_sib, two_far, two_on, back_y, branch_sib, branch_far, branch_on):
+        grad_home(k).wait()
+        leave(k, 0, grad_ref, grad_out).wait()
+        leave(k, 1, rest_ref, rest_out).wait()
+        leave(k, 2, fardown_ref, fardown_out).wait()
+        for made in grad_copies:
+            made(k).wait_recv()
+        for made in [two_sib, two_far, two_on, back_y] + head_copies + grad_copies:
             made(k).wait_send()
 
     each(close, STEPS)
     for m in range(2):
-        for made in (back_one, down_one, back_a, down_three, cot_one, cot_three):
+        for made in (back_a, down_three, cot_one, cot_three):
             made(m).wait_send()
-    table_home.wait()
+    for copy in (out_sib(1), out_far):
+        copy.wait_send()
+    for j in range(early):
+        table_home(j).wait()
     for j in range(half):
         table_sib(True, j).wait_recv()
         table_sib(False, j).wait_recv()
@@ -797,8 +916,9 @@
         table_sib(False, j).wait_send()
         for w in range(2):
             weight_away(w, j).wait_send()
+    for j in range(early, half):
+        table_level(j).wait_send()
     for j in range(1, half):
-        table_level(j).wait_send()
         up_away(j).wait_send()
 
 
@@ -816,8 +936,8 @@
     rows_bf = vm((rows, model), BF)
     return pl.pallas_call(
         functools.partial(middle_kernel, seq_count),
-        in_specs=[VM] * 6 + [ANY] * 4,
-        out_specs=[VM] * 6 + [ANY] * 2 + [VM] * half,
+        in_specs=[ANY] * 3 + [VM] + [ANY] * (5 + len(tables)),
+        out_specs=[ANY] * 3 + [VM] * 5 + [ANY] * 2 + [VM] * half,
         out_shape=[
             shape((rows, model), F32),
             shape((rows, model), BF),
@@ -825,31 +945,39 @@
             shape((1, model), F32),
             shape(block, BF),
             shape(block, BF),
-            shape((4, rows, model), BF),
-            shape((2, half, 2) + tables.shape, BF),
+            shape((half, piece, heads_out.shape[2]), BF),
+            shape((half, piece, heads_out.shape[2]), BF),
+            shape(heads_out.shape, BF),
+            shape((2, half, 2) + tables[0].shape, BF),
         ]
         + [shape((2,) + block, BF)] * half,
-        scratch_shapes=[rows_bf, rows_bf, vm((4, rows, model), BF)]
+        scratch_shapes=[vm((rows, model), F32)] * 2
+        + [vm(wo.shape, BF)]
+        + [rows_bf] * 5
+        + [vm((2,) + wo.shape[1:], BF), vm((2,) + wo.shape[1:], BF), vm(wo.shape[1:], BF)]
+        + [vm((4, rows, model), BF)]
         + [vm((wide, model), BF)] * 3
         + [vm((wide, 4 * rows), BF)] * 3
-        + [rows_bf] * 13
+        + [rows_bf] * 8
+        + [vm(heads_out.shape, BF)] * 2
         + [vm((2, half) + block, BF)] * 3
         + [vm((half, 2) + block, BF), vm((half - 1, 2) + block, BF)]
-        + [dma((16, STEPS))] * 2
+        + [dma((20, STEPS))] * 2
         + [dma((2, half))] * 2
         + [dma((half,))] * 2
         + [dma((4, half))] * 2
-        + [dma((STEPS,)), dma((4,))],
+        + [dma((3,))] * 2
+        + [dma((4, STEPS)), dma((9,)), dma((half // 2 + 1,))],
         compiler_params=params(collective_id=1, has_side_effects=True),
         cost_estimate=cost(100_000_000_000, 30_000_000),
         name="middle",
-    )(heads_out, wo, x, gain, cot, cot_far, *weights, tables)
+    )(heads_out, wo, x, gain, cot, cot_far, *weights, *tables)
 
 
 def last_kernel(
-    seq_count, mixed_in, w_in, x_in, gain_ref, grad_in, n_in, heads_in, branch_in, gain_in,
-    out_ref, wqkv_ref, wout_ref, gains_ref,
-    mixed_ref, w_ref, x_ref, grad_ref, n_ref, heads_ref, branch_ref,
+    seq_count, mixed_in, w_in, x_in, gain_ref, grad_in, n_in, gain_in,
+    out_out, wqkv_ref, gains_ref,
+    mixed_ref, w_ref, x_ref, grad_ref, n_ref,
     as_ref, ar_ref, ys_ref, yr_ref, bs_ref, br_ref, dw_ref, got_ref, sum_ref, zr_ref, gs_ref, gr_ref,
     snd, rcv, xsnd, xrcv, zsnd, zrcv, gsnd, grcv, loc,
 ):
@@ -862,8 +990,7 @@
         pltpu.make_async_copy(src, dst, loc.at[n])
         for n, (src, dst) in enumerate(
             (
-                (mixed_in, mixed_ref), (w_in, w_ref), (n_in, n_ref), (branch_in, branch_ref),
-                (heads_in, heads_ref), (x_in, x_ref), (grad_in, grad_ref),
+                (mixed_in, mixed_ref), (w_in, w_ref), (n_in, n_ref), (x_in, x_ref), (grad_in, grad_ref),
             )
         )
     ]
@@ -922,26 +1049,23 @@
     def weights_step(kk):
         k = lax.rem(place // per + 1 + kk, STEPS)
         cols = chunk(k, span)
-        to_qkv, to_out = None, None
+        total = None
         for r in range(4):
             term = dot_tn(n_ref[r, :, cols], mixed_ref[r])
-            to_qkv = term if to_qkv is None else to_qkv + term
-            term = dot_tn(branch_ref[r, :, cols], heads_ref[r])
-            to_out = term if to_out is None else to_out + term
-        for ref_at, value in ((slice(0, wide), to_qkv), (slice(wide, None), to_out)):
-            tile = value.astype(BF).reshape(per, 2, piece, value.shape[1])
-            for j in range(per):
-                b = k * per + j
-
-                @pl.when(parity == 0)
-                def _():
-                    dw_ref[0, b, :, ref_at] = tile[j, 0]
-                    dw_ref[1, b, :, ref_at] = tile[j, 1]
-
-                @pl.when(parity == 1)
-                def _():
-                    dw_ref[0, b, :, ref_at] = tile[j, 1]
-                    dw_ref[1, b, :, ref_at] = tile[j, 0]
+            total = term if total is None else total + term
+        tile = total.astype(BF).reshape(per, 2, piece, wide)
+        for j in range(per):
+            b = k * per + j
+
+            @pl.when(parity == 0)
+            def _():
+                dw_ref[0, b] = tile[j, 0]
+                dw_ref[1, b] = tile[j, 1]
+
+            @pl.when(parity == 1)
+            def _():
+                dw_ref[0, b] = tile[j, 1]
+                dw_ref[1, b] = tile[j, 0]
 
         for j in range(per):
             near_copy(k * per + j).start()
@@ -949,15 +1073,19 @@
     for load in loads[:2]:
         load.wait()
     each(send_three, STEPS)
+    loads[2].wait()
+    weights_step(0)
     each(send_two, STEPS)
-    for load in loads[2:5]:
+    each(lambda k: weights_step(k + 1), STEPS - 1)
+    each(send_one, STEPS)
+    for load in loads[3:]:
         load.wait()
-    each(weights_step, STEPS)
-    each(send_one, STEPS)
-    for load in loads[5:]:
-        load.wait()
 
     gs_ref[...] = jnp.zeros_like(gs_ref)
+
+    def leave(k):
+        part = chunk(k, size)
+        return pltpu.make_async_copy(grad_ref.at[part], out_out.at[part], loc.at[5 + k])
 
     def own_chunk(k):
         part = chunk(k, size)
@@ -968,7 +1096,8 @@
         back_y(k).wait_recv()
         grad_norm = total + br_ref[part].astype(F32) + yr_ref[part].astype(F32)
         grad_rows, grad_gain = norm_back(x, scaling, gain_ref[...], grad_norm)
-        out_ref[part] = grad_ref[part] + grad_rows
+        grad_ref[part] = grad_ref[part] + grad_rows
+        leave(k).start()
         gs_ref[0, 0:1] += grad_gain
 
     def near_sum(b):
@@ -1011,13 +1140,13 @@
         total = total + zr_ref[j].astype(F32)
     for c in range(3):
         wqkv_ref[c] = total[:, c * width : (c + 1) * width]
-    wout_ref[...] = total[:, wide:]
 
     def close(k):
         for made in (back_a, back_y, back_b):
             made(k).wait_send()
 
     each(close, STEPS)
+    each(lambda k: leave(k).wait(), STEPS)
     each(lambda b: near_copy(b).wait_send(), half)
     for n, to in enumerate(others):
         gain_copy(n, n, to).wait_send()
@@ -1026,31 +1155,30 @@
         level_copy(j).wait_send()
 
 
-def last_call(mixed, w, x, gain, grad, normed, heads_out, branch, gain_two):
+def last_call(mixed, w, x, gain, grad, normed, gain_two):
     seq_count = lax.axis_size("seq")
     rows, model = x.shape
     half = seq_count // 2
     piece = model // seq_count
-    wide, width = mixed.shape[-1], heads_out.shape[-1]
+    wide, width = mixed.shape[-1], w.shape[-1]
     dma = pltpu.SemaphoreType.DMA
     shape = jax.ShapeDtypeStruct
     rows_bf = pltpu.VMEM((rows, model), BF)
-    pieces = pltpu.VMEM((half, piece, wide + width), BF)
+    pieces = pltpu.VMEM((half, piece, wide), BF)
     return pl.pallas_call(
         functools.partial(last_kernel, seq_count),
-        in_specs=[ANY] * 3 + [VM] + [ANY] * 4 + [VM],
-        out_specs=[VM] * 4,
+        in_specs=[ANY] * 3 + [VM] + [ANY] * 2 + [VM],
+        out_specs=[ANY] + [VM] * 2,
         out_shape=[
             shape((rows, model), F32),
             shape((3, piece, width), F32),
-            shape((piece, width), F32),
             shape((8, model), F32),
         ],
         scratch_shapes=[
-            pltpu.VMEM(a.shape, a.dtype) for a in (mixed, w, x, grad, normed, heads_out, branch)
+            pltpu.VMEM(a.shape, a.dtype) for a in (mixed, w, x, grad, normed)
         ]
         + [rows_bf] * 6
-        + [pltpu.VMEM((2, half, piece, wide + width), BF), pieces, pieces, pieces]
+        + [pltpu.VMEM((2, half, piece, wide), BF), pieces, pieces, pieces]
         + [pltpu.VMEM((4, 8, model), F32), pltpu.VMEM((half + 2, 8, model), F32)]
         + [
             dma((3, STEPS)),
@@ -1061,46 +1189,12 @@
             dma((half,)),
             dma((half + 2,)),
             dma((half + 2,)),
-            dma((7,)),
+            dma((5 + STEPS,)),
         ],
         compiler_params=params(collective_id=2, has_side_effects=True),
-        cost_estimate=cost(1_000_000, 1_000_000),
+        cost_estimate=cost(90_000_000_000, 30_000_000),
         name="last",
-    )(mixed, w, x, gain, grad, normed, heads_out, branch, gain_two)
-
-
-def spread_kernel(in_ref, out_ref, flat_ref):
-    tables, high_rows = in_ref.shape[2], in_ref.shape[3]
-    for n in range(tables):
-        for side in range(2):
-            flat_ref[side, n * high_rows : (n + 1) * high_rows] = in_ref[
-                0, 0, n, :, side * 128 : (side + 1) * 128
-            ].astype(F32)
-
-    def body(n, carry):
-        for u in range(8):
-            row = n * 8 + u
-            for side in range(2):
-                at = pl.multiple_of(row * LANES + side * 128, 128)
-                out_ref[:, pl.ds(at, 128)] = flat_ref[side, pl.ds(row, tables, stride=high_rows)]
-        return carry
-
-    lax.fori_loop(0, high_rows // 8, body, 0)
-
-
-def spread_call(tables, hash_rows):
-    parities, half, count, high_rows, lanes = tables.shape
-    return pl.pallas_call(
-        spread_kernel,
-        grid=(parities * half,),
-        in_specs=[pl.BlockSpec((1, 1, count, high_rows, lanes), lambda i: (i % 2, i // 2, 0, 0, 0))],
-        out_specs=pl.BlockSpec((count, high_rows * lanes), lambda i: (0, i)),
-        out_shape=jax.ShapeDtypeStruct((count, hash_rows), F32),
-        scratch_shapes=[pltpu.VMEM((2, count * high_rows, 128), F32)],
-        compiler_params=params(),
-        cost_estimate=cost(1_000_000, 24_000_000),
-        name="hash_spread",
-    )(tables)
+    )(mixed, w, x, gain, grad, normed, gain_two)
 
 
 def shards(
@@ -1123,62 +1217,58 @@
     group_rows = 4 * local_rows
     units = w_gate.shape[1]
     rank = lax.axis_index("tp")
-    seq = lax.axis_index("seq")
-    core = rank % 2
     seq_count = lax.axis_size("seq")
-    lengths, valid = doc_lengths[0], valid_lengths[0]
-    start_one = lengths[0]
-    start_two = lengths[0] + lengths[1]
-    sc = jnp.stack(
-        [rank, start_one, start_two, valid[0], start_one + valid[1], start_two + valid[2]]
-    ).astype(jnp.int32)
+    sc = (jnp.full((1,), rank, jnp.int32), doc_lengths.reshape(-1), valid_lengths.reshape(-1))
     gain_one, gain_two = gain_one[None], gain_two[None]
 
-    tables = hash_ids.shape[0] // 2
-    blank = jnp.zeros((8 - 2 * tables, local_rows), F32)
-    pairs = jnp.stack(
-        [
-            jnp.concatenate(
-                [
-                    hash_ids[c * tables : (c + 1) * tables].astype(F32),
-                    hash_weights[c * tables : (c + 1) * tables],
-                    blank,
-                ]
-            )
-            for c in range(2)
-        ]
-    )
     per_seq = -(-HASH_ROWS // seq_count)
     high_rows = -(-per_seq // (LANES * 8)) * 8
 
     qkv_weight = w_qkv.transpose(1, 0, 2)
-    normed, qkv, sums = front_call(latents_in, gain_one, qkv_weight, pairs, high_rows)
+    piece = model_width // seq_count
+    wo_four = w_out.reshape(seq_count // 2, 2, piece, local_width)
+    normed, qkv, sums, wo_all = front_call(
+        latents_in, gain_one, qkv_weight, hash_ids, hash_weights, wo_four, high_rows
+    )
+    wo_all = wo_all.reshape(4, model_width, local_width)
     qkv, cotangent_late = lax.optimization_barrier((qkv, cotangent))
+
+    def level_flip(x, j):
+        return lax.ppermute(x, "seq", [(s, (s + 2 * j) % seq_count) for s in range(seq_count)])
+
+    table_parts = [sums] + [level_flip(sums, j) for j in range(1, seq_count // 4 + 1)]
     qkv = qkv.reshape(group_rows, 3 * local_width)
     cot_far = flip(cotangent_late, "tp", 2)
     heads_out, lse = attend_call(sc, qkv)
     heads_four = heads_out.reshape(4, local_rows, local_width)
     (
-        rest, far_down, grad_hidden, gain_two_part, up_keep, up_send, branch, hash_parts, *pieces
+        rest, far_down, grad_hidden, gain_two_part, up_keep, up_send, out_stay, out_away,
+        grad_heads, hash_parts, *pieces,
     ) = middle_call(
-        heads_four, w_out, latents_in, gain_two, cotangent, cot_far,
-        (w_gate.T, w_up.T, w_down.T), sums,
+        heads_four, wo_all, latents_in, gain_two, cotangent, cot_far,
+        (w_gate.T, w_up.T, w_down.T), table_parts,
     )
+    out_got = flip(out_away, "seq", 1)
     down_far = flip(far_down, "tp", 2)
     up_got = flip(up_send, "seq", 1)
-    arrived = [
-        lax.ppermute(pieces[j], "seq", [(s, (s + 2 * j) % seq_count) for s in range(seq_count)])
-        for j in range(1, seq_count // 2)
+    arrived = [level_flip(pieces[j], j) for j in range(1, seq_count // 2)]
+    hash_parts = hash_parts.reshape(2, seq_count // 2, hash_ids.shape[0], high_rows, LANES)
+    mixed, hash_counts = attend_back_call(
+        sc, grad_heads.reshape(group_rows, local_width), qkv, heads_out, lse, hash_parts, HASH_ROWS
+    )
+    mixed, up_got, arrived, down_far, out_got = lax.optimization_barrier(
+        (mixed, up_got, arrived, down_far, out_got)
+    )
+    out_half = [
+        (out_stay[j].astype(F32) + out_got[j].astype(F32)).astype(BF) for j in range(seq_count // 2)
     ]
-    mixed = attend_back_call(
-        sc, branch.reshape(group_rows, model_width), w_out, qkv, heads_out, lse
-    )
-    mixed, up_got, arrived, down_far = lax.optimization_barrier((mixed, up_got, arrived, down_far))
-    hash_parts = hash_parts.reshape(2, seq_count // 2, 2 * tables, high_rows, LANES)
-    hash_counts = spread_call(hash_parts, HASH_ROWS)
-    grad_latents, qkv_total, out_total, gains = last_call(
+    mixed, out_half = lax.optimization_barrier((mixed, out_half))
+    out_total = out_half[0].astype(F32)
+    for j in range(1, seq_count // 2):
+        out_total = out_total + level_flip(out_half[j], j).astype(F32)
+    grad_latents, qkv_total, gains = last_call(
         mixed.reshape(4, local_rows, -1), qkv_weight, latents_in, gain_one, grad_hidden,
-        normed, heads_four, branch, gain_two_part,
+        normed, gain_two_part,
     )
     total = pieces[0].astype(F32)
     for piece in arrived:

time: 281 us -> 264 us (0.940)
  Pallas kernels: 253 us -> 229 us
  waiting for transfers between devices: 1.91 us -> 9.96 us
  starting transfers between devices: 8.18 us -> 14 us
  between operations: 4 us -> 0.77 us
    pallas_call x3 -> x2, Pallas kernels: 159 us -> 132 us  [the longest x1 92.3 us: middle_call(): pl.pallas_call(functools.partial(middle_kernel, seq_count), in_specs=[ANY...]
    ppermute x3 -> x8, waiting for transfers between devices: 0.01 us -> 8.68 us  [level_flip(): lax.ppermute(x, 'seq', [(s, (s + 2 * j) % seq_count) for s in range(seq_c...]
    pallas_call x1, Pallas kernels: 27.4 us -> 33.1 us  [attend_back_call(): pl.pallas_call(functools.partial(attend_back_kernel, heads), grid_spec=pl...]
    ppermute x3 -> x8, starting transfers between devices: 6.55 us -> 10.9 us  [level_flip(): lax.ppermute(x, 'seq', [(s, (s + 2 * j) % seq_count) for s in range(seq_c...]
    pallas_call x1, Pallas kernels: 49.9 us -> 46.2 us  [last_call(): pl.pallas_call(functools.partial(last_kernel, seq_count), in_specs=[ANY]...]
  transfers between devices with their start and end apart: 6 -> 12, of which waited for: 1 -> 2; matrix products, arithmetic and copies ran while one was open for 1% -> 2% of each run, Pallas kernels for 20% -> 37%
where the time goes in v4:
time: 264 us
  Pallas kernels  229 us (87%)
  starting transfers between devices  14 us (5%)
  waiting for transfers between devices  9.96 us (4%)
  local copies, waits for them, and re-layouts  7.52 us (3%)
  other arithmetic  3.06 us (1%)
    pallas_call x1, Pallas kernels, middle_call(): pl.pallas_call(functools.partial(middle_kernel, seq_count), in_specs=[ANY...  92.3 us
    pallas_call x1, Pallas kernels, last_call(): pl.pallas_call(functools.partial(last_kernel, seq_count), in_specs=[ANY]...  46.2 us
    pallas_call x1, Pallas kernels, front_call(): pl.pallas_call(functools.partial(front_kernel, seq_count), in_specs=[VM]...  40.2 us
    pallas_call x1, Pallas kernels, attend_back_call(): pl.pallas_call(functools.partial(attend_back_kernel, heads), grid_spec=pl...  33.1 us
    pallas_call x1, Pallas kernels, attend_call(): pl.pallas_call(functools.partial(attend_kernel, heads), grid_spec=pltpu.P...  17.3 us
    ppermute x8, starting transfers between devices, level_flip(): lax.ppermute(x, 'seq', [(s, (s + 2 * j) % seq_count) for s in range(seq_c...  10.9 us
    ppermute x8, waiting for transfers between devices, level_flip(): lax.ppermute(x, 'seq', [(s, (s + 2 * j) % seq_count) for s in range(seq_c...  8.68 us
  transfers between devices with their start and end apart: 12, of which 2 were waited for; matrix products, arithmetic and copies ran while one was open for 2% of the time, Pallas kernels for 37%

profile of v4, /device:TPU:0, one launch (start us, length us, event | category | flops | bytes accessed | tf_op | source)
XLA Modules:
  0.0 264.5 jit_solution(12690868509178109807)
XLA Ops:
  0.7 40.2 %front.1 = (bf16[4,512,1024]{2,1,0:T(8,128)(2,1)}, bf16[4,512,768]{2,1,0:T(8,128)(2,1)}, bf16[3,248,256]{2,1,0:T(8,128)(2,1)}, bf16[4,4,2,128,256]{4,3,2,1,0:T(8,128)(2,1)}) custom-call(bf16[512,1024]{1,0:T(8,128)(2,1)} %x_in.3, f32[1,1024]{1,0:T(1,128)} %bitcast.41, bf16[3,1024,256]{2,1,0:T(8,128)(2,1)} %bitcast.37, s32[6,512]{1,0:T(8,128)} %ids_ref.1, ...), custom_call_target="tpu_custom_call" | custom-call | flops 1000000 | bytes 1000000 | tf_op jit(solution)/shard_map/front/pallas_call | solution.py:282
  40.8 0.6 collective-permute-start.2
  41.5 1.5 collective-permute-start.1
  43.5 17.3 %attend.1 = (bf16[2048,256]{1,0:T(8,128)(2,1)}, f32[8,2048]{1,0:T(8,128)}) custom-call(s32[1]{0:T(128)} %bitcast.rank, s32[3]{0:T(128)} %bitcast.52, s32[3]{0:T(128)} %bitcast.54, bf16[2048,768]{1,0:T(8,128)(2,1)} %bitcast.45), custom_call_target="tpu_custom_call" | custom-call | flops 60000002048 | bytes 8000000 | tf_op jit(solution)/shard_map/attend/pallas_call | solution.py:384
  60.8 8.7 %collective-permute-done.2.refs_2_ = bf16[3,248,256]{2,1,0:T(8,128)(2,1)S(1)} collective-permute-done((bf16[3,248,256]{2,1,0:T(8,128)(2,1)}, bf16[3,248,256]{2,1,0:T(8,128)(2,1)S(1)}, u32[]{:S(2)}, u32[]{:S(2)}) %collective-permute-start.2) | collective-permute-done | bytes 380960 | tf_op jit(solution)/shard_map/ppermute | solution.py:1237
  69.5 0.7 copy-done.7
  70.7 92.3 %middle.1 = (f32[512,1024]{1,0:T(8,128)}, bf16[512,1024]{1,0:T(8,128)(2,1)}, f32[512,1024]{1,0:T(8,128)}, f32[1,1024]{1,0:T(1,128)}, bf16[704,128]{1,0:T(8,128)(...) custom-call(bf16[4,512,256]{2,1,0:T(8,128)(2,1)} %bitcast.58, ...), custom_call_target="tpu_custom_call" | custom-call | flops 99999997952 | bytes 30000000 | tf_op jit(solution)/shard_map/middle/pallas_call | solution.py:937
  163.0 0.6 collective-permute-start.3
  163.5 1.5 collective-permute-start.8
  165.6 2.4 collective-permute-start.5
  168.0 1.5 collective-permute-start.6
  169.4 1.3 collective-permute-done.3
  171.2 33.1 %attend_back.1 = (bf16[2048,768]{1,0:T(8,128)(2,1)}, f32[6,500002]{1,0:T(8,128)}) custom-call(s32[1]{0:T(128)} %bitcast.rank, s32[3]{0:T(128)} %bitcast.53, s32[3]{0:T(128)} %bitcast.55, bf16[2048,256]{1,0:T(8,128)(2,1)} %bitcast.59, bf16[2048,768]{1,0:T(8,128)(2,1)} %bitcast.46, bf16[2048,256]{1,0:T(8,128)(2,1)} %get-tuple-element.51.heads_ref, ...), custom_call_target="tpu_custom_call" | custom-call | flops 89999998976 | bytes 12000000 | tf_op jit(solution)/shard_map/attend_back/pallas_call | solution.py:513
  204.4 0.6 collective-permute-start.9
  205.0 2.4 collective-permute-start.10
  207.4 1.5 collective-permute-start.11
  209.0 0.9 slice_bitcast_fusion
  209.9 1.4 add_convert_fusion
  211.3 0.8 add_bitcast_fusion
  212.1 46.2 %last.1 = (f32[512,1024]{1,0:T(8,128)}, f32[3,128,256]{2,1,0:T(8,128)}, f32[8,1024]{1,0:T(8,128)}) custom-call(bf16[4,512,768]{2,1,0:T(8,128)(2,1)} %bitcast.57, bf16[3,1024,256]{2,1,0:T(8,128)(2,1)} %bitcast.38, bf16[512,1024]{1,0:T(8,128)(2,1)} %x_in.3, f32[1,1024]{1,0:T(1,128)} %bitcast.42, f32[512,1024]{1,0:T(8,128)} %get-tuple-element.71.grad_in, ...), custom_call_target="tpu_custom_call" | custom-call | flops 89999998976 | bytes 30000000 | tf_op jit(solution)/shard_map/last/pallas_call | solution.py:1168
  258.3 1.4 fusion.4
  259.8 0.7 convert_add_fusion.1
  260.5 3.2 %copy.25 = f32[512,1024]{1,0:T(8,128)} copy(f32[512,1024]{1,0:T(8,128)} %get-tuple-element.107) | data formatting | bytes 4194304
  263.7 0.7 copy.26
  (32 shorter events, 2.3 us)
Async XLA Ops:
  0.6 42.4 %copy-start.5 = (bf16[512,1024]{1,0:T(8,128)(2,1)S(1)}, bf16[512,1024]{1,0:T(8,128)(2,1)}, u32[]{:S(2)}) copy-start(bf16[512,1024]{1,0:T(8,128)(2,1)} %c0_in.1) | copy-start | bytes 3145732
  40.8 28.7 %collective-permute-start.2 = (bf16[3,248,256]{2,1,0:T(8,128)(2,1)}, bf16[3,248,256]{2,1,0:T(8,128)(2,1)S(1)}, u32[]{:S(2)}, u32[]{:S(2)}) collective-permute-start(bf16[3,248,256]{2,1,0:T(8,128)(2,1)} %get-tuple-element.54.refs_0_), channel_id=1, source_target_pairs={{0,16},{4,20},{8,24},{12,28},{16,0},{20,4},{24,8},{28,12},{1,17},{... | collective-permute-start | bytes 1142792 | tf_op jit(solution)/shard_map/ppermute | solution.py:1237
  41.5 28.0 %collective-permute-start.1 = (bf16[3,248,256]{2,1,0:T(8,128)(2,1)}, bf16[3,248,256]{2,1,0:T(8,128)(2,1)S(1)}, u32[]{:S(2)}, u32[]{:S(2)}) collective-permute-start(bf16[3,248,256]{2,1,0:T(8,128)(2,1)} %get-tuple-element.54.refs_0_), channel_id=1, source_target_pairs={{0,8},{4,12},{8,16},{12,20},{16,24},{20,28},{24,0},{28,4},{1,9},{5... | collective-permute-start | bytes 1142792 | tf_op jit(solution)/shard_map/ppermute | solution.py:1237
  43.0 26.5 %collective-permute-start = (bf16[512,1024]{1,0:T(8,128)(2,1)S(1)}, bf16[512,1024]{1,0:T(8,128)(2,1)S(1)}, u32[]{:S(2)}, u32[]{:S(2)}) collective-permute-start(bf16[512,1024]{1,0:T(8,128)(2,1)S(1)} %copy-done.5), channel_id=1, source_target_pairs={{0,2},{1,3},{2,0},{3,1},{4,6},{5,7},{6,4},{7,5},{8,10},{9,11},{10,... | collective-permute-start | bytes 3145736 | tf_op jit(solution)/shard_map/ppermute | solution.py:25
  69.5 0.7 copy-start.7
  69.5 0.9 copy-start.8
  69.5 1.2 copy-start.6
  163.0 7.7 %collective-permute-start.3 = (bf16[704,128]{1,0:T(8,128)(2,1)}, bf16[704,128]{1,0:T(8,128)(2,1)S(1)}, u32[]{:S(2)}, u32[]{:S(2)}) collective-permute-start(bf16[704,128]{1,0:T(8,128)(2,1)} %get-tuple-element.60), channel_id=1, source_target_pairs={{0,4},{4,0},{8,12},{12,8},{16,20},{20,16},{24,28},{28,24},{1,5},{5... | collective-permute-start | bytes 540680 | tf_op jit(solution)/shard_map/ppermute | solution.py:25
  163.5 40.8 %collective-permute-start.8 = (bf16[4,128,256]{2,1,0:T(8,128)(2,1)}, bf16[4,128,256]{2,1,0:T(8,128)(2,1)S(1)}, u32[]{:S(2)}, u32[]{:S(2)}) collective-permute-start(bf16[4,128,256]{2,1,0:T(8,128)(2,1)} %get-tuple-element.65), channel_id=1, source_target_pairs={{0,4},{4,0},{8,12},{12,8},{16,20},{20,16},{24,28},{28,24},{1,5},{5... | collective-permute-start | bytes 786440 | tf_op jit(solution)/shard_map/ppermute | solution.py:25
  165.1 39.2 %collective-permute-start.4 = (bf16[2,704,128]{2,1,0:T(8,128)(2,1)}, bf16[2,704,128]{2,1,0:T(8,128)(2,1)S(1)}, u32[]{:S(2)}, u32[]{:S(2)}) collective-permute-start(bf16[2,704,128]{2,1,0:T(8,128)(2,1)} %get-tuple-element.61), channel_id=1, source_target_pairs={{0,8},{4,12},{8,16},{12,20},{16,24},{20,28},{24,0},{28,4},{1,9},{5... | collective-permute-start | bytes 1081352 | tf_op jit(solution)/shard_map/ppermute | solution.py:1237
  165.6 38.7 %collective-permute-start.5 = (bf16[2,704,128]{2,1,0:T(8,128)(2,1)}, bf16[2,704,128]{2,1,0:T(8,128)(2,1)S(1)}, u32[]{:S(2)}, u32[]{:S(2)}) collective-permute-start(bf16[2,704,128]{2,1,0:T(8,128)(2,1)} %get-tuple-element.62), channel_id=1, source_target_pairs={{0,16},{4,20},{8,24},{12,28},{16,0},{20,4},{24,8},{28,12},{1,17},{... | collective-permute-start | bytes 1081352 | tf_op jit(solution)/shard_map/ppermute | solution.py:1237
  168.0 36.4 %collective-permute-start.6 = (bf16[2,704,128]{2,1,0:T(8,128)(2,1)}, bf16[2,704,128]{2,1,0:T(8,128)(2,1)S(1)}, u32[]{:S(2)}, u32[]{:S(2)}) collective-permute-start(bf16[2,704,128]{2,1,0:T(8,128)(2,1)} %get-tuple-element.63), channel_id=1, source_target_pairs={{0,24},{4,28},{8,0},{12,4},{16,8},{20,12},{24,16},{28,20},{1,25},{... | collective-permute-start | bytes 1081352 | tf_op jit(solution)/shard_map/ppermute | solution.py:1237
  170.7 33.6 %collective-permute-start.7 = (bf16[512,1024]{1,0:T(8,128)(2,1)}, bf16[512,1024]{1,0:T(8,128)(2,1)S(1)}, u32[]{:S(2)}, u32[]{:S(2)}) collective-permute-start(bf16[512,1024]{1,0:T(8,128)(2,1)} %get-tuple-element.64), channel_id=1, source_target_pairs={{0,2},{1,3},{2,0},{3,1},{4,6},{5,7},{6,4},{7,5},{8,10},{9,11},{10,... | collective-permute-start | bytes 3145736 | tf_op jit(solution)/shard_map/ppermute | solution.py:25
  171.2 33.2 %copy-start.3 = (bf16[4,128,256]{2,1,0:T(8,128)(2,1)S(1)}, bf16[4,128,256]{2,1,0:T(8,128)(2,1)}, u32[]{:S(2)}) copy-start(bf16[4,128,256]{2,1,0:T(8,128)(2,1)} %get-tuple-element.68) | copy-start | bytes 786436
  171.2 37.7 %copy-start.2 = (bf16[2,704,128]{2,1,0:T(8,128)(2,1)S(1)}, bf16[2,704,128]{2,1,0:T(8,128)(2,1)}, u32[]{:S(2)}) copy-start(bf16[2,704,128]{2,1,0:T(8,128)(2,1)} %get-tuple-element.81) | copy-start | bytes 1081348
  204.4 5.6 %copy-start = (f32[512,1024]{1,0:T(8,128)S(1)}, f32[512,1024]{1,0:T(8,128)}, u32[]{:S(2)}) copy-start(f32[512,1024]{1,0:T(8,128)} %get-tuple-element.55) | copy-start | bytes 6291460
  204.4 55.3 %collective-permute-start.9 = (bf16[128,256]{1,0:T(8,128)(2,1)S(1)}, bf16[128,256]{1,0:T(8,128)(2,1)S(1)}, u32[]{:S(2)}, u32[]{:S(2)}) collective-permute-start(bf16[128,256]{1,0:T(8,128)(2,1)S(1)} %get-tuple-element.78), channel_id=1, source_target_pairs={{0,8},{4,12},{8,16},{12,20},{16,24},{20,28},{24,0},{28,4},{1,9},{5... | collective-permute-start | bytes 196616 | tf_op jit(solution)/shard_map/ppermute | solution.py:1237
  205.0 54.8 %collective-permute-start.10 = (bf16[128,256]{1,0:T(8,128)(2,1)S(1)}, bf16[128,256]{1,0:T(8,128)(2,1)S(1)}, u32[]{:S(2)}, u32[]{:S(2)}) collective-permute-start(bf16[128,256]{1,0:T(8,128)(2,1)S(1)} %get-tuple-element.79), channel_id=1, source_target_pairs={{0,16},{4,20},{8,24},{12,28},{16,0},{20,4},{24,8},{28,12},{1,17},{... | collective-permute-start | bytes 196616 | tf_op jit(solution)/shard_map/ppermute | solution.py:1237
  207.4 52.4 %collective-permute-start.11 = (bf16[128,256]{1,0:T(8,128)(2,1)S(1)}, bf16[128,256]{1,0:T(8,128)(2,1)S(1)}, u32[]{:S(2)}, u32[]{:S(2)}) collective-permute-start(bf16[128,256]{1,0:T(8,128)(2,1)S(1)} %get-tuple-element.80), channel_id=1, source_target_pairs={{0,24},{4,28},{8,0},{12,4},{16,8},{20,12},{24,16},{28,20},{1,25},{... | collective-permute-start | bytes 196616 | tf_op jit(solution)/shard_map/ppermute | solution.py:1237
  209.9 1.4 copy-start.4
  260.5 3.2 %copy-start.1 = (f32[3,128,256]{2,1,0:T(8,128)S(1)}, f32[3,128,256]{2,1,0:T(8,128)}, u32[]{:S(2)}) copy-start(f32[3,128,256]{2,1,0:T(8,128)} %get-tuple-element.76) | copy-start | bytes 1179652

commit v5 on v4

--- a/solution.py
+++ b/solution.py
@@ -557,11 +557,11 @@
     early = half // 2 + 1
     table_ins, refs = refs[:early], refs[early:]
     rest_out, fardown_out, grad_out, gain_out, keep_out, send_out = refs[:6]
-    ostay_out, oaway_out, gh_out, table_ref = refs[6:10]
-    piece_refs, refs = refs[10 : 10 + half], refs[10 + half :]
+    osums, gh_out, table_ref = refs[6:10], refs[10], refs[11]
+    piece_refs, refs = refs[12 : 12 + half], refs[12 + half :]
     (
         rest_ref, grad_ref, wo_ref, c0, c1, c2, c3, x_ref,
-        ps_ref, pr_ref, py_ref, n_ref, wg_ref, wu_ref, wd_ref, act_ref, gg_ref, gu_ref,
+        ps_ref, pr_ref, ofar_ref, n_ref, wg_ref, wu_ref, wd_ref, act_ref, gg_ref, gu_ref,
         g0_ref, g1s_ref, g1r_ref, d0_ref, d1s_ref, d1r_ref,
         ys_ref, yr_ref, all_ref, gh_ref,
         stay_ref, away_ref, got_ref, up_ref, upgot_ref,
@@ -711,6 +711,72 @@
         d0_ref[part] = down[:long].astype(BF)
         d1s_ref[part] = down[long:].astype(BF)
         down_one(m).start()
+
+    piece = model // seq_count
+    span = model // STEPS
+    per = half // STEPS
+    upright = piece % 128 == 0
+
+    def weight_away(w, b):
+        return push(
+            away_ref.at[w, b], got_ref.at[w, b], xsnd.at[w, b], xrcv.at[w, b], (near, me)
+        )
+
+    def up_away(j):
+        b = lax.rem(place + j, half)
+        return push(
+            up_ref.at[b], upgot_ref.at[j - 1], zsnd.at[j], zrcv.at[j],
+            (lax.rem(seq + 2 * j, seq_count), me),
+        )
+
+    def weight_tile(w, k, blocks):
+        cots = (c0, c1, c2, c3)
+        order = (me, sib, far, farsib)
+        left = (act_ref, gg_ref, gu_ref)[w]
+        total = None
+        for r in blocks:
+            cols = chunk(k, span)
+            right = cots[r][:, cols] if w == 0 else n_ref[order[r], :, cols]
+            lanes = pl.ds(pl.multiple_of(order[r] * rows, rows), rows)
+            term = dot(left[:units, lanes], right)
+            total = term if total is None else total + term
+        return total
+
+    def weights_step(kk):
+        k = lax.rem(place // per + 1 + kk, STEPS)
+        for w in range(3):
+            tile = weight_tile(w, k, range(4))
+            tile = tile if upright else tile.T
+
+            def put(ref, value):
+                ref[...] = value.astype(BF)
+
+            for n in range(per):
+                b = k * per + n
+                take = lambda i: slice(i * piece, (i + 1) * piece)
+                even = tile[:, take(2 * n)] if upright else tile[take(2 * n)]
+                odd = tile[:, take(2 * n + 1)] if upright else tile[take(2 * n + 1)]
+                if w == 2:
+                    put(up_ref.at[b, 0], even)
+                    put(up_ref.at[b, 1], odd)
+
+                    @pl.when(b != place)
+                    def _():
+                        up_away(lax.rem(b + half - place, half)).start()
+
+                else:
+
+                    @pl.when(parity == 0)
+                    def _():
+                        put(stay_ref.at[w, b], even)
+                        put(away_ref.at[w, b], odd)
+
+                    @pl.when(parity == 1)
+                    def _():
+                        put(stay_ref.at[w, b], odd)
+                        put(away_ref.at[w, b], even)
+
+                    weight_away(w, b).start()
 
     each(own_half, 2)
     for j in range(early, half):
@@ -749,67 +815,6 @@
 
     each(far_half, 2)
 
-    piece = model // seq_count
-    span = model // STEPS
-    per = half // STEPS
-    upright = piece % 128 == 0
-
-    def weight_away(w, b):
-        return push(
-            away_ref.at[w, b], got_ref.at[w, b], xsnd.at[w, b], xrcv.at[w, b], (near, me)
-        )
-
-    def up_away(j):
-        b = lax.rem(place + j, half)
-        return push(
-            up_ref.at[b], upgot_ref.at[j - 1], zsnd.at[j], zrcv.at[j],
-            (lax.rem(seq + 2 * j, seq_count), me),
-        )
-
-    def weight_tile(w, k):
-        cots = (c0, c1, c2, c3)
-        order = (me, sib, far, farsib)
-        left = (act_ref, gg_ref, gu_ref)[w]
-        total = None
-        for r in range(4):
-            cols = chunk(k, span)
-            right = cots[r][:, cols] if w == 0 else n_ref[order[r], :, cols]
-            lanes = pl.ds(pl.multiple_of(order[r] * rows, rows), rows)
-            term = dot(left[:units, lanes], right)
-            total = term if total is None else total + term
-        return total.astype(BF)
-
-    def weights_step(kk):
-        k = lax.rem(place // per + 1 + kk, STEPS)
-        for w in range(3):
-            tile = weight_tile(w, k)
-            tile = tile if upright else tile.T
-            for n in range(per):
-                b = k * per + n
-                take = lambda i: slice(i * piece, (i + 1) * piece)
-                even = tile[:, take(2 * n)] if upright else tile[take(2 * n)]
-                odd = tile[:, take(2 * n + 1)] if upright else tile[take(2 * n + 1)]
-                if w == 2:
-                    up_ref[b, 0] = even
-                    up_ref[b, 1] = odd
-
-                    @pl.when(b != place)
-                    def _():
-                        up_away(lax.rem(b + half - place, half)).start()
-                else:
-
-                    @pl.when(parity == 0)
-                    def _():
-                        stay_ref[w, b] = even
-                        away_ref[w, b] = odd
-
-                    @pl.when(parity == 1)
-                    def _():
-                        stay_ref[w, b] = odd
-                        away_ref[w, b] = even
-
-                    weight_away(w, b).start()
-
     gain_out[...] = jnp.zeros_like(gain_out)
 
     def leave(k, n, ref, out):
@@ -848,30 +853,37 @@
         table_sib(False, j).start()
 
     def out_part(block):
-        return dot_tn(gb_ref[...], all_ref[block])
+        return dot_tn(all_ref[block], gb_ref[...])
 
     def out_sib(n):
         return push(ps_ref.at[n], pr_ref.at[n], psnd.at[n], prcv.at[n], (seq, sib))
 
-    out_far = push(ps_ref.at[0], py_ref, psnd.at[2], prcv.at[2], (seq, far))
     for n, block in enumerate((farsib, sib)):
         ps_ref[n] = out_part(block).astype(BF)
         out_sib(n).start()
-    total = out_part(far)
-    out_sib(0).wait_recv()
-    out_sib(0).wait_send()
-    ps_ref[0] = (total + pr_ref[0].astype(F32)).astype(BF)
-    out_far.start()
-    total = out_part(me)
-    out_sib(1).wait_recv()
-    total = total + pr_ref[1].astype(F32)
-    out_far.wait_recv()
-    pr_ref[0] = (total + py_ref[...].astype(F32)).astype(BF)
-    for j in range(half):
-        b = lax.rem(place + j, half)
-        take = lambda which: pl.ds(pl.multiple_of((2 * b + which) * piece, piece), piece)
-        ostay_out[j] = pr_ref[0, take(parity)]
-        oaway_out[j] = pr_ref[0, take(1 - parity)]
+    full_ref = wo_ref.at[0]
+    width = full_ref.shape[1]
+    ofar_home = pltpu.make_async_copy(ofar_ref, fardown_out.at[rows:], wloc.at[3])
+    for n, (block, outs) in enumerate(((far, osums[2:]), (me, osums[:2]))):
+        total = out_part(block)
+        out_sib(n).wait_recv()
+        full_ref[...] = (total + pr_ref[n].astype(F32)).astype(BF).T
+        for j in range(half):
+            b = lax.rem(place + j, half)
+            for side, (which, out) in enumerate(zip((parity, 1 - parity), outs)):
+                part = full_ref[pl.ds(pl.multiple_of((2 * b + which) * piece, piece), piece)]
+                if n == 0 and side == 0:
+                    beside = model // width
+                    at, lane = j // beside * piece, j % beside * width
+                    ofar_ref[at : at + piece, lane : lane + width] = part
+                elif n == 1 and side == 1 and piece == 128:
+                    for m in range(width // piece):
+                        at = units + (j * (width // piece) + m) * piece
+                        send_out[at : at + piece] = part[:, m * piece : (m + 1) * piece]
+                else:
+                    out[j] = part
+        if n == 0:
+            ofar_home.start()
 
     for j in range(half):
         b = lax.rem(place + j, half)
@@ -888,7 +900,10 @@
     for j in range(1, half):
         up_away(j).wait_recv()
     keep_out[...] = up_sum(parity)
-    send_out[...] = up_sum(1 - parity)
+    if piece == 128:
+        send_out[:units] = up_sum(1 - parity)
+    else:
+        send_out[...] = up_sum(1 - parity)
 
     def close(k):
         grad_home(k).wait()
@@ -904,7 +919,8 @@
     for m in range(2):
         for made in (back_a, down_three, cot_one, cot_three):
             made(m).wait_send()
-    for copy in (out_sib(1), out_far):
+    ofar_home.wait()
+    for copy in (out_sib(0), out_sib(1)):
         copy.wait_send()
     for j in range(early):
         table_home(j).wait()
@@ -930,6 +946,9 @@
     units = weights[0].shape[0]
     wide = units + -units % 256
     block = (units, piece) if piece % 128 == 0 else (piece, units)
+    width = heads_out.shape[2]
+    tall = half * piece * width // model
+    joined = (units + half * width, piece) if piece == 128 else block
     dma = pltpu.SemaphoreType.DMA
     shape = jax.ShapeDtypeStruct
     vm = pltpu.VMEM
@@ -937,16 +956,17 @@
     return pl.pallas_call(
         functools.partial(middle_kernel, seq_count),
         in_specs=[ANY] * 3 + [VM] + [ANY] * (5 + len(tables)),
-        out_specs=[ANY] * 3 + [VM] * 5 + [ANY] * 2 + [VM] * half,
+        out_specs=[ANY] * 3 + [VM] * 7 + [ANY] * 2 + [VM] * half,
         out_shape=[
             shape((rows, model), F32),
-            shape((rows, model), BF),
+            shape((rows + tall, model), BF),
             shape((rows, model), F32),
             shape((1, model), F32),
             shape(block, BF),
-            shape(block, BF),
-            shape((half, piece, heads_out.shape[2]), BF),
-            shape((half, piece, heads_out.shape[2]), BF),
+            shape(joined, BF),
+        ]
+        + [shape((half, piece, heads_out.shape[2]), BF)] * 4
+        + [
             shape(heads_out.shape, BF),
             shape((2, half, 2) + tables[0].shape, BF),
         ]
@@ -954,7 +974,8 @@
         scratch_shapes=[vm((rows, model), F32)] * 2
         + [vm(wo.shape, BF)]
         + [rows_bf] * 5
-        + [vm((2,) + wo.shape[1:], BF), vm((2,) + wo.shape[1:], BF), vm(wo.shape[1:], BF)]
+        + [vm((2, wo.shape[2], model), BF)] * 2
+        + [vm((tall, model), BF)]
         + [vm((4, rows, model), BF)]
         + [vm((wide, model), BF)] * 3
         + [vm((wide, 4 * rows), BF)] * 3
@@ -966,7 +987,7 @@
         + [dma((2, half))] * 2
         + [dma((half,))] * 2
         + [dma((4, half))] * 2
-        + [dma((3,))] * 2
+        + [dma((2,))] * 2
         + [dma((4, STEPS)), dma((9,)), dma((half // 2 + 1,))],
         compiler_params=params(collective_id=1, has_side_effects=True),
         cost_estimate=cost(100_000_000_000, 30_000_000),
@@ -975,28 +996,30 @@
 
 
 def last_kernel(
-    seq_count, mixed_in, w_in, x_in, gain_ref, grad_in, n_in, gain_in,
-    out_out, wqkv_ref, gains_ref,
-    mixed_ref, w_ref, x_ref, grad_ref, n_ref,
+    seq_count, mixed_in, w_in, x_in, gain_ref, grad_in, n_in, o0, o1, o2, o3, gain_in,
+    out_out, wqkv_ref, wout_ref, gains_ref,
+    mixed_ref, w_ref, x_ref, grad_ref, n_ref, osum_ref, oz_ref,
     as_ref, ar_ref, ys_ref, yr_ref, bs_ref, br_ref, dw_ref, got_ref, sum_ref, zr_ref, gs_ref, gr_ref,
-    snd, rcv, xsnd, xrcv, zsnd, zrcv, gsnd, grcv, loc,
+    snd, rcv, xsnd, xrcv, zsnd, zrcv, gsnd, grcv, osnd, orcv, loc,
 ):
     me, sib, far, farsib, core = places()
     seq = lax.axis_index("seq")
     parity, place, half = lax.rem(seq, 2), seq // 2, seq_count // 2
     near = seq + 1 - 2 * parity
-    level = [lax.rem(seq + 2 * j, seq_count) for j in range(1, half)]
     loads = [
         pltpu.make_async_copy(src, dst, loc.at[n])
         for n, (src, dst) in enumerate(
             (
-                (mixed_in, mixed_ref), (w_in, w_ref), (n_in, n_ref), (x_in, x_ref), (grad_in, grad_ref),
+                (mixed_in, mixed_ref), (n_in, n_ref), (w_in, w_ref), (x_in, x_ref), (grad_in, grad_ref),
             )
         )
     ]
     for load in loads:
         load.start()
-    greet([(seq, sib), (seq, far), (near, me)] + [(s, me) for s in level])
+    greet(
+        [(seq, sib), (seq, far), (seq, farsib)]
+        + [(lax.rem(seq + j, seq_count), me) for j in range(1, seq_count)]
+    )
     rows, model = x_ref.shape
     size = rows // STEPS
     piece = model // seq_count
@@ -1070,13 +1093,34 @@
         for j in range(per):
             near_copy(k * per + j).start()
 
+    def out_copy(j):
+        return push(
+            osum_ref.at[j], oz_ref.at[j], osnd.at[j], orcv.at[j], (lax.rem(seq + 2 * j, seq_count), me)
+        )
+
+    def add(j):
+        beside = model // width
+        at, lane = j // beside * piece, j % beside * width
+        parts = [o0[j], o2[at : at + piece, lane : lane + width], o3[j]]
+        if piece == 128:
+            count = width // piece
+            rows_of = lambda m: slice((j * count + m) * piece, (j * count + m + 1) * piece)
+            parts.append(jnp.concatenate([o1[rows_of(m)] for m in range(count)], axis=1))
+        else:
+            parts.append(o1[j])
+        return sum(part.astype(F32) for part in parts)
+
+    for j in range(1, half):
+        osum_ref[j] = add(j).astype(BF)
+        out_copy(j).start()
     for load in loads[:2]:
         load.wait()
+    weights_step(0)
+    loads[2].wait()
     each(send_three, STEPS)
-    loads[2].wait()
-    weights_step(0)
+    weights_step(1)
     each(send_two, STEPS)
-    each(lambda k: weights_step(k + 1), STEPS - 1)
+    each(lambda k: weights_step(k + 2), STEPS - 2)
     each(send_one, STEPS)
     for load in loads[3:]:
         load.wait()
@@ -1108,30 +1152,39 @@
         def _():
             level_copy(lax.rem(b + half - place, half)).start()
 
-    def both(kk):
+    def near_sums(kk):
         k = lax.rem(place // per + 1 + kk, STEPS)
-        own_chunk(kk)
         for n in range(per):
             near_sum(k * per + n)
 
-    each(both, STEPS)
+    near_sums(0)
+
+    def both(kk):
+        near_sums(kk + 1)
+        own_chunk(kk)
+
+    each(both, STEPS - 1)
+    own_chunk(STEPS - 1)
 
     gs_ref[0, 1:2] = gain_in[...]
-    others = [(seq, sib), (seq, far), (near, me)]
-
-    def gain_copy(n, slot, to):
-        return push(gs_ref.at[n], gr_ref.at[slot], gsnd.at[slot], grcv.at[slot], to)
-
-    for n, to in enumerate(others):
-        gain_copy(n, n, to).start()
-        gain_copy(n, n, to).wait_recv()
-        gs_ref[n + 1] = gs_ref[n] + gr_ref[n]
-    for j in range(1, half):
-        gain_copy(3, 2 + j, (level[j - 1], me)).start()
-    gains = gs_ref[3]
-    for j in range(1, half):
-        gain_copy(3, 2 + j, (level[j - 1], me)).wait_recv()
-        gains = gains + gr_ref[2 + j]
+    rounds = [
+        [(seq, sib), (seq, far), (seq, farsib)],
+        [(lax.rem(seq + j, seq_count), me) for j in range(1, seq_count)],
+    ]
+
+    def gain_copy(stage, n):
+        slot = 3 * stage + n
+        return push(gs_ref.at[stage], gr_ref.at[slot], gsnd.at[slot], grcv.at[slot], rounds[stage][n])
+
+    gains = gs_ref[0]
+    for stage in range(2):
+        for n in range(len(rounds[stage])):
+            gain_copy(stage, n).start()
+        for n in range(len(rounds[stage])):
+            gain_copy(stage, n).wait_recv()
+            gains = gains + gr_ref[3 * stage + n]
+        if stage == 0:
+            gs_ref[1] = gains
     gains_ref[...] = gains
 
     total = sum_ref[place].astype(F32)
@@ -1140,6 +1193,11 @@
         total = total + zr_ref[j].astype(F32)
     for c in range(3):
         wqkv_ref[c] = total[:, c * width : (c + 1) * width]
+    out_total = add(0)
+    for j in range(1, half):
+        out_copy(j).wait_recv()
+        out_total = out_total + oz_ref[j].astype(F32)
+    wout_ref[...] = out_total
 
     def close(k):
         for made in (back_a, back_y, back_b):
@@ -1148,14 +1206,15 @@
     each(close, STEPS)
     each(lambda k: leave(k).wait(), STEPS)
     each(lambda b: near_copy(b).wait_send(), half)
-    for n, to in enumerate(others):
-        gain_copy(n, n, to).wait_send()
+    for stage in range(2):
+        for n in range(len(rounds[stage])):
+            gain_copy(stage, n).wait_send()
     for j in range(1, half):
-        gain_copy(3, 2 + j, (level[j - 1], me)).wait_send()
         level_copy(j).wait_send()
-
-
-def last_call(mixed, w, x, gain, grad, normed, gain_two):
+        out_copy(j).wait_send()
+
+
+def last_call(mixed, w, x, gain, grad, normed, outs, gain_two):
     seq_count = lax.axis_size("seq")
     rows, model = x.shape
     half = seq_count // 2
@@ -1167,19 +1226,20 @@
     pieces = pltpu.VMEM((half, piece, wide), BF)
     return pl.pallas_call(
         functools.partial(last_kernel, seq_count),
-        in_specs=[ANY] * 3 + [VM] + [ANY] * 2 + [VM],
-        out_specs=[ANY] + [VM] * 2,
+        in_specs=[ANY] * 3 + [VM] + [ANY] * 2 + [VM] * 5,
+        out_specs=[ANY] + [VM] * 3,
         out_shape=[
             shape((rows, model), F32),
             shape((3, piece, width), F32),
+            shape((piece, width), F32),
             shape((8, model), F32),
         ],
         scratch_shapes=[
-            pltpu.VMEM(a.shape, a.dtype) for a in (mixed, w, x, grad, normed)
+            pltpu.VMEM(a.shape, a.dtype) for a in (mixed, w, x, grad, normed, outs[0], outs[0])
         ]
         + [rows_bf] * 6
         + [pltpu.VMEM((2, half, piece, wide), BF), pieces, pieces, pieces]
-        + [pltpu.VMEM((4, 8, model), F32), pltpu.VMEM((half + 2, 8, model), F32)]
+        + [pltpu.VMEM((2, 8, model), F32), pltpu.VMEM((seq_count + 2, 8, model), F32)]
         + [
             dma((3, STEPS)),
             dma((3, STEPS)),
@@ -1187,14 +1247,16 @@
             dma((half,)),
             dma((half,)),
             dma((half,)),
-            dma((half + 2,)),
-            dma((half + 2,)),
+            dma((seq_count + 2,)),
+            dma((seq_count + 2,)),
+            dma((half,)),
+            dma((half,)),
             dma((5 + STEPS,)),
         ],
         compiler_params=params(collective_id=2, has_side_effects=True),
         cost_estimate=cost(90_000_000_000, 30_000_000),
         name="last",
-    )(mixed, w, x, gain, grad, normed, gain_two)
+    )(mixed, w, x, gain, grad, normed, *outs, gain_two)
 
 
 def shards(
@@ -1242,39 +1304,38 @@
     heads_out, lse = attend_call(sc, qkv)
     heads_four = heads_out.reshape(4, local_rows, local_width)
     (
-        rest, far_down, grad_hidden, gain_two_part, up_keep, up_send, out_stay, out_away,
-        grad_heads, hash_parts, *pieces,
+        rest, far_down, grad_hidden, gain_two_part, up_keep, up_send, out_own, out_near,
+        out_far, out_cross, grad_heads, hash_parts, *pieces,
     ) = middle_call(
         heads_four, wo_all, latents_in, gain_two, cotangent, cot_far,
         (w_gate.T, w_up.T, w_down.T), table_parts,
     )
-    out_got = flip(out_away, "seq", 1)
     down_far = flip(far_down, "tp", 2)
     up_got = flip(up_send, "seq", 1)
+    cross = [(4 * s + t, 4 * (s ^ 1) + (t ^ 2)) for s in range(seq_count) for t in range(4)]
+    out_parts = [
+        out_own,
+        up_got[units:] if piece == 128 else flip(out_near, "seq", 1),
+        down_far[local_rows:],
+        lax.ppermute(out_cross, ("seq", "tp"), cross),
+    ]
     arrived = [level_flip(pieces[j], j) for j in range(1, seq_count // 2)]
     hash_parts = hash_parts.reshape(2, seq_count // 2, hash_ids.shape[0], high_rows, LANES)
     mixed, hash_counts = attend_back_call(
         sc, grad_heads.reshape(group_rows, local_width), qkv, heads_out, lse, hash_parts, HASH_ROWS
     )
-    mixed, up_got, arrived, down_far, out_got = lax.optimization_barrier(
-        (mixed, up_got, arrived, down_far, out_got)
+    mixed, up_got, arrived, down_far, out_parts = lax.optimization_barrier(
+        (mixed, up_got, arrived, down_far, out_parts)
     )
-    out_half = [
-        (out_stay[j].astype(F32) + out_got[j].astype(F32)).astype(BF) for j in range(seq_count // 2)
-    ]
-    mixed, out_half = lax.optimization_barrier((mixed, out_half))
-    out_total = out_half[0].astype(F32)
-    for j in range(1, seq_count // 2):
-        out_total = out_total + level_flip(out_half[j], j).astype(F32)
-    grad_latents, qkv_total, gains = last_call(
+    grad_latents, qkv_total, out_total, gains = last_call(
         mixed.reshape(4, local_rows, -1), qkv_weight, latents_in, gain_one, grad_hidden,
-        normed, gain_two_part,
+        normed, out_parts, gain_two_part,
     )
     total = pieces[0].astype(F32)
-    for piece in arrived:
-        total = total + piece.astype(F32)
-    up_total = up_keep.astype(F32) + up_got.astype(F32)
-    latents_out = (rest + down_far.astype(F32)).astype(BF)
+    for part in arrived:
+        total = total + part.astype(F32)
+    up_total = up_keep.astype(F32) + (up_got[:units] if piece == 128 else up_got).astype(F32)
+    latents_out = (rest + down_far[:local_rows].astype(F32)).astype(BF)
     upright = lambda w: w.T if w.shape[0] == units else w
     return (
         latents_out,

time: 264 us -> 266 us (level)
    pallas_call x1, Pallas kernels: 46.2 us -> 51.9 us  [last_call(): pl.pallas_call(functools.partial(last_kernel, seq_count), in_specs=[ANY]...]
    pallas_call x1, Pallas kernels: 92.3 us -> 86.7 us  [middle_call(): pl.pallas_call(functools.partial(middle_kernel, seq_count), in_specs=[ANY...]
    ppermute x8 -> x5, starting transfers between devices: 10.9 us -> 10.2 us  [level_flip(): lax.ppermute(x, 'seq', [(s, (s + 2 * j) % seq_count) for s in range(seq_c...]
    ppermute x8 -> x5, waiting for transfers between devices: 8.68 us -> 8.98 us  [level_flip(): lax.ppermute(x, 'seq', [(s, (s + 2 * j) % seq_count) for s in range(seq_c...]
  transfers between devices with their start and end apart: 12 -> 9, of which waited for: 2 -> 2; matrix products, arithmetic and copies ran while one was open for 2% -> 1% of each run, Pallas kernels for 37% -> 19%
where the time goes in v5:
time: 266 us
  Pallas kernels  229 us (86%)
  starting transfers between devices  14.2 us (5%)
  waiting for transfers between devices  11.4 us (4%)
  local copies, waits for them, and re-layouts  8.29 us (3%)
    pallas_call x1, Pallas kernels, middle_call(): pl.pallas_call(functools.partial(middle_kernel, seq_count), in_specs=[ANY...  86.7 us
    pallas_call x1, Pallas kernels, last_call(): pl.pallas_call(functools.partial(last_kernel, seq_count), in_specs=[ANY]...  51.9 us
    pallas_call x1, Pallas kernels, front_call(): pl.pallas_call(functools.partial(front_kernel, seq_count), in_specs=[VM]...  40.2 us
    pallas_call x1, Pallas kernels, attend_back_call(): pl.pallas_call(functools.partial(attend_back_kernel, heads), grid_spec=pl...  33.1 us
    pallas_call x1, Pallas kernels, attend_call(): pl.pallas_call(functools.partial(attend_kernel, heads), grid_spec=pltpu.P...  17.3 us
    ppermute x5, starting transfers between devices, level_flip(): lax.ppermute(x, 'seq', [(s, (s + 2 * j) % seq_count) for s in range(seq_c...  10.2 us
    ppermute x5, waiting for transfers between devices, level_flip(): lax.ppermute(x, 'seq', [(s, (s + 2 * j) % seq_count) for s in range(seq_c...  8.98 us
  transfers between devices with their start and end apart: 9, of which 2 were waited for; matrix products, arithmetic and copies ran while one was open for 1% of the time, Pallas kernels for 19%

profile of v5, /device:TPU:0, one launch (start us, length us, event | category | flops | bytes accessed | tf_op | source)
XLA Modules:
  0.0 266.1 jit_solution(8488252219672495751)
XLA Ops:
  0.7 40.2 %front.1 = (bf16[4,512,1024]{2,1,0:T(8,128)(2,1)}, bf16[4,512,768]{2,1,0:T(8,128)(2,1)}, bf16[3,248,256]{2,1,0:T(8,128)(2,1)}, bf16[4,4,2,128,256]{4,3,2,1,0:T(8,128)(2,1)}) custom-call(bf16[512,1024]{1,0:T(8,128)(2,1)} %x_in.3, f32[1,1024]{1,0:T(1,128)} %bitcast.33, bf16[3,1024,256]{2,1,0:T(8,128)(2,1)} %bitcast.29, s32[6,512]{1,0:T(8,128)} %ids_ref.1, ...), custom_call_target="tpu_custom_call" | custom-call | flops 1000000 | bytes 1000000 | tf_op jit(solution)/shard_map/front/pallas_call | solution.py:282
  40.9 0.8 collective-permute-start.1
  41.7 1.5 collective-permute-start.2
  43.6 17.3 %attend.1 = (bf16[2048,256]{1,0:T(8,128)(2,1)}, f32[8,2048]{1,0:T(8,128)}) custom-call(s32[1]{0:T(128)} %bitcast.rank, s32[3]{0:T(128)} %bitcast.44, s32[3]{0:T(128)} %bitcast.46, bf16[2048,768]{1,0:T(8,128)(2,1)} %bitcast.37), custom_call_target="tpu_custom_call" | custom-call | flops 60000002048 | bytes 8000000 | tf_op jit(solution)/shard_map/attend/pallas_call | solution.py:384
  61.0 9.0 %collective-permute-done.2.refs_2_ = bf16[3,248,256]{2,1,0:T(8,128)(2,1)S(1)} collective-permute-done((bf16[3,248,256]{2,1,0:T(8,128)(2,1)}, bf16[3,248,256]{2,1,0:T(8,128)(2,1)S(1)}, u32[]{:S(2)}, u32[]{:S(2)}) %collective-permute-start.2) | collective-permute-done | bytes 380960 | tf_op jit(solution)/shard_map/ppermute | solution.py:1299
  70.0 0.7 copy-done.9
  71.0 86.7 %middle.1 = (f32[512,1024]{1,0:T(8,128)}, bf16[640,1024]{1,0:T(8,128)(2,1)}, f32[512,1024]{1,0:T(8,128)}, f32[1,1024]{1,0:T(1,128)}, bf16[704,128]{1,0:T(8,128)(...) custom-call(bf16[4,512,256]{2,1,0:T(8,128)(2,1)} %bitcast.50, ...), custom_call_target="tpu_custom_call" | custom-call | flops 99999997952 | bytes 30000000 | tf_op jit(solution)/shard_map/middle/pallas_call | solution.py:956
  158.3 1.4 collective-permute-start.7
  159.7 5.5 %collective-permute-start.4 = (bf16[2,704,128]{2,1,0:T(8,128)(2,1)}, bf16[2,704,128]{2,1,0:T(8,128)(2,1)S(1)}, u32[]{:S(2)}, u32[]{:S(2)}) collective-permute-start(bf16[2,704,128]{2,1,0:T(8,128)(2,1)} %get-tuple-element.60), channel_id=1, source_target_pairs={{0,8},{4,12},{8,16},{12,20},{16,24},{20,28},{24,0},{28,4},{1,9},{5... | collective-permute-start | bytes 1081352 | tf_op jit(solution)/shard_map/ppermute | solution.py:1299
  165.7 1.9 collective-permute-start.6
  167.6 2.4 collective-permute-done.3
  170.0 1.5 collective-permute-start.8
  171.6 33.1 %attend_back.1 = (bf16[2048,768]{1,0:T(8,128)(2,1)}, f32[6,500002]{1,0:T(8,128)}) custom-call(s32[1]{0:T(128)} %bitcast.rank, s32[3]{0:T(128)} %bitcast.45, s32[3]{0:T(128)} %bitcast.47, bf16[2048,256]{1,0:T(8,128)(2,1)} %bitcast.51, bf16[2048,768]{1,0:T(8,128)(2,1)} %bitcast.38, bf16[2048,256]{1,0:T(8,128)(2,1)} %get-tuple-element.50.heads_ref, ...), custom_call_target="tpu_custom_call" | custom-call | flops 89999998976 | bytes 12000000 | tf_op jit(solution)/shard_map/attend_back/pallas_call | solution.py:513
  204.7 0.7 slice.32.o1
  205.4 0.7 slice.33.o2
  206.4 0.9 slice_bitcast_fusion
  207.3 51.9 %last.1 = (f32[512,1024]{1,0:T(8,128)}, f32[3,128,256]{2,1,0:T(8,128)}, f32[128,256]{1,0:T(8,128)}, f32[8,1024]{1,0:T(8,128)}) custom-call(bf16[4,512,768]{2,1,0:T(8,128)(2,1)} %bitcast.49, bf16[3,1024,256]{2,1,0:T(8,128)(2,1)} %bitcast.30, bf16[512,1024]{1,0:T(8,128)(2,1)} %x_in.3, f32[1,1024]{1,0:T(1,128)} %bitcast.34, ...), custom_call_target="tpu_custom_call" | custom-call | flops 89999998976 | bytes 30000000 | tf_op jit(solution)/shard_map/last/pallas_call | solution.py:1227
  259.2 1.4 fusion
  260.6 0.8 add_bitcast_fusion
  261.4 1.3 add_convert_fusion
  262.7 0.7 copy-done.1
  263.3 1.3 copy.26
  264.7 0.7 copy.27
  265.4 0.7 copy.28
  (31 shorter events, 2.1 us)
Async XLA Ops:
  0.6 42.5 %copy-start.6 = (bf16[512,1024]{1,0:T(8,128)(2,1)S(1)}, bf16[512,1024]{1,0:T(8,128)(2,1)}, u32[]{:S(2)}) copy-start(bf16[512,1024]{1,0:T(8,128)(2,1)} %c0_in.1) | copy-start | bytes 3145732
  40.9 20.1 %collective-permute-start.1 = (bf16[3,248,256]{2,1,0:T(8,128)(2,1)}, bf16[3,248,256]{2,1,0:T(8,128)(2,1)S(1)}, u32[]{:S(2)}, u32[]{:S(2)}) collective-permute-start(bf16[3,248,256]{2,1,0:T(8,128)(2,1)} %get-tuple-element.53.refs_0_), channel_id=1, source_target_pairs={{0,8},{4,12},{8,16},{12,20},{16,24},{20,28},{24,0},{28,4},{1,9},{5... | collective-permute-start | bytes 1142792 | tf_op jit(solution)/shard_map/ppermute | solution.py:1299
  41.7 28.3 %collective-permute-start.2 = (bf16[3,248,256]{2,1,0:T(8,128)(2,1)}, bf16[3,248,256]{2,1,0:T(8,128)(2,1)S(1)}, u32[]{:S(2)}, u32[]{:S(2)}) collective-permute-start(bf16[3,248,256]{2,1,0:T(8,128)(2,1)} %get-tuple-element.53.refs_0_), channel_id=1, source_target_pairs={{0,16},{4,20},{8,24},{12,28},{16,0},{20,4},{24,8},{28,12},{1,17},{... | collective-permute-start | bytes 1142792 | tf_op jit(solution)/shard_map/ppermute | solution.py:1299
  43.2 26.8 %collective-permute-start = (bf16[512,1024]{1,0:T(8,128)(2,1)S(1)}, bf16[512,1024]{1,0:T(8,128)(2,1)S(1)}, u32[]{:S(2)}, u32[]{:S(2)}) collective-permute-start(bf16[512,1024]{1,0:T(8,128)(2,1)S(1)} %copy-done.6), channel_id=1, source_target_pairs={{0,2},{1,3},{2,0},{3,1},{4,6},{5,7},{6,4},{7,5},{8,10},{9,11},{10,... | collective-permute-start | bytes 3145736 | tf_op jit(solution)/shard_map/ppermute | solution.py:25
  61.0 9.0 %copy-start.8 = (bf16[3,248,256]{2,1,0:T(8,128)(2,1)}, bf16[3,248,256]{2,1,0:T(8,128)(2,1)S(1)}, u32[]{:S(2)}) copy-start(bf16[3,248,256]{2,1,0:T(8,128)(2,1)S(1)} %collective-permute-done.1.refs_1_) | copy-start | bytes 1142788
  69.9 0.7 copy-start.9
  70.0 1.1 copy-start.7
  157.7 12.3 %collective-permute-start.3 = (bf16[1728,128]{1,0:T(8,128)(2,1)}, bf16[1728,128]{1,0:T(8,128)(2,1)S(1)}, u32[]{:S(2)}, u32[]{:S(2)}) collective-permute-start(bf16[1728,128]{1,0:T(8,128)(2,1)} %get-tuple-element.59), channel_id=1, source_target_pairs={{0,4},{4,0},{8,12},{12,8},{16,20},{20,16},{24,28},{28,24},{1,5},{5... | collective-permute-start | bytes 1327112 | tf_op jit(solution)/shard_map/ppermute | solution.py:25
  158.3 47.1 %collective-permute-start.7 = (bf16[640,1024]{1,0:T(8,128)(2,1)}, bf16[640,1024]{1,0:T(8,128)(2,1)S(1)}, u32[]{:S(2)}, u32[]{:S(2)}) collective-permute-start(bf16[640,1024]{1,0:T(8,128)(2,1)} %get-tuple-element.63), channel_id=1, source_target_pairs={{0,2},{1,3},{2,0},{3,1},{4,6},{5,7},{6,4},{7,5},{8,10},{9,11},{10,... | collective-permute-start | bytes 3932168 | tf_op jit(solution)/shard_map/ppermute | solution.py:25
  159.7 46.4 %collective-permute-start.4 = (bf16[2,704,128]{2,1,0:T(8,128)(2,1)}, bf16[2,704,128]{2,1,0:T(8,128)(2,1)S(1)}, u32[]{:S(2)}, u32[]{:S(2)}) collective-permute-start(bf16[2,704,128]{2,1,0:T(8,128)(2,1)} %get-tuple-element.60), channel_id=1, source_target_pairs={{0,8},{4,12},{8,16},{12,20},{16,24},{20,28},{24,0},{28,4},{1,9},{5... | collective-permute-start | bytes 1081352 | tf_op jit(solution)/shard_map/ppermute | solution.py:1299
  165.3 40.9 %collective-permute-start.5 = (bf16[2,704,128]{2,1,0:T(8,128)(2,1)}, bf16[2,704,128]{2,1,0:T(8,128)(2,1)S(1)}, u32[]{:S(2)}, u32[]{:S(2)}) collective-permute-start(bf16[2,704,128]{2,1,0:T(8,128)(2,1)} %get-tuple-element.61), channel_id=1, source_target_pairs={{0,16},{4,20},{8,24},{12,28},{16,0},{20,4},{24,8},{28,12},{1,17},{... | collective-permute-start | bytes 1081352 | tf_op jit(solution)/shard_map/ppermute | solution.py:1299
  165.7 40.5 %collective-permute-start.6 = (bf16[2,704,128]{2,1,0:T(8,128)(2,1)}, bf16[2,704,128]{2,1,0:T(8,128)(2,1)S(1)}, u32[]{:S(2)}, u32[]{:S(2)}) collective-permute-start(bf16[2,704,128]{2,1,0:T(8,128)(2,1)} %get-tuple-element.62), channel_id=1, source_target_pairs={{0,24},{4,28},{8,0},{12,4},{16,8},{20,12},{24,16},{28,20},{1,25},{... | collective-permute-start | bytes 1081352 | tf_op jit(solution)/shard_map/ppermute | solution.py:1299
  170.0 36.1 %collective-permute-start.8 = (bf16[4,128,256]{2,1,0:T(8,128)(2,1)}, bf16[4,128,256]{2,1,0:T(8,128)(2,1)S(1)}, u32[]{:S(2)}, u32[]{:S(2)}) collective-permute-start(bf16[4,128,256]{2,1,0:T(8,128)(2,1)} %get-tuple-element.65), channel_id=1, source_target_pairs={{0,6},{1,7},{2,4},{3,5},{4,2},{5,3},{6,0},{7,1},{8,14},{9,15},{10,... | collective-permute-start | bytes 786440 | tf_op jit(solution)/shard_map/ppermute | solution.py:1320
  171.6 34.6 %copy-start.3 = (bf16[2,704,128]{2,1,0:T(8,128)(2,1)S(1)}, bf16[2,704,128]{2,1,0:T(8,128)(2,1)}, u32[]{:S(2)}) copy-start(bf16[2,704,128]{2,1,0:T(8,128)(2,1)} %get-tuple-element.79) | copy-start | bytes 1081348
  206.1 1.1 copy-start.10
  207.3 53.3 %copy-start.4 = (bf16[704,128]{1,0:T(8,128)(2,1)S(1)}, bf16[704,128]{1,0:T(8,128)(2,1)}, u32[]{:S(2)}) copy-start(bf16[704,128]{1,0:T(8,128)(2,1)} %get-tuple-element.83) | copy-start | bytes 540676
  207.3 54.1 %copy-start = (f32[512,1024]{1,0:T(8,128)S(1)}, f32[512,1024]{1,0:T(8,128)}, u32[]{:S(2)}) copy-start(f32[512,1024]{1,0:T(8,128)} %get-tuple-element.54) | copy-start | bytes 6291460
  261.4 2.0 copy-start.1
  263.3 1.3 copy-start.2
  263.3 2.1 copy-start.5

commit v6 on v5

--- a/solution.py
+++ b/solution.py
@@ -557,11 +557,11 @@
     early = half // 2 + 1
     table_ins, refs = refs[:early], refs[early:]
     rest_out, fardown_out, grad_out, gain_out, keep_out, send_out = refs[:6]
-    osums, gh_out, table_ref = refs[6:10], refs[10], refs[11]
-    piece_refs, refs = refs[12 : 12 + half], refs[12 + half :]
+    ostay_out, oaway_out, gh_out, table_ref = refs[6:10]
+    piece_refs, refs = refs[10 : 10 + half], refs[10 + half :]
     (
         rest_ref, grad_ref, wo_ref, c0, c1, c2, c3, x_ref,
-        ps_ref, pr_ref, ofar_ref, n_ref, wg_ref, wu_ref, wd_ref, act_ref, gg_ref, gu_ref,
+        ps_ref, pr_ref, n_ref, wg_ref, wu_ref, wd_ref, act_ref, gg_ref, gu_ref,
         g0_ref, g1s_ref, g1r_ref, d0_ref, d1s_ref, d1r_ref,
         ys_ref, yr_ref, all_ref, gh_ref,
         stay_ref, away_ref, got_ref, up_ref, upgot_ref,
@@ -861,29 +861,10 @@
     for n, block in enumerate((farsib, sib)):
         ps_ref[n] = out_part(block).astype(BF)
         out_sib(n).start()
-    full_ref = wo_ref.at[0]
-    width = full_ref.shape[1]
-    ofar_home = pltpu.make_async_copy(ofar_ref, fardown_out.at[rows:], wloc.at[3])
-    for n, (block, outs) in enumerate(((far, osums[2:]), (me, osums[:2]))):
+    for n, (block, out) in enumerate(((far, oaway_out), (me, ostay_out))):
         total = out_part(block)
         out_sib(n).wait_recv()
-        full_ref[...] = (total + pr_ref[n].astype(F32)).astype(BF).T
-        for j in range(half):
-            b = lax.rem(place + j, half)
-            for side, (which, out) in enumerate(zip((parity, 1 - parity), outs)):
-                part = full_ref[pl.ds(pl.multiple_of((2 * b + which) * piece, piece), piece)]
-                if n == 0 and side == 0:
-                    beside = model // width
-                    at, lane = j // beside * piece, j % beside * width
-                    ofar_ref[at : at + piece, lane : lane + width] = part
-                elif n == 1 and side == 1 and piece == 128:
-                    for m in range(width // piece):
-                        at = units + (j * (width // piece) + m) * piece
-                        send_out[at : at + piece] = part[:, m * piece : (m + 1) * piece]
-                else:
-                    out[j] = part
-        if n == 0:
-            ofar_home.start()
+        out[...] = (total + pr_ref[n].astype(F32)).astype(BF).T
 
     for j in range(half):
         b = lax.rem(place + j, half)
@@ -900,10 +881,7 @@
     for j in range(1, half):
         up_away(j).wait_recv()
     keep_out[...] = up_sum(parity)
-    if piece == 128:
-        send_out[:units] = up_sum(1 - parity)
-    else:
-        send_out[...] = up_sum(1 - parity)
+    send_out[...] = up_sum(1 - parity)
 
     def close(k):
         grad_home(k).wait()
@@ -919,7 +897,6 @@
     for m in range(2):
         for made in (back_a, down_three, cot_one, cot_three):
             made(m).wait_send()
-    ofar_home.wait()
     for copy in (out_sib(0), out_sib(1)):
         copy.wait_send()
     for j in range(early):
@@ -946,9 +923,6 @@
     units = weights[0].shape[0]
     wide = units + -units % 256
     block = (units, piece) if piece % 128 == 0 else (piece, units)
-    width = heads_out.shape[2]
-    tall = half * piece * width // model
-    joined = (units + half * width, piece) if piece == 128 else block
     dma = pltpu.SemaphoreType.DMA
     shape = jax.ShapeDtypeStruct
     vm = pltpu.VMEM
@@ -956,17 +930,16 @@
     return pl.pallas_call(
         functools.partial(middle_kernel, seq_count),
         in_specs=[ANY] * 3 + [VM] + [ANY] * (5 + len(tables)),
-        out_specs=[ANY] * 3 + [VM] * 7 + [ANY] * 2 + [VM] * half,
+        out_specs=[ANY] * 3 + [VM] * 5 + [ANY] * 2 + [VM] * half,
         out_shape=[
             shape((rows, model), F32),
-            shape((rows + tall, model), BF),
+            shape((rows, model), BF),
             shape((rows, model), F32),
             shape((1, model), F32),
             shape(block, BF),
-            shape(joined, BF),
-        ]
-        + [shape((half, piece, heads_out.shape[2]), BF)] * 4
-        + [
+            shape(block, BF),
+            shape((model, heads_out.shape[2]), BF),
+            shape((model, heads_out.shape[2]), BF),
             shape(heads_out.shape, BF),
             shape((2, half, 2) + tables[0].shape, BF),
         ]
@@ -975,7 +948,6 @@
         + [vm(wo.shape, BF)]
         + [rows_bf] * 5
         + [vm((2, wo.shape[2], model), BF)] * 2
-        + [vm((tall, model), BF)]
         + [vm((4, rows, model), BF)]
         + [vm((wide, model), BF)] * 3
         + [vm((wide, 4 * rows), BF)] * 3
@@ -996,11 +968,11 @@
 
 
 def last_kernel(
-    seq_count, mixed_in, w_in, x_in, gain_ref, grad_in, n_in, o0, o1, o2, o3, gain_in,
+    seq_count, mixed_in, w_in, x_in, gain_ref, grad_in, n_in, ostay_in, ogot_in, gain_in,
     out_out, wqkv_ref, wout_ref, gains_ref,
-    mixed_ref, w_ref, x_ref, grad_ref, n_ref, osum_ref, oz_ref,
+    mixed_ref, w_ref, x_ref, grad_ref, n_ref, ostay_ref, ogot_ref,
     as_ref, ar_ref, ys_ref, yr_ref, bs_ref, br_ref, dw_ref, got_ref, sum_ref, zr_ref, gs_ref, gr_ref,
-    snd, rcv, xsnd, xrcv, zsnd, zrcv, gsnd, grcv, osnd, orcv, loc,
+    snd, rcv, xsnd, xrcv, zsnd, zrcv, gsnd, grcv, loc,
 ):
     me, sib, far, farsib, core = places()
     seq = lax.axis_index("seq")
@@ -1010,7 +982,8 @@
         pltpu.make_async_copy(src, dst, loc.at[n])
         for n, (src, dst) in enumerate(
             (
-                (mixed_in, mixed_ref), (n_in, n_ref), (w_in, w_ref), (x_in, x_ref), (grad_in, grad_ref),
+                (mixed_in, mixed_ref), (n_in, n_ref), (ostay_in, ostay_ref),
+                (ogot_in, ogot_ref), (w_in, w_ref), (x_in, x_ref), (grad_in, grad_ref),
             )
         )
     ]
@@ -1076,60 +1049,42 @@
         for r in range(4):
             term = dot_tn(n_ref[r, :, cols], mixed_ref[r])
             total = term if total is None else total + term
-        tile = total.astype(BF).reshape(per, 2, piece, wide)
-        for j in range(per):
-            b = k * per + j
-
-            @pl.when(parity == 0)
-            def _():
-                dw_ref[0, b] = tile[j, 0]
-                dw_ref[1, b] = tile[j, 1]
-
-            @pl.when(parity == 1)
-            def _():
-                dw_ref[0, b] = tile[j, 1]
-                dw_ref[1, b] = tile[j, 0]
+        to_out = ostay_ref[cols].astype(F32) + ogot_ref[cols].astype(F32)
+        for lanes, value in ((slice(0, wide), total), (slice(wide, wide + width), to_out)):
+            tile = value.astype(BF).reshape(per, 2, piece, value.shape[1])
+            for j in range(per):
+                b = k * per + j
+
+                @pl.when(parity == 0)
+                def _():
+                    dw_ref[0, b, :, lanes] = tile[j, 0]
+                    dw_ref[1, b, :, lanes] = tile[j, 1]
+
+                @pl.when(parity == 1)
+                def _():
+                    dw_ref[0, b, :, lanes] = tile[j, 1]
+                    dw_ref[1, b, :, lanes] = tile[j, 0]
 
         for j in range(per):
             near_copy(k * per + j).start()
 
-    def out_copy(j):
-        return push(
-            osum_ref.at[j], oz_ref.at[j], osnd.at[j], orcv.at[j], (lax.rem(seq + 2 * j, seq_count), me)
-        )
-
-    def add(j):
-        beside = model // width
-        at, lane = j // beside * piece, j % beside * width
-        parts = [o0[j], o2[at : at + piece, lane : lane + width], o3[j]]
-        if piece == 128:
-            count = width // piece
-            rows_of = lambda m: slice((j * count + m) * piece, (j * count + m + 1) * piece)
-            parts.append(jnp.concatenate([o1[rows_of(m)] for m in range(count)], axis=1))
-        else:
-            parts.append(o1[j])
-        return sum(part.astype(F32) for part in parts)
-
-    for j in range(1, half):
-        osum_ref[j] = add(j).astype(BF)
-        out_copy(j).start()
-    for load in loads[:2]:
+    for load in loads[:4]:
         load.wait()
     weights_step(0)
-    loads[2].wait()
+    loads[4].wait()
     each(send_three, STEPS)
     weights_step(1)
     each(send_two, STEPS)
     each(lambda k: weights_step(k + 2), STEPS - 2)
     each(send_one, STEPS)
-    for load in loads[3:]:
+    for load in loads[5:]:
         load.wait()
 
     gs_ref[...] = jnp.zeros_like(gs_ref)
 
     def leave(k):
         part = chunk(k, size)
-        return pltpu.make_async_copy(grad_ref.at[part], out_out.at[part], loc.at[5 + k])
+        return pltpu.make_async_copy(grad_ref.at[part], out_out.at[part], loc.at[7 + k])
 
     def own_chunk(k):
         part = chunk(k, size)
@@ -1193,11 +1148,7 @@
         total = total + zr_ref[j].astype(F32)
     for c in range(3):
         wqkv_ref[c] = total[:, c * width : (c + 1) * width]
-    out_total = add(0)
-    for j in range(1, half):
-        out_copy(j).wait_recv()
-        out_total = out_total + oz_ref[j].astype(F32)
-    wout_ref[...] = out_total
+    wout_ref[...] = total[:, wide:]
 
     def close(k):
         for made in (back_a, back_y, back_b):
@@ -1211,10 +1162,9 @@
             gain_copy(stage, n).wait_send()
     for j in range(1, half):
         level_copy(j).wait_send()
-        out_copy(j).wait_send()
-
-
-def last_call(mixed, w, x, gain, grad, normed, outs, gain_two):
+
+
+def last_call(mixed, w, x, gain, grad, normed, out_stay, out_got, gain_two):
     seq_count = lax.axis_size("seq")
     rows, model = x.shape
     half = seq_count // 2
@@ -1223,10 +1173,10 @@
     dma = pltpu.SemaphoreType.DMA
     shape = jax.ShapeDtypeStruct
     rows_bf = pltpu.VMEM((rows, model), BF)
-    pieces = pltpu.VMEM((half, piece, wide), BF)
+    pieces = pltpu.VMEM((half, piece, wide + width), BF)
     return pl.pallas_call(
         functools.partial(last_kernel, seq_count),
-        in_specs=[ANY] * 3 + [VM] + [ANY] * 2 + [VM] * 5,
+        in_specs=[ANY] * 3 + [VM] + [ANY] * 4 + [VM],
         out_specs=[ANY] + [VM] * 3,
         out_shape=[
             shape((rows, model), F32),
@@ -1235,10 +1185,10 @@
             shape((8, model), F32),
         ],
         scratch_shapes=[
-            pltpu.VMEM(a.shape, a.dtype) for a in (mixed, w, x, grad, normed, outs[0], outs[0])
+            pltpu.VMEM(a.shape, a.dtype) for a in (mixed, w, x, grad, normed, out_stay, out_got)
         ]
         + [rows_bf] * 6
-        + [pltpu.VMEM((2, half, piece, wide), BF), pieces, pieces, pieces]
+        + [pltpu.VMEM((2, half, piece, wide + width), BF), pieces, pieces, pieces]
         + [pltpu.VMEM((2, 8, model), F32), pltpu.VMEM((seq_count + 2, 8, model), F32)]
         + [
             dma((3, STEPS)),
@@ -1249,14 +1199,12 @@
             dma((half,)),
             dma((seq_count + 2,)),
             dma((seq_count + 2,)),
-            dma((half,)),
-            dma((half,)),
-            dma((5 + STEPS,)),
+            dma((7 + STEPS,)),
         ],
         compiler_params=params(collective_id=2, has_side_effects=True),
         cost_estimate=cost(90_000_000_000, 30_000_000),
         name="last",
-    )(mixed, w, x, gain, grad, normed, *outs, gain_two)
+    )(mixed, w, x, gain, grad, normed, out_stay, out_got, gain_two)
 
 
 def shards(
@@ -1304,38 +1252,32 @@
     heads_out, lse = attend_call(sc, qkv)
     heads_four = heads_out.reshape(4, local_rows, local_width)
     (
-        rest, far_down, grad_hidden, gain_two_part, up_keep, up_send, out_own, out_near,
-        out_far, out_cross, grad_heads, hash_parts, *pieces,
+        rest, far_down, grad_hidden, gain_two_part, up_keep, up_send, out_stay, out_away,
+        grad_heads, hash_parts, *pieces,
     ) = middle_call(
         heads_four, wo_all, latents_in, gain_two, cotangent, cot_far,
         (w_gate.T, w_up.T, w_down.T), table_parts,
     )
+    out_got = flip(out_away, "tp", 2)
     down_far = flip(far_down, "tp", 2)
     up_got = flip(up_send, "seq", 1)
-    cross = [(4 * s + t, 4 * (s ^ 1) + (t ^ 2)) for s in range(seq_count) for t in range(4)]
-    out_parts = [
-        out_own,
-        up_got[units:] if piece == 128 else flip(out_near, "seq", 1),
-        down_far[local_rows:],
-        lax.ppermute(out_cross, ("seq", "tp"), cross),
-    ]
     arrived = [level_flip(pieces[j], j) for j in range(1, seq_count // 2)]
     hash_parts = hash_parts.reshape(2, seq_count // 2, hash_ids.shape[0], high_rows, LANES)
     mixed, hash_counts = attend_back_call(
         sc, grad_heads.reshape(group_rows, local_width), qkv, heads_out, lse, hash_parts, HASH_ROWS
     )
-    mixed, up_got, arrived, down_far, out_parts = lax.optimization_barrier(
-        (mixed, up_got, arrived, down_far, out_parts)
+    mixed, up_got, arrived, down_far, out_got = lax.optimization_barrier(
+        (mixed, up_got, arrived, down_far, out_got)
     )
     grad_latents, qkv_total, out_total, gains = last_call(
         mixed.reshape(4, local_rows, -1), qkv_weight, latents_in, gain_one, grad_hidden,
-        normed, out_parts, gain_two_part,
+        normed, out_stay, out_got, gain_two_part,
     )
     total = pieces[0].astype(F32)
-    for part in arrived:
-        total = total + part.astype(F32)
-    up_total = up_keep.astype(F32) + (up_got[:units] if piece == 128 else up_got).astype(F32)
-    latents_out = (rest + down_far[:local_rows].astype(F32)).astype(BF)
+    for piece in arrived:
+        total = total + piece.astype(F32)
+    up_total = up_keep.astype(F32) + up_got.astype(F32)
+    latents_out = (rest + down_far.astype(F32)).astype(BF)
     upright = lambda w: w.T if w.shape[0] == units else w
     return (
         latents_out,

time: 266 us -> 260 us (0.977)
  waiting for transfers between devices: 11.4 us -> 8.74 us
    unnamed x25 -> x29, local copies, waits for them, and re-layouts: 4.49 us -> 5.37 us
  transfers between devices with their start and end apart: 9 -> 9, of which waited for: 2 -> 2; matrix products, arithmetic and copies ran while one was open for 1% -> 0% of each run, Pallas kernels for 19% -> 19%
where the time goes in v6:
time: 260 us
  Pallas kernels  227 us (87%)
  starting transfers between devices  12.9 us (5%)
  waiting for transfers between devices  8.74 us (3%)
  local copies, waits for them, and re-layouts  7.8 us (3%)
    pallas_call x1, Pallas kernels, middle_call(): pl.pallas_call(functools.partial(middle_kernel, seq_count), in_specs=[ANY...  86.6 us
    pallas_call x1, Pallas kernels, last_call(): pl.pallas_call(functools.partial(last_kernel, seq_count), in_specs=[ANY]...  49.9 us
    pallas_call x1, Pallas kernels, front_call(): pl.pallas_call(functools.partial(front_kernel, seq_count), in_specs=[VM]...  40.2 us
    pallas_call x1, Pallas kernels, attend_back_call(): pl.pallas_call(functools.partial(attend_back_kernel, heads), grid_spec=pl...  33 us
    pallas_call x1, Pallas kernels, attend_call(): pl.pallas_call(functools.partial(attend_kernel, heads), grid_spec=pltpu.P...  17.3 us
    ppermute x5, starting transfers between devices, level_flip(): lax.ppermute(x, 'seq', [(s, (s + 2 * j) % seq_count) for s in range(seq_c...  9.82 us
    ppermute x5, waiting for transfers between devices, level_flip(): lax.ppermute(x, 'seq', [(s, (s + 2 * j) % seq_count) for s in range(seq_c...  8.67 us
    unnamed x29, local copies, waits for them, and re-layouts  5.37 us
  transfers between devices with their start and end apart: 9, of which 2 were waited for; matrix products, arithmetic and copies ran while one was open for 0% of the time, Pallas kernels for 19%

profile of v6, /device:TPU:0, one launch (start us, length us, event | category | flops | bytes accessed | tf_op | source)
XLA Modules:
  0.0 259.5 jit_solution(6064364409055364024)
XLA Ops:
  0.7 40.2 %front.1 = (bf16[4,512,1024]{2,1,0:T(8,128)(2,1)}, bf16[4,512,768]{2,1,0:T(8,128)(2,1)}, bf16[3,248,256]{2,1,0:T(8,128)(2,1)}, bf16[4,4,2,128,256]{4,3,2,1,0:T(8,128)(2,1)}) custom-call(bf16[512,1024]{1,0:T(8,128)(2,1)} %x_in.3, f32[1,1024]{1,0:T(1,128)} %bitcast.33, bf16[3,1024,256]{2,1,0:T(8,128)(2,1)} %bitcast.29, s32[6,512]{1,0:T(8,128)} %ids_ref.1, ...), custom_call_target="tpu_custom_call" | custom-call | flops 1000000 | bytes 1000000 | tf_op jit(solution)/shard_map/front/pallas_call | solution.py:282
  40.8 0.6 collective-permute-start.2
  41.5 1.5 collective-permute-start.1
  43.0 0.5 collective-permute-start
  43.5 17.3 %attend.1 = (bf16[2048,256]{1,0:T(8,128)(2,1)}, f32[8,2048]{1,0:T(8,128)}) custom-call(s32[1]{0:T(128)} %bitcast.rank, s32[3]{0:T(128)} %bitcast.44, s32[3]{0:T(128)} %bitcast.46, bf16[2048,768]{1,0:T(8,128)(2,1)} %bitcast.37), custom_call_target="tpu_custom_call" | custom-call | flops 60000002048 | bytes 8000000 | tf_op jit(solution)/shard_map/attend/pallas_call | solution.py:384
  60.8 8.7 %collective-permute-done.2.refs_2_ = bf16[3,248,256]{2,1,0:T(8,128)(2,1)S(1)} collective-permute-done((bf16[3,248,256]{2,1,0:T(8,128)(2,1)}, bf16[3,248,256]{2,1,0:T(8,128)(2,1)S(1)}, u32[]{:S(2)}, u32[]{:S(2)}) %collective-permute-start.2) | collective-permute-done | bytes 380960 | tf_op jit(solution)/shard_map/ppermute | solution.py:1247
  69.5 0.7 copy-done.11
  70.7 86.6 %middle.1 = (f32[512,1024]{1,0:T(8,128)}, bf16[512,1024]{1,0:T(8,128)(2,1)}, f32[512,1024]{1,0:T(8,128)}, f32[1,1024]{1,0:T(1,128)}, bf16[704,128]{1,0:T(8,128)(...) custom-call(bf16[4,512,256]{2,1,0:T(8,128)(2,1)} %bitcast.50, ...), custom_call_target="tpu_custom_call" | custom-call | flops 99999997952 | bytes 30000000 | tf_op jit(solution)/shard_map/middle/pallas_call | solution.py:930
  157.3 0.6 collective-permute-start.3
  157.9 5.3 %collective-permute-start.4 = (bf16[2,704,128]{2,1,0:T(8,128)(2,1)}, bf16[2,704,128]{2,1,0:T(8,128)(2,1)S(1)}, u32[]{:S(2)}, u32[]{:S(2)}) collective-permute-start(bf16[2,704,128]{2,1,0:T(8,128)(2,1)} %get-tuple-element.57), channel_id=1, source_target_pairs={{0,8},{4,12},{8,16},{12,20},{16,24},{20,28},{24,0},{28,4},{1,9},{5... | collective-permute-start | bytes 1081352 | tf_op jit(solution)/shard_map/ppermute | solution.py:1247
  163.6 1.9 collective-permute-start.6
  165.6 1.6 collective-permute-start.8
  167.1 0.7 copy-done.5
  167.8 0.5 collective-permute-start.7
  168.3 33.0 %attend_back.1 = (bf16[2048,768]{1,0:T(8,128)(2,1)}, f32[6,500002]{1,0:T(8,128)}) custom-call(s32[1]{0:T(128)} %bitcast.rank, s32[3]{0:T(128)} %bitcast.45, s32[3]{0:T(128)} %bitcast.47, bf16[2048,256]{1,0:T(8,128)(2,1)} %bitcast.51, bf16[2048,768]{1,0:T(8,128)(2,1)} %bitcast.38, bf16[2048,256]{1,0:T(8,128)(2,1)} %get-tuple-element.47.heads_ref, ...), custom_call_target="tpu_custom_call" | custom-call | flops 89999998976 | bytes 12000000 | tf_op jit(solution)/shard_map/attend_back/pallas_call | solution.py:513
  201.3 0.7 copy-done.10
  202.1 49.9 %last.1 = (f32[512,1024]{1,0:T(8,128)}, f32[3,128,256]{2,1,0:T(8,128)}, f32[128,256]{1,0:T(8,128)}, f32[8,1024]{1,0:T(8,128)}) custom-call(bf16[4,512,768]{2,1,0:T(8,128)(2,1)} %bitcast.49, bf16[3,1024,256]{2,1,0:T(8,128)(2,1)} %bitcast.30, bf16[512,1024]{1,0:T(8,128)(2,1)} %x_in.3, f32[1,1024]{1,0:T(1,128)} %bitcast.34, ...), custom_call_target="tpu_custom_call" | custom-call | flops 89999998976 | bytes 30000000 | tf_op jit(solution)/shard_map/last/pallas_call | solution.py:1177
  252.0 1.5 fusion
  253.7 0.9 slice_bitcast_fusion
  254.6 1.4 add_convert_fusion
  256.0 0.8 add_bitcast_fusion
  256.8 1.3 copy.26
  258.1 0.7 copy.27
  258.9 0.7 copy.28
  (33 shorter events, 1.2 us)
Async XLA Ops:
  0.6 42.4 %copy-start.8 = (bf16[512,1024]{1,0:T(8,128)(2,1)S(1)}, bf16[512,1024]{1,0:T(8,128)(2,1)}, u32[]{:S(2)}) copy-start(bf16[512,1024]{1,0:T(8,128)(2,1)} %c0_in.1) | copy-start | bytes 3145732
  40.8 28.7 %collective-permute-start.2 = (bf16[3,248,256]{2,1,0:T(8,128)(2,1)}, bf16[3,248,256]{2,1,0:T(8,128)(2,1)S(1)}, u32[]{:S(2)}, u32[]{:S(2)}) collective-permute-start(bf16[3,248,256]{2,1,0:T(8,128)(2,1)} %get-tuple-element.50.refs_0_), channel_id=1, source_target_pairs={{0,16},{4,20},{8,24},{12,28},{16,0},{20,4},{24,8},{28,12},{1,17},{... | collective-permute-start | bytes 1142792 | tf_op jit(solution)/shard_map/ppermute | solution.py:1247
  41.5 28.0 %collective-permute-start.1 = (bf16[3,248,256]{2,1,0:T(8,128)(2,1)}, bf16[3,248,256]{2,1,0:T(8,128)(2,1)S(1)}, u32[]{:S(2)}, u32[]{:S(2)}) collective-permute-start(bf16[3,248,256]{2,1,0:T(8,128)(2,1)} %get-tuple-element.50.refs_0_), channel_id=1, source_target_pairs={{0,8},{4,12},{8,16},{12,20},{16,24},{20,28},{24,0},{28,4},{1,9},{5... | collective-permute-start | bytes 1142792 | tf_op jit(solution)/shard_map/ppermute | solution.py:1247
  43.0 26.5 %collective-permute-start = (bf16[512,1024]{1,0:T(8,128)(2,1)S(1)}, bf16[512,1024]{1,0:T(8,128)(2,1)S(1)}, u32[]{:S(2)}, u32[]{:S(2)}) collective-permute-start(bf16[512,1024]{1,0:T(8,128)(2,1)S(1)} %copy-done.8), channel_id=1, source_target_pairs={{0,2},{1,3},{2,0},{3,1},{4,6},{5,7},{6,4},{7,5},{8,10},{9,11},{10,... | collective-permute-start | bytes 3145736 | tf_op jit(solution)/shard_map/ppermute | solution.py:25
  69.5 0.7 copy-start.11
  69.5 0.9 copy-start.12
  69.5 1.2 copy-start.9
  157.3 9.8 %collective-permute-start.3 = (bf16[704,128]{1,0:T(8,128)(2,1)}, bf16[704,128]{1,0:T(8,128)(2,1)S(1)}, u32[]{:S(2)}, u32[]{:S(2)}) collective-permute-start(bf16[704,128]{1,0:T(8,128)(2,1)} %get-tuple-element.56), channel_id=1, source_target_pairs={{0,4},{4,0},{8,12},{12,8},{16,20},{20,16},{24,28},{28,24},{1,5},{5... | collective-permute-start | bytes 540680 | tf_op jit(solution)/shard_map/ppermute | solution.py:25
  157.9 43.4 %collective-permute-start.4 = (bf16[2,704,128]{2,1,0:T(8,128)(2,1)}, bf16[2,704,128]{2,1,0:T(8,128)(2,1)S(1)}, u32[]{:S(2)}, u32[]{:S(2)}) collective-permute-start(bf16[2,704,128]{2,1,0:T(8,128)(2,1)} %get-tuple-element.57), channel_id=1, source_target_pairs={{0,8},{4,12},{8,16},{12,20},{16,24},{20,28},{24,0},{28,4},{1,9},{5... | collective-permute-start | bytes 1081352 | tf_op jit(solution)/shard_map/ppermute | solution.py:1247
  163.2 38.1 %collective-permute-start.5 = (bf16[2,704,128]{2,1,0:T(8,128)(2,1)}, bf16[2,704,128]{2,1,0:T(8,128)(2,1)S(1)}, u32[]{:S(2)}, u32[]{:S(2)}) collective-permute-start(bf16[2,704,128]{2,1,0:T(8,128)(2,1)} %get-tuple-element.58), channel_id=1, source_target_pairs={{0,16},{4,20},{8,24},{12,28},{16,0},{20,4},{24,8},{28,12},{1,17},{... | collective-permute-start | bytes 1081352 | tf_op jit(solution)/shard_map/ppermute | solution.py:1247
  163.6 37.6 %collective-permute-start.6 = (bf16[2,704,128]{2,1,0:T(8,128)(2,1)}, bf16[2,704,128]{2,1,0:T(8,128)(2,1)S(1)}, u32[]{:S(2)}, u32[]{:S(2)}) collective-permute-start(bf16[2,704,128]{2,1,0:T(8,128)(2,1)} %get-tuple-element.59), channel_id=1, source_target_pairs={{0,24},{4,28},{8,0},{12,4},{16,8},{20,12},{24,16},{28,20},{1,25},{... | collective-permute-start | bytes 1081352 | tf_op jit(solution)/shard_map/ppermute | solution.py:1247
  165.6 35.7 %collective-permute-start.8 = (bf16[1024,256]{1,0:T(8,128)(2,1)}, bf16[1024,256]{1,0:T(8,128)(2,1)S(1)}, u32[]{:S(2)}, u32[]{:S(2)}) collective-permute-start(bf16[1024,256]{1,0:T(8,128)(2,1)} %get-tuple-element.61), channel_id=1, source_target_pairs={{0,2},{1,3},{2,0},{3,1},{4,6},{5,7},{6,4},{7,5},{8,10},{9,11},{10,... | collective-permute-start | bytes 1572872 | tf_op jit(solution)/shard_map/ppermute | solution.py:25
  167.1 0.7 copy-start.5
  167.8 33.6 %collective-permute-start.7 = (bf16[512,1024]{1,0:T(8,128)(2,1)}, bf16[512,1024]{1,0:T(8,128)(2,1)S(1)}, u32[]{:S(2)}, u32[]{:S(2)}) collective-permute-start(bf16[512,1024]{1,0:T(8,128)(2,1)} %get-tuple-element.60), channel_id=1, source_target_pairs={{0,2},{1,3},{2,0},{3,1},{4,6},{5,7},{6,4},{7,5},{8,10},{9,11},{10,... | collective-permute-start | bytes 3145736 | tf_op jit(solution)/shard_map/ppermute | solution.py:25
  201.3 0.8 copy-start.10
  202.1 51.5 %copy-start.3 = (bf16[2,704,128]{2,1,0:T(8,128)(2,1)S(1)}, bf16[2,704,128]{2,1,0:T(8,128)(2,1)}, u32[]{:S(2)}) copy-start(bf16[2,704,128]{2,1,0:T(8,128)(2,1)} %get-tuple-element.73) | copy-start | bytes 1081348
  252.0 2.6 %copy-start = (f32[512,1024]{1,0:T(8,128)S(1)}, f32[512,1024]{1,0:T(8,128)}, u32[]{:S(2)}) copy-start(f32[512,1024]{1,0:T(8,128)} %get-tuple-element.51) | copy-start | bytes 6291460
  254.6 1.4 copy-start.4
  254.6 1.4 copy-start.6
  254.6 2.2 copy-start.1
  256.8 1.3 copy-start.2
  256.8 2.1 copy-start.7

commit v7 on v6

--- a/solution.py
+++ b/solution.py
@@ -410,6 +410,7 @@
 
 def spread(table_ref, out_ref, flat_ref):
     parities, levels, tables, high_rows, _ = table_ref.shape
+    unroll = next(u for u in (62, 32, 8) if high_rows % u == 0)
     for piece in range(parities * levels):
         p, q = piece % parities, piece // parities
         for n in range(tables):
@@ -419,14 +420,14 @@
                 ].astype(F32)
 
         def body(n, carry):
-            for u in range(8):
-                row = n * 8 + u
+            for u in range(unroll):
+                row = n * unroll + u
                 for side in range(2):
                     at = pl.multiple_of((piece * high_rows + row) * LANES + side * 128, 128)
                     out_ref[:, pl.ds(at, 128)] = flat_ref[side, pl.ds(row, tables, stride=high_rows)]
             return carry
 
-        lax.fori_loop(0, high_rows // 8, body, 0)
+        lax.fori_loop(0, high_rows // unroll, body, 0)
 
 
 def attend_back_kernel(

time: 260 us -> 259 us (level)
  no operation moved by 1% of the time
where the time goes in v7:
time: 259 us; the launch traced here: 260 us
  Pallas kernels  226 us (87%)
  starting transfers between devices  12.9 us (5%)
  waiting for transfers between devices  10.4 us (4%)
  local copies, waits for them, and re-layouts  7.07 us (3%)
    pallas_call x1, Pallas kernels, middle_call(): pl.pallas_call(functools.partial(middle_kernel, seq_count), in_specs=[ANY...  86.6 us
    pallas_call x1, Pallas kernels, last_call(): pl.pallas_call(functools.partial(last_kernel, seq_count), in_specs=[ANY]...  50.7 us
    pallas_call x1, Pallas kernels, front_call(): pl.pallas_call(functools.partial(front_kernel, seq_count), in_specs=[VM]...  40.2 us
    pallas_call x1, Pallas kernels, attend_back_call(): pl.pallas_call(functools.partial(attend_back_kernel, heads), grid_spec=pl...  31.3 us
    pallas_call x1, Pallas kernels, attend_call(): pl.pallas_call(functools.partial(attend_kernel, heads), grid_spec=pltpu.P...  17.3 us
    ppermute x5, starting transfers between devices, level_flip(): lax.ppermute(x, 'seq', [(s, (s + 2 * j) % seq_count) for s in range(seq_c...  9.82 us
    ppermute x5, waiting for transfers between devices, level_flip(): lax.ppermute(x, 'seq', [(s, (s + 2 * j) % seq_count) for s in range(seq_c...  8.67 us
  transfers between devices with their start and end apart: 9, of which 2 were waited for; matrix products, arithmetic and copies ran while one was open for 0% of the time, Pallas kernels for 19%

profile of v7, /device:TPU:0, one launch (start us, length us, event | category | flops | bytes accessed | tf_op | source)
XLA Modules:
  0.0 259.6 jit_solution(18336917959644326469)
XLA Ops:
  0.7 40.2 %front.1 = (bf16[4,512,1024]{2,1,0:T(8,128)(2,1)}, bf16[4,512,768]{2,1,0:T(8,128)(2,1)}, bf16[3,248,256]{2,1,0:T(8,128)(2,1)}, bf16[4,4,2,128,256]{4,3,2,1,0:T(8,128)(2,1)}) custom-call(bf16[512,1024]{1,0:T(8,128)(2,1)} %x_in.3, f32[1,1024]{1,0:T(1,128)} %bitcast.33, bf16[3,1024,256]{2,1,0:T(8,128)(2,1)} %bitcast.29, s32[6,512]{1,0:T(8,128)} %ids_ref.1, ...), custom_call_target="tpu_custom_call" | custom-call | flops 1000000 | bytes 1000000 | tf_op jit(solution)/shard_map/front/pallas_call | solution.py:282
  40.8 0.6 collective-permute-start.2
  41.5 1.5 collective-permute-start.1
  43.0 0.5 collective-permute-start
  43.5 17.3 %attend.1 = (bf16[2048,256]{1,0:T(8,128)(2,1)}, f32[8,2048]{1,0:T(8,128)}) custom-call(s32[1]{0:T(128)} %bitcast.rank, s32[3]{0:T(128)} %bitcast.44, s32[3]{0:T(128)} %bitcast.46, bf16[2048,768]{1,0:T(8,128)(2,1)} %bitcast.37), custom_call_target="tpu_custom_call" | custom-call | flops 60000002048 | bytes 8000000 | tf_op jit(solution)/shard_map/attend/pallas_call | solution.py:384
  60.8 8.7 %collective-permute-done.2.refs_2_ = bf16[3,248,256]{2,1,0:T(8,128)(2,1)S(1)} collective-permute-done((bf16[3,248,256]{2,1,0:T(8,128)(2,1)}, bf16[3,248,256]{2,1,0:T(8,128)(2,1)S(1)}, u32[]{:S(2)}, u32[]{:S(2)}) %collective-permute-start.2) | collective-permute-done | bytes 380960 | tf_op jit(solution)/shard_map/ppermute | solution.py:1248
  69.5 0.7 copy-done.11
  70.7 86.6 %middle.1 = (f32[512,1024]{1,0:T(8,128)}, bf16[512,1024]{1,0:T(8,128)(2,1)}, f32[512,1024]{1,0:T(8,128)}, f32[1,1024]{1,0:T(1,128)}, bf16[704,128]{1,0:T(8,128)(...) custom-call(bf16[4,512,256]{2,1,0:T(8,128)(2,1)} %bitcast.50, ...), custom_call_target="tpu_custom_call" | custom-call | flops 99999997952 | bytes 30000000 | tf_op jit(solution)/shard_map/middle/pallas_call | solution.py:931
  157.3 0.6 collective-permute-start.3
  157.9 5.3 %collective-permute-start.4 = (bf16[2,704,128]{2,1,0:T(8,128)(2,1)}, bf16[2,704,128]{2,1,0:T(8,128)(2,1)S(1)}, u32[]{:S(2)}, u32[]{:S(2)}) collective-permute-start(bf16[2,704,128]{2,1,0:T(8,128)(2,1)} %get-tuple-element.57), channel_id=1, source_target_pairs={{0,8},{4,12},{8,16},{12,20},{16,24},{20,28},{24,0},{28,4},{1,9},{5... | collective-permute-start | bytes 1081352 | tf_op jit(solution)/shard_map/ppermute | solution.py:1248
  163.6 1.9 collective-permute-start.6
  165.6 1.6 collective-permute-start.8
  167.1 0.7 copy-done.5
  167.8 0.5 collective-permute-start.7
  168.3 31.3 %attend_back.1 = (bf16[2048,768]{1,0:T(8,128)(2,1)}, f32[6,500002]{1,0:T(8,128)}) custom-call(s32[1]{0:T(128)} %bitcast.rank, s32[3]{0:T(128)} %bitcast.45, s32[3]{0:T(128)} %bitcast.47, bf16[2048,256]{1,0:T(8,128)(2,1)} %bitcast.51, bf16[2048,768]{1,0:T(8,128)(2,1)} %bitcast.38, bf16[2048,256]{1,0:T(8,128)(2,1)} %get-tuple-element.47.heads_ref, ...), custom_call_target="tpu_custom_call" | custom-call | flops 89999998976 | bytes 12000000 | tf_op jit(solution)/shard_map/attend_back/pallas_call | solution.py:514
  199.6 1.7 collective-permute-done.7
  201.3 50.7 %last.1 = (f32[512,1024]{1,0:T(8,128)}, f32[3,128,256]{2,1,0:T(8,128)}, f32[128,256]{1,0:T(8,128)}, f32[8,1024]{1,0:T(8,128)}) custom-call(bf16[4,512,768]{2,1,0:T(8,128)(2,1)} %bitcast.49, bf16[3,1024,256]{2,1,0:T(8,128)(2,1)} %bitcast.30, bf16[512,1024]{1,0:T(8,128)(2,1)} %x_in.3, f32[1,1024]{1,0:T(1,128)} %bitcast.34, ...), custom_call_target="tpu_custom_call" | custom-call | flops 89999998976 | bytes 30000000 | tf_op jit(solution)/shard_map/last/pallas_call | solution.py:1178
  252.1 1.5 fusion
  253.7 0.9 slice_bitcast_fusion
  254.7 1.4 add_convert_fusion
  256.0 0.8 add_bitcast_fusion
  256.8 1.3 copy.26
  258.2 0.7 copy.27
  258.9 0.7 copy.28
  (33 shorter events, 1.1 us)
Async XLA Ops:
  0.6 42.4 %copy-start.8 = (bf16[512,1024]{1,0:T(8,128)(2,1)S(1)}, bf16[512,1024]{1,0:T(8,128)(2,1)}, u32[]{:S(2)}) copy-start(bf16[512,1024]{1,0:T(8,128)(2,1)} %c0_in.1) | copy-start | bytes 3145732
  40.8 28.7 %collective-permute-start.2 = (bf16[3,248,256]{2,1,0:T(8,128)(2,1)}, bf16[3,248,256]{2,1,0:T(8,128)(2,1)S(1)}, u32[]{:S(2)}, u32[]{:S(2)}) collective-permute-start(bf16[3,248,256]{2,1,0:T(8,128)(2,1)} %get-tuple-element.50.refs_0_), channel_id=1, source_target_pairs={{0,16},{4,20},{8,24},{12,28},{16,0},{20,4},{24,8},{28,12},{1,17},{... | collective-permute-start | bytes 1142792 | tf_op jit(solution)/shard_map/ppermute | solution.py:1248
  41.5 28.0 %collective-permute-start.1 = (bf16[3,248,256]{2,1,0:T(8,128)(2,1)}, bf16[3,248,256]{2,1,0:T(8,128)(2,1)S(1)}, u32[]{:S(2)}, u32[]{:S(2)}) collective-permute-start(bf16[3,248,256]{2,1,0:T(8,128)(2,1)} %get-tuple-element.50.refs_0_), channel_id=1, source_target_pairs={{0,8},{4,12},{8,16},{12,20},{16,24},{20,28},{24,0},{28,4},{1,9},{5... | collective-permute-start | bytes 1142792 | tf_op jit(solution)/shard_map/ppermute | solution.py:1248
  43.0 26.5 %collective-permute-start = (bf16[512,1024]{1,0:T(8,128)(2,1)S(1)}, bf16[512,1024]{1,0:T(8,128)(2,1)S(1)}, u32[]{:S(2)}, u32[]{:S(2)}) collective-permute-start(bf16[512,1024]{1,0:T(8,128)(2,1)S(1)} %copy-done.8), channel_id=1, source_target_pairs={{0,2},{1,3},{2,0},{3,1},{4,6},{5,7},{6,4},{7,5},{8,10},{9,11},{10,... | collective-permute-start | bytes 3145736 | tf_op jit(solution)/shard_map/ppermute | solution.py:25
  69.5 0.7 copy-start.11
  69.5 0.9 copy-start.12
  69.5 1.2 copy-start.9
  157.3 9.8 %collective-permute-start.3 = (bf16[704,128]{1,0:T(8,128)(2,1)}, bf16[704,128]{1,0:T(8,128)(2,1)S(1)}, u32[]{:S(2)}, u32[]{:S(2)}) collective-permute-start(bf16[704,128]{1,0:T(8,128)(2,1)} %get-tuple-element.56), channel_id=1, source_target_pairs={{0,4},{4,0},{8,12},{12,8},{16,20},{20,16},{24,28},{28,24},{1,5},{5... | collective-permute-start | bytes 540680 | tf_op jit(solution)/shard_map/ppermute | solution.py:25
  157.9 41.7 %collective-permute-start.4 = (bf16[2,704,128]{2,1,0:T(8,128)(2,1)}, bf16[2,704,128]{2,1,0:T(8,128)(2,1)S(1)}, u32[]{:S(2)}, u32[]{:S(2)}) collective-permute-start(bf16[2,704,128]{2,1,0:T(8,128)(2,1)} %get-tuple-element.57), channel_id=1, source_target_pairs={{0,8},{4,12},{8,16},{12,20},{16,24},{20,28},{24,0},{28,4},{1,9},{5... | collective-permute-start | bytes 1081352 | tf_op jit(solution)/shard_map/ppermute | solution.py:1248
  163.2 36.4 %collective-permute-start.5 = (bf16[2,704,128]{2,1,0:T(8,128)(2,1)}, bf16[2,704,128]{2,1,0:T(8,128)(2,1)S(1)}, u32[]{:S(2)}, u32[]{:S(2)}) collective-permute-start(bf16[2,704,128]{2,1,0:T(8,128)(2,1)} %get-tuple-element.58), channel_id=1, source_target_pairs={{0,16},{4,20},{8,24},{12,28},{16,0},{20,4},{24,8},{28,12},{1,17},{... | collective-permute-start | bytes 1081352 | tf_op jit(solution)/shard_map/ppermute | solution.py:1248
  163.6 36.0 %collective-permute-start.6 = (bf16[2,704,128]{2,1,0:T(8,128)(2,1)}, bf16[2,704,128]{2,1,0:T(8,128)(2,1)S(1)}, u32[]{:S(2)}, u32[]{:S(2)}) collective-permute-start(bf16[2,704,128]{2,1,0:T(8,128)(2,1)} %get-tuple-element.59), channel_id=1, source_target_pairs={{0,24},{4,28},{8,0},{12,4},{16,8},{20,12},{24,16},{28,20},{1,25},{... | collective-permute-start | bytes 1081352 | tf_op jit(solution)/shard_map/ppermute | solution.py:1248
  165.6 34.0 %collective-permute-start.8 = (bf16[1024,256]{1,0:T(8,128)(2,1)}, bf16[1024,256]{1,0:T(8,128)(2,1)S(1)}, u32[]{:S(2)}, u32[]{:S(2)}) collective-permute-start(bf16[1024,256]{1,0:T(8,128)(2,1)} %get-tuple-element.61), channel_id=1, source_target_pairs={{0,2},{1,3},{2,0},{3,1},{4,6},{5,7},{6,4},{7,5},{8,10},{9,11},{10,... | collective-permute-start | bytes 1572872 | tf_op jit(solution)/shard_map/ppermute | solution.py:25
  167.1 0.7 copy-start.5
  167.8 33.6 %collective-permute-start.7 = (bf16[512,1024]{1,0:T(8,128)(2,1)}, bf16[512,1024]{1,0:T(8,128)(2,1)S(1)}, u32[]{:S(2)}, u32[]{:S(2)}) collective-permute-start(bf16[512,1024]{1,0:T(8,128)(2,1)} %get-tuple-element.60), channel_id=1, source_target_pairs={{0,2},{1,3},{2,0},{3,1},{4,6},{5,7},{6,4},{7,5},{8,10},{9,11},{10,... | collective-permute-start | bytes 3145736 | tf_op jit(solution)/shard_map/ppermute | solution.py:25
  199.6 1.7 copy-start.10
  201.3 52.2 %copy-start.3 = (bf16[2,704,128]{2,1,0:T(8,128)(2,1)S(1)}, bf16[2,704,128]{2,1,0:T(8,128)(2,1)}, u32[]{:S(2)}) copy-start(bf16[2,704,128]{2,1,0:T(8,128)(2,1)} %get-tuple-element.73) | copy-start | bytes 1081348
  252.0 2.6 %copy-start = (f32[512,1024]{1,0:T(8,128)S(1)}, f32[512,1024]{1,0:T(8,128)}, u32[]{:S(2)}) copy-start(f32[512,1024]{1,0:T(8,128)} %get-tuple-element.51) | copy-start | bytes 6291460
  254.7 1.4 copy-start.4
  254.7 1.4 copy-start.6
  254.7 2.2 copy-start.1
  256.8 1.3 copy-start.2
  256.8 2.1 copy-start.7
